TPU v7x, 32 devices: a whole 2x2x4 slice. The times are simulated.
32 devices in a mesh: pipe: 2 (over core), dp: 4 (over z), tensor: 4 (over y, x).
Axes of the slice: x: 2, y: 2, z: 4, core: 2. Of those that a mesh axis runs over, the one named last changes fastest.
Arguments:
- stream_in: bfloat16 [2, 2048, 4096], P('pipe', 'dp', 'tensor'), may hold values from -4.5 to 4.5
- saved_in: bfloat16 [2, 2048, 4096], P('pipe', 'dp', 'tensor'), may hold values from -4.5 to 4.5
- grad_out: bfloat16 [2, 2048, 4096], P('pipe', 'dp', 'tensor'), may hold values from -6 to 6
- mem_keys: bfloat16 [2, 8, 8, 4096], P('pipe', 'dp', None, 'tensor'), may hold values from -4.5 to 4.5
- mem_values: bfloat16 [2, 8, 8, 4096], P('pipe', 'dp', None, 'tensor'), may hold values from -6 to 6
- owner_map: int32 [8], replicated, may hold values from 0 to 7, as said below
- block_ids: int32 [2, 2, 4, 1], P(None, 'pipe', 'dp'), may hold values from 0 to 7, as said below
Outputs:
- next_input: bfloat16 [2, 2048, 4096], P('pipe', 'dp', 'tensor')
- grad_back: bfloat16 [2, 2048, 4096], P('pipe', 'dp', 'tensor')
- key_grad: bfloat16 [2, 8, 8, 4096], P('pipe', 'dp', None, 'tensor')
- value_grad: bfloat16 [2, 8, 8, 4096], P('pipe', 'dp', None, 'tensor')
Inputs may be any that keep to these rules, and one draw needn't show every extreme that they name: `owner_map`: A permutation of the block ids; location loc lies with replica loc // 2 in slot loc % 2. `block_ids`: for each section and replica, the 2 ids of both micro-batches together lie with 2 different replicas, so at most one block is requested from one replica; in every section one replica is asked for a block by every replica, itself included.
All inputs are finite; a program needn't handle non-finite values.
Results may differ from a plain program's by a relative error of at most 0.0057.
Values may be sent and summed in bfloat16 or wider, within the bound.
No kernel may reach another device: no remote copies, remote signals or barrier semaphores. Data moves between devices by JAX's collectives and lax.ppermute only.
A program may use at most 64 MiB of HBM per device.

v0:
```python
import math

import jax
import jax.numpy as jnp
from jax import lax
from jax.sharding import PartitionSpec as P

HEAD_DIM = 128


def from_behind(x, axis, by):
    peers = lax.axis_size(axis)
    pairs = [(i, i + by) for i in range(peers) if 0 <= i + by < peers]
    return lax.ppermute(x, axis, pairs)


def forward_part(inputs, memory_keys, memory_values):
    rows = inputs.shape[0]
    heads_count = inputs.shape[1] // HEAD_DIM
    scale = 1.0 / math.sqrt(HEAD_DIM)
    queries = inputs.reshape(rows, heads_count, HEAD_DIM)
    key_rows = memory_keys.reshape(-1, heads_count, HEAD_DIM)
    value_rows = memory_values.reshape(-1, heads_count, HEAD_DIM)
    scores = (
        jnp.einsum("thd,khd->htk", queries, key_rows, preferred_element_type=jnp.float32) * scale
    )
    exponent = jnp.exp(scores - jnp.max(scores, axis=-1, keepdims=True))
    weights = exponent / jnp.sum(exponent, axis=-1, keepdims=True)
    rounded = weights.astype(jnp.bfloat16)
    attended = jnp.einsum(
        "htk,khd->thd", rounded, value_rows, preferred_element_type=jnp.float32
    ).reshape(rows, -1)
    return (queries, key_rows, value_rows, weights, rounded, attended)


def backward_part(inputs, grads, memory_keys, memory_values):
    queries, key_rows, value_rows, weights, rounded, attended = forward_part(
        inputs, memory_keys, memory_values
    )
    rows = inputs.shape[0]
    heads_count = queries.shape[1]
    scale = 1.0 / math.sqrt(HEAD_DIM)
    grad_rows = grads.reshape(rows, heads_count, HEAD_DIM)
    grad_weights = jnp.einsum(
        "thd,khd->htk", grad_rows, value_rows, preferred_element_type=jnp.float32
    )
    centre = jnp.sum(weights * grad_weights, axis=-1, keepdims=True)
    grad_scores = (weights * (grad_weights - centre) * scale).astype(jnp.bfloat16)
    grad_queries = jnp.einsum(
        "htk,khd->thd", grad_scores, key_rows, preferred_element_type=jnp.float32
    ).reshape(rows, -1)
    key_terms = jnp.einsum("htk,thd->khd", grad_scores, queries, preferred_element_type=jnp.float32)
    value_terms = jnp.einsum("htk,thd->khd", rounded, grad_rows, preferred_element_type=jnp.float32)
    input_grad = (grads.astype(jnp.float32) + grad_queries).astype(jnp.bfloat16)
    key_count = key_rows.shape[0]
    return (
        input_grad,
        key_terms.reshape(key_count, -1).astype(jnp.bfloat16),
        value_terms.reshape(key_count, -1).astype(jnp.bfloat16),
    )


def local(stream_in, saved_in, grad_out, mem_keys, mem_values, owner_map, block_ids):
    replicas = lax.axis_size("dp")
    local_blocks = mem_keys.shape[1]
    block_rows = mem_keys.shape[2]
    width = stream_in.shape[2]
    table_size = owner_map.shape[0]
    requested = block_ids.reshape(-1)
    picks = requested.shape[0]
    half = picks // 2
    matches = requested[:, None] == jnp.arange(table_size, dtype=jnp.int32)[None, :]
    places = jnp.sum(jnp.where(matches, owner_map[None, :], 0), axis=1)
    owners = places // local_blocks
    slot_ids = places % local_blocks
    owner_hits = owners[:, None] == jnp.arange(replicas, dtype=jnp.int32)[None, :]
    served = None
    wanted = jnp.sum(jnp.where(owner_hits, slot_ids[:, None], 0), axis=0)
    served = lax.all_to_all(
        wanted.reshape(replicas, 1), "dp", split_axis=0, concat_axis=0, tiled=True
    ).reshape(replicas)
    out_keys = jnp.take(mem_keys[0], served, axis=0)
    out_values = jnp.take(mem_values[0], served, axis=0)
    got_keys, got_values = (
        lax.all_to_all(out_keys, "dp", split_axis=0, concat_axis=0, tiled=True),
        lax.all_to_all(out_values, "dp", split_axis=0, concat_axis=0, tiled=True),
    )
    fetched_keys = jnp.take(got_keys, owners, axis=0)
    fetched_values = jnp.take(got_values, owners, axis=0)
    forward_keys = fetched_keys[:half].reshape(-1, width)
    forward_values = fetched_values[:half].reshape(-1, width)
    backward_keys = fetched_keys[half:].reshape(-1, width)
    backward_values = fetched_values[half:].reshape(-1, width)
    attended = forward_part(stream_in[0], forward_keys, forward_values)[5]
    section_out = (stream_in[0].astype(jnp.float32) + attended).astype(jnp.bfloat16)
    next_input = from_behind(section_out[None], "pipe", 1)
    input_grad, key_terms, value_terms = backward_part(
        saved_in[0], grad_out[0], backward_keys, backward_values
    )
    grad_back = from_behind(input_grad[None], "pipe", -1)
    key_blocks = key_terms.reshape(half, block_rows, width)
    value_blocks = value_terms.reshape(half, block_rows, width)
    back_hits = owner_hits[half:].astype(jnp.bfloat16)
    send_keys = jnp.einsum(
        "ro,rtf->otf", back_hits, key_blocks, preferred_element_type=jnp.float32
    ).astype(jnp.bfloat16)
    send_values = jnp.einsum(
        "ro,rtf->otf", back_hits, value_blocks, preferred_element_type=jnp.float32
    ).astype(jnp.bfloat16)
    recv_keys, recv_values = (
        lax.all_to_all(send_keys, "dp", split_axis=0, concat_axis=0, tiled=True),
        lax.all_to_all(send_values, "dp", split_axis=0, concat_axis=0, tiled=True),
    )
    slot_hits = (served[:, None] == jnp.arange(local_blocks, dtype=jnp.int32)[None, :]).astype(
        jnp.bfloat16
    )
    key_grad = jnp.einsum(
        "sm,stf->mtf", slot_hits, recv_keys, preferred_element_type=jnp.float32
    ).astype(jnp.bfloat16)
    value_grad = jnp.einsum(
        "sm,stf->mtf", slot_hits, recv_values, preferred_element_type=jnp.float32
    ).astype(jnp.bfloat16)
    return (next_input, grad_back, key_grad[None], value_grad[None])


def solution(mesh):
    in_specs = (
        P("pipe", "dp", "tensor"),
        P("pipe", "dp", "tensor"),
        P("pipe", "dp", "tensor"),
        P("pipe", "dp", None, "tensor"),
        P("pipe", "dp", None, "tensor"),
        P(),
        P(None, "pipe", "dp", None),
    )
    out_specs = (
        P("pipe", "dp", "tensor"),
        P("pipe", "dp", "tensor"),
        P("pipe", "dp", None, "tensor"),
        P("pipe", "dp", None, "tensor"),
    )
    return jax.shard_map(local, mesh=mesh, in_specs=in_specs, out_specs=out_specs, check_vma=False)
```

profile of v0, /device:TPU:0, one launch (start us, length us, event | category | flops | bytes accessed | tf_op | source)
XLA Modules:
  0.0 77.6 jit_solution(11579633971073450565)
XLA Ops:
  0.7 0.9 %fusion.38 = s32[2]{0:T(128)S(1)} fusion(s32[8]{0:T(128)} %param.16, s32[2]{0:T(128)} %bitcast.76), kind=kLoop, calls=%fused_computation.75 | loop fusion | flops 46 | bytes 48 | tf_op jit(solution)/shard_map/reduce_sum | solution.py:73
  2.4 6.3 %all-to-all-start = ((s32[4,1,1]{2,1,0:T(1,128)}), s32[4,1,1]{2,1,0:T(1,128)S(1)}, u32[]{:S(2)}, u32[]{:S(2)}) async-start(s32[4,1,1]{2,1,0:T(1,128)} %copy.44), calls=%async_computation | async-start | bytes 4096 | tf_op jit(solution)/shard_map/all_to_all | solution.py:79
  8.7 5.5 %all-to-all-done = s32[4,1,1]{2,1,0:T(1,128)S(1)} async-done(((s32[4,1,1]{2,1,0:T(1,128)}), s32[4,1,1]{2,1,0:T(1,128)S(1)}, u32[]{:S(2)}, u32[]{:S(2)}) %all-to-all-start) | async-done | bytes 48 | tf_op jit(solution)/shard_map/all_to_all | solution.py:79
  14.9 1.3 %gather_fusion = bf16[4,8,1024]{2,1,0:T(8,128)(2,1)S(1)} fusion(bf16[2,8,1024]{2,1,0:T(8,128)(2,1)} %bitcast.74, s32[1024]{0:T(1024)S(1)} %pad_clamp_fusion.1), kind=kCustom, calls=%fused_computation.clone | custom fusion | bytes 131088 | tf_op jit(solution)/shard_map/jit(_take)/gather | solution.py:83
  16.3 0.7 broadcast_select_fusion.1
  17.0 3.3 %all-to-all-start.1 = ((bf16[4,8,1024]{2,1,0:T(8,128)(2,1)}), bf16[4,8,1024]{2,1,0:T(8,128)(2,1)S(1)}, u32[]{:S(2)}, u32[]{:S(2)}) async-start(bf16[4,8,1024]{2,1,0:T(8,128)(2,1)} %get-tuple-element.28), calls=%async_computation.1 | async-start | bytes 131072 | tf_op jit(solution)/shard_map/all_to_all | solution.py:86
  20.4 1.6 %copy.57 = bf16[64,8,8,128]{3,2,1,0:T(8,128)(2,1)S(1)} copy(bf16[64,8,8,128]{3,1,2,0:T(8,128)(2,1)} %bitcast.71) | data formatting | bytes 2097152
  22.5 3.5 %all-to-all-done.1 = bf16[4,8,1024]{2,1,0:T(8,128)(2,1)S(1)} async-done(((bf16[4,8,1024]{2,1,0:T(8,128)(2,1)}), bf16[4,8,1024]{2,1,0:T(8,128)(2,1)S(1)}, u32[]{:S(2)}, u32[]{:S(2)}) %all-to-all-start.1) | async-done | bytes 65568 | tf_op jit(solution)/shard_map/all_to_all | solution.py:86
  26.0 3.3 %all-to-all-start.2 = ((bf16[4,8,1024]{2,1,0:T(8,128)(2,1)}), bf16[4,8,1024]{2,1,0:T(8,128)(2,1)S(1)}, u32[]{:S(2)}, u32[]{:S(2)}) async-start(bf16[4,8,1024]{2,1,0:T(8,128)(2,1)} %get-tuple-element.29), calls=%async_computation.2 | async-start | bytes 131072 | tf_op jit(solution)/shard_map/all_to_all | solution.py:85
  29.9 5.1 %all-to-all-done.2 = bf16[4,8,1024]{2,1,0:T(8,128)(2,1)S(1)} async-done(((bf16[4,8,1024]{2,1,0:T(8,128)(2,1)}), bf16[4,8,1024]{2,1,0:T(8,128)(2,1)S(1)}, u32[]{:S(2)}, u32[]{:S(2)}) %all-to-all-start.2) | async-done | bytes 65568 | tf_op jit(solution)/shard_map/all_to_all | solution.py:85
  35.6 1.1 %fusion.47 = (f32[8,512]{1,0:T(8,128)S(1)}, f32[8,512,8]{1,2,0:T(8,128)}) fusion(bf16[512,8,128]{2,1,0:T(8,128)(2,1)S(1)} %bitcast.72, bf16[2,8,1024]{2,1,0:T(8,128)(2,1)S(1)} %get-tuple-element.27), kind=kOutput, calls=%fused_computation.87 | convolution fusion | flops 8486919 | bytes 1212416 | tf_op jit(solution)/shard_map/sub | solution.py:27
  37.6 1.5 %fusion.19 = f32[8,128,512]{2,1,0:T(8,128)S(1)} fusion(f32[8,512,8]{1,2,0:T(8,128)S(1)} %convolution_bitcast_fusion, bf16[2,8,1024]{2,1,0:T(8,128)(2,1)S(1)} %get-tuple-element.27, f32[8,512,8]{1,2,0:T(8,128)} %get-tuple-element.31, f32[8,512]{1,0:T(8,128)S(1)} %get-tuple-element.30), kind=kOutput, calls=%fused_computation.32 | convolution fusion | flops 8622087 | bytes 2670592 | tf_op jit(solution)/shard_map/htk,khd->thd/dot_general | solution.py:49
  39.0 1.9 %copy.49 = f32[1,512,1024]{2,1,0:T(8,128)} copy(f32[1,512,1024]{1,2,0:T(8,128)S(1)} %bitcast.65) | data formatting | bytes 4194304 | tf_op jit(solution)/shard_map/reshape | solution.py:51
  40.9 3.2 %add_convert_fusion = bf16[1,512,1024]{2,1,0:T(8,128)(2,1)} fusion(f32[1,512,1024]{2,1,0:T(8,128)} %copy.49, bf16[1,512,1024]{2,1,0:T(8,128)(2,1)} %param.13), kind=kLoop, calls=%fused_computation.7 | loop fusion | flops 1572864 | bytes 4194304 | tf_op jit(solution)/shard_map/convert_element_type | solution.py:54
  44.1 1.3 %collective-permute-start.1 = (bf16[1,512,1024]{2,1,0:T(8,128)(2,1)}, bf16[1,512,1024]{2,1,0:T(8,128)(2,1)}, u32[]{:S(2)}, u32[]{:S(2)}) collective-permute-start(bf16[1,512,1024]{2,1,0:T(8,128)(2,1)} %add_convert_fusion), channel_id=1, source_target_pairs={{16,0},{17,1},{18,2},{19,3},{20,4},{21,5},{22,6},{23,7},{24,8},{25... | collective-permute-start | bytes 3145736 | tf_op jit(solution)/shard_map/ppermute | solution.py:14
  45.9 1.9 %copy.46 = f32[1,512,1024]{2,1,0:T(8,128)} copy(f32[1,512,1024]{1,2,0:T(8,128)S(1)} %bitcast.64) | data formatting | bytes 4194304 | tf_op jit(solution)/shard_map/reshape | solution.py:32
  47.7 3.3 %add_convert_fusion.1 = bf16[1,512,1024]{2,1,0:T(8,128)(2,1)} fusion(f32[1,512,1024]{2,1,0:T(8,128)} %copy.46, bf16[1,512,1024]{2,1,0:T(8,128)(2,1)} %param.11), kind=kLoop, calls=%fused_computation.8 | loop fusion | flops 1572864 | bytes 4194304 | tf_op jit(solution)/shard_map/convert_element_type | solution.py:95
  51.0 4.1 %collective-permute-start = (bf16[1,512,1024]{2,1,0:T(8,128)(2,1)}, bf16[1,512,1024]{2,1,0:T(8,128)(2,1)S(1)}, u32[]{:S(2)}, u32[]{:S(2)}) collective-permute-start(bf16[1,512,1024]{2,1,0:T(8,128)(2,1)} %add_convert_fusion.1), channel_id=1, source_target_pairs={{0,16},{1,17},{2,18},{3,19},{4,20},{5,21},{6,22},{7,23},{8,24},{9,... | collective-permute-start | bytes 3145736 | tf_op jit(solution)/shard_map/ppermute | solution.py:14
  55.8 0.7 multiply_convert_fusion
  56.5 8.1 %all_to_all.29 = bf16[4,8,1024]{2,1,0:T(8,128)(2,1)S(1)} all-to-all(bf16[4,8,1024]{2,1,0:T(8,128)(2,1)S(1)} %get-tuple-element.24), channel_id=1, replica_groups=mesh['pipe'=2,'dp'=4,'tensor'=4] {'dp'}, dimensions={0} | all-to-all | bytes 131072 | tf_op jit(solution)/shard_map/all_to_all | solution.py:112
  64.6 3.3 %all-to-all-start.3 = ((bf16[4,8,1024]{2,1,0:T(8,128)(2,1)}), bf16[4,8,1024]{2,1,0:T(8,128)(2,1)S(1)}, u32[]{:S(2)}, u32[]{:S(2)}) async-start(bf16[4,8,1024]{2,1,0:T(8,128)(2,1)} %get-tuple-element.25), calls=%async_computation.3 | async-start | bytes 131072 | tf_op jit(solution)/shard_map/all_to_all | solution.py:111
  68.7 4.9 %all-to-all-done.3 = bf16[4,8,1024]{2,1,0:T(8,128)(2,1)S(1)} async-done(((bf16[4,8,1024]{2,1,0:T(8,128)(2,1)}), bf16[4,8,1024]{2,1,0:T(8,128)(2,1)S(1)}, u32[]{:S(2)}, u32[]{:S(2)}) %all-to-all-start.3) | async-done | bytes 65568 | tf_op jit(solution)/shard_map/all_to_all | solution.py:111
  74.4 1.0 %copy.77 = bf16[1,512,1024]{2,1,0:T(8,128)(2,1)} copy(bf16[1,512,1024]{2,1,0:T(8,128)(2,1)S(1)} %collective-permute-done) | data formatting | bytes 2097152
  75.3 2.3 %copy.78 = bf16[1,512,1024]{2,1,0:T(8,128)(2,1)} copy(bf16[1,512,1024]{2,1,0:T(8,128)(2,1)} %collective-permute-done.1) | data formatting | bytes 2097152
  (42 shorter events, 6.9 us)
Async XLA Ops:
  0.6 13.7 %copy-start = (bf16[1,2,8,1024]{3,2,1,0:T(8,128)(2,1)S(1)}, bf16[1,2,8,1024]{3,2,1,0:T(8,128)(2,1)}, u32[]{:S(2)}) copy-start(bf16[1,2,8,1024]{3,2,1,0:T(8,128)(2,1)} %param.14) | copy-start | bytes 98308
  0.6 21.3 %copy-start.1 = (bf16[1,512,1024]{2,1,0:T(8,128)(2,1)S(1)}, bf16[1,512,1024]{2,1,0:T(8,128)(2,1)}, u32[]{:S(2)}) copy-start(bf16[1,512,1024]{2,1,0:T(8,128)(2,1)} %param.13) | copy-start | bytes 3145732
  2.4 11.8 %all-to-all-start = ((s32[4,1,1]{2,1,0:T(1,128)}), s32[4,1,1]{2,1,0:T(1,128)S(1)}, u32[]{:S(2)}, u32[]{:S(2)}) async-start(s32[4,1,1]{2,1,0:T(1,128)} %copy.44), calls=%async_computation | async-start | bytes 4096 | tf_op jit(solution)/shard_map/all_to_all | solution.py:79
  17.0 9.0 %all-to-all-start.1 = ((bf16[4,8,1024]{2,1,0:T(8,128)(2,1)}), bf16[4,8,1024]{2,1,0:T(8,128)(2,1)S(1)}, u32[]{:S(2)}, u32[]{:S(2)}) async-start(bf16[4,8,1024]{2,1,0:T(8,128)(2,1)} %get-tuple-element.28), calls=%async_computation.1 | async-start | bytes 131072 | tf_op jit(solution)/shard_map/all_to_all | solution.py:86
  20.4 1.9 %copy-start.2 = (bf16[1,512,1024]{2,1,0:T(8,128)(2,1)S(1)}, bf16[1,512,1024]{2,1,0:T(8,128)(2,1)}, u32[]{:S(2)}) copy-start(bf16[1,512,1024]{2,1,0:T(8,128)(2,1)} %param.11) | copy-start | bytes 3145732
  21.9 13.7 %copy-start.3 = (bf16[64,8,8,128]{3,2,1,0:T(8,128)(2,1)}, bf16[64,8,8,128]{3,2,1,0:T(8,128)(2,1)S(1)}, u32[]{:S(2)}) copy-start(bf16[64,8,8,128]{3,2,1,0:T(8,128)(2,1)S(1)} %copy.57) | copy-start | bytes 3145732
  26.0 9.0 %all-to-all-start.2 = ((bf16[4,8,1024]{2,1,0:T(8,128)(2,1)}), bf16[4,8,1024]{2,1,0:T(8,128)(2,1)S(1)}, u32[]{:S(2)}, u32[]{:S(2)}) async-start(bf16[4,8,1024]{2,1,0:T(8,128)(2,1)} %get-tuple-element.29), calls=%async_computation.2 | async-start | bytes 131072 | tf_op jit(solution)/shard_map/all_to_all | solution.py:85
  44.1 30.3 %collective-permute-start.1 = (bf16[1,512,1024]{2,1,0:T(8,128)(2,1)}, bf16[1,512,1024]{2,1,0:T(8,128)(2,1)}, u32[]{:S(2)}, u32[]{:S(2)}) collective-permute-start(bf16[1,512,1024]{2,1,0:T(8,128)(2,1)} %add_convert_fusion), channel_id=1, source_target_pairs={{16,0},{17,1},{18,2},{19,3},{20,4},{21,5},{22,6},{23,7},{24,8},{25... | collective-permute-start | bytes 3145736 | tf_op jit(solution)/shard_map/ppermute | solution.py:14
  47.7 7.4 %copy-start.4 = (bf16[64,8,8,128]{3,2,1,0:T(8,128)(2,1)S(1)}, bf16[64,8,8,128]{3,2,1,0:T(8,128)(2,1)}, u32[]{:S(2)}) copy-start(bf16[64,8,8,128]{3,2,1,0:T(8,128)(2,1)} %copy-done.3) | copy-start | bytes 3145732
  47.7 7.4 %copy-start.5 = (f32[8,512,8]{1,2,0:T(8,128)S(1)}, f32[8,512,8]{1,2,0:T(8,128)}, u32[]{:S(2)}) copy-start(f32[8,512,8]{1,2,0:T(8,128)} %get-tuple-element.31) | copy-start | bytes 393220
  51.0 23.4 %collective-permute-start = (bf16[1,512,1024]{2,1,0:T(8,128)(2,1)}, bf16[1,512,1024]{2,1,0:T(8,128)(2,1)S(1)}, u32[]{:S(2)}, u32[]{:S(2)}) collective-permute-start(bf16[1,512,1024]{2,1,0:T(8,128)(2,1)} %add_convert_fusion.1), channel_id=1, source_target_pairs={{0,16},{1,17},{2,18},{3,19},{4,20},{5,21},{6,22},{7,23},{8,24},{9,... | collective-permute-start | bytes 3145736 | tf_op jit(solution)/shard_map/ppermute | solution.py:14
  64.6 9.0 %all-to-all-start.3 = ((bf16[4,8,1024]{2,1,0:T(8,128)(2,1)}), bf16[4,8,1024]{2,1,0:T(8,128)(2,1)S(1)}, u32[]{:S(2)}, u32[]{:S(2)}) async-start(bf16[4,8,1024]{2,1,0:T(8,128)(2,1)} %get-tuple-element.25), calls=%async_computation.3 | async-start | bytes 131072 | tf_op jit(solution)/shard_map/all_to_all | solution.py:111
where the time goes:
time: 78.3 us; the launch traced here: 77.6 us
  starting transfers between devices  21.5 us (27%)
  waiting for transfers between devices  19 us (24%)
  local copies, waits for them, and re-layouts  14 us (18%)
  other arithmetic  9.39 us (12%)
  blocking collectives  8.1 us (10%)
  matrix products  4.73 us (6%)
  between operations  0.88 us (1%)
    all_to_all x1, blocking collectives, local(): lax.all_to_all(send_values, 'dp', split_axis=0, concat_axis=0, tiled=True)  8.1 us
    unnamed x19, local copies, waits for them, and re-layouts  6.62 us
    all_to_all x1, starting transfers between devices, local(): lax.all_to_all(wanted.reshape(replicas, 1), 'dp', split_axis=0, concat_ax...  6.32 us
    all_to_all x1, waiting for transfers between devices, local(): lax.all_to_all(wanted.reshape(replicas, 1), 'dp', split_axis=0, concat_ax...  5.47 us
    ppermute x2, starting transfers between devices, from_behind(): return lax.ppermute(x, axis, pairs)  5.35 us
    all_to_all x1, waiting for transfers between devices, local(): lax.all_to_all(out_keys, 'dp', split_axis=0, concat_axis=0, tiled=True)  5.14 us
    all_to_all x1, waiting for transfers between devices, local(): lax.all_to_all(send_keys, 'dp', split_axis=0, concat_axis=0, tiled=True)  4.91 us
    all_to_all x1, waiting for transfers between devices, local(): lax.all_to_all(out_values, 'dp', split_axis=0, concat_axis=0, tiled=True)  3.47 us
  transfers between devices with their start and end apart: 6, of which 4 were waited for; matrix products, arithmetic and copies ran while one was open for 15% of the time, Pallas kernels for 0%

commit v1 on v0

--- a/solution.py
+++ b/solution.py
@@ -1,11 +1,172 @@
+import functools
 import math
 
 import jax
 import jax.numpy as jnp
 from jax import lax
+from jax.experimental import pallas as pl
+from jax.experimental.pallas import tpu as pltpu
 from jax.sharding import PartitionSpec as P
 
 HEAD_DIM = 128
+DIRECT_REPLICAS = 8
+VMEM = pl.BlockSpec(memory_space=pltpu.VMEM)
+SMEM = pl.BlockSpec(memory_space=pltpu.SMEM)
+NT = (((1,), (1,)), ((), ()))
+NN = (((1,), (0,)), ((), ()))
+TN = (((0,), (0,)), ((), ()))
+
+
+def dot(a, b, dims):
+    return lax.dot_general(a, b, dims, preferred_element_type=jnp.float32)
+
+
+def by_head(block):
+    keys, width = block.shape
+    heads = width // HEAD_DIM
+    wide = jnp.broadcast_to(block.astype(jnp.float32)[None], (heads, keys, width))
+    head = lax.broadcasted_iota(jnp.int32, wide.shape, 0)
+    feature_head = lax.broadcasted_iota(jnp.int32, wide.shape, 2) // HEAD_DIM
+    return jnp.where(head == feature_head, wide, 0.0).reshape(heads * keys, width).astype(block.dtype)
+
+
+def own_head(product, keys):
+    heads = product.shape[0] // keys
+    parts = [
+        product[h * keys : (h + 1) * keys, h * HEAD_DIM : (h + 1) * HEAD_DIM] for h in range(heads)
+    ]
+    return jnp.concatenate(parts, axis=1)
+
+
+def softmax_t(keys_by_head, rows, heads):
+    scores = dot(keys_by_head, rows, NT) * (1.0 / math.sqrt(HEAD_DIM))
+    scores = scores.reshape(heads, -1, rows.shape[0])
+    exponent = jnp.exp(scores - jnp.max(scores, axis=1, keepdims=True))
+    return exponent / jnp.sum(exponent, axis=1, keepdims=True)
+
+
+def pick(refs, owner, slot, me, replicas):
+    behind = lax.rem(me - owner + replicas, replicas)
+    block = refs[0][slot]
+    for d in range(1, replicas):
+        block = jnp.where(behind == d, refs[d][slot], block)
+    return block
+
+
+def score_kernel(replicas, slots, *refs):
+    map_ref, ids_ref, stream_ref, saved_ref, grad_ref = refs[:5]
+    key_refs, value_refs = refs[5 : 5 + replicas], refs[5 + replicas : 5 + 2 * replicas]
+    terms_ref, weights_ref, block_ref = refs[5 + 2 * replicas :]
+    me = lax.axis_index("dp")
+    width = stream_ref.shape[1]
+    heads = width // HEAD_DIM
+    back = map_ref[ids_ref[1]]
+    owner, slot = back // slots, back % slots
+    keys = pick(key_refs, owner, slot, me, replicas)
+    values = pick(value_refs, owner, slot, me, replicas)
+    count = keys.shape[0]
+    saved, grads = saved_ref[...], grad_ref[...]
+    weights = softmax_t(by_head(keys), saved, heads)
+    grad_weights = dot(by_head(values), grads, NT).reshape(weights.shape)
+    centre = jnp.sum(weights * grad_weights, axis=1, keepdims=True)
+    grad_scores = weights * (grad_weights - centre) * (1.0 / math.sqrt(HEAD_DIM))
+    flat = (heads * count, saved.shape[0])
+    grad_scores = grad_scores.astype(jnp.bfloat16).reshape(flat)
+    rounded = weights.astype(jnp.bfloat16).reshape(flat)
+    terms_ref[:, :width] = own_head(dot(grad_scores, saved, NN), count).astype(jnp.bfloat16)
+    terms_ref[:, width : 2 * width] = own_head(dot(rounded, grads, NN), count).astype(jnp.bfloat16)
+    place = jnp.full((count, HEAD_DIM), back, jnp.int32)
+    terms_ref[:, 2 * width :] = place.astype(jnp.float32).astype(jnp.bfloat16)
+    section = lax.axis_index("pipe")
+
+    @pl.when(section == 0)
+    def _():
+        ahead = map_ref[ids_ref[0]]
+        owner, slot = ahead // slots, ahead % slots
+        first = by_head(pick(key_refs, owner, slot, me, replicas))
+        block_ref[...] = pick(value_refs, owner, slot, me, replicas)
+        wide = softmax_t(first, stream_ref[...], heads)
+        weights_ref[...] = wide.astype(jnp.bfloat16).reshape(flat)
+
+    @pl.when(section != 0)
+    def _():
+        weights_ref[...] = grad_scores
+        block_ref[...] = keys
+
+
+def output_kernel(rows_ref, weights_ref, block_ref, next_ref, back_ref):
+    section = lax.axis_index("pipe")
+    added = dot(weights_ref[...], by_head(block_ref[...]), TN)
+    out = (rows_ref[...].astype(jnp.float32) + added).astype(jnp.bfloat16)
+    blank = jnp.zeros_like(out)
+    next_ref[...] = jnp.where(section == 0, blank, out)
+    back_ref[...] = jnp.where(section == 0, out, blank)
+
+
+def sum_kernel(replicas, slots, *refs):
+    terms_refs, (key_ref, value_ref) = refs[:replicas], refs[replicas:]
+    me = lax.axis_index("dp")
+    width = key_ref.shape[2]
+    tiles = width // HEAD_DIM
+    terms = [ref[...].astype(jnp.float32) for ref in terms_refs]
+    for slot in range(slots):
+        here = (me * slots + slot).astype(jnp.float32)
+        hits = [t[:, 2 * width :] == here for t in terms]
+        for i in range(2 * tiles):
+            at = slice(i * HEAD_DIM, (i + 1) * HEAD_DIM)
+            total = sum(jnp.where(hit, t[:, at], 0.0) for hit, t in zip(hits, terms))
+            out, j = (key_ref, i) if i < tiles else (value_ref, i - tiles)
+            out[slot, :, j * HEAD_DIM : (j + 1) * HEAD_DIM] = total.astype(jnp.bfloat16)
+
+
+def around(x, replicas):
+    return [x] + [
+        lax.ppermute(x, "dp", [(i, (i + d) % replicas) for i in range(replicas)])
+        for d in range(1, replicas)
+    ]
+
+
+def direct(stream_in, saved_in, grad_out, mem_keys, mem_values, owner_map, block_ids):
+    replicas = lax.axis_size("dp")
+    slots, block_rows, width = mem_keys.shape[1:]
+    rows = stream_in.shape[1]
+    heads = width // HEAD_DIM
+    swap = [(0, 1), (1, 0)]
+    key_parts = around(mem_keys[0], replicas)
+    value_parts = around(mem_values[0], replicas)
+    section = lax.axis_index("pipe")
+    sent = jnp.where(section == 0, stream_in[0], grad_out[0])
+    other_rows = lax.ppermute(sent, "pipe", swap)
+    terms, weights, block = pl.pallas_call(
+        functools.partial(score_kernel, replicas, slots),
+        out_shape=(
+            jax.ShapeDtypeStruct((block_rows, 2 * width + HEAD_DIM), jnp.bfloat16),
+            jax.ShapeDtypeStruct((heads * block_rows, rows), jnp.bfloat16),
+            jax.ShapeDtypeStruct((block_rows, width), jnp.bfloat16),
+        ),
+        in_specs=[SMEM] * 2 + [VMEM] * (3 + 2 * replicas),
+        out_specs=(VMEM,) * 3,
+        name="scores",
+    )(owner_map, block_ids.reshape(-1), stream_in[0], saved_in[0], grad_out[0], *key_parts, *value_parts)
+    term_parts = around(terms, replicas)
+    other_weights = lax.ppermute(weights, "pipe", swap)
+    other_block = lax.ppermute(block, "pipe", swap)
+    next_input, grad_back = pl.pallas_call(
+        output_kernel,
+        out_shape=(jax.ShapeDtypeStruct((rows, width), jnp.bfloat16),) * 2,
+        in_specs=[VMEM] * 3,
+        out_specs=(VMEM,) * 2,
+        cost_estimate=pl.CostEstimate(flops=2 * 256 * rows * width, bytes_accessed=6 * rows * width, transcendentals=0),
+        name="outputs",
+    )(other_rows, other_weights, other_block)
+    key_grad, value_grad = pl.pallas_call(
+        functools.partial(sum_kernel, replicas, slots),
+        out_shape=(jax.ShapeDtypeStruct((slots, block_rows, width), jnp.bfloat16),) * 2,
+        in_specs=[VMEM] * replicas,
+        out_specs=(VMEM,) * 2,
+        name="sums",
+    )(*term_parts)
+    return next_input[None], grad_back[None], key_grad[None], value_grad[None]
 
 
 def from_behind(x, axis, by):
@@ -60,7 +221,7 @@
     )
 
 
-def local(stream_in, saved_in, grad_out, mem_keys, mem_values, owner_map, block_ids):
+def routed(stream_in, saved_in, grad_out, mem_keys, mem_values, owner_map, block_ids):
     replicas = lax.axis_size("dp")
     local_blocks = mem_keys.shape[1]
     block_rows = mem_keys.shape[2]
@@ -123,6 +284,12 @@
     return (next_input, grad_back, key_grad[None], value_grad[None])
 
 
+def local(*args):
+    one_each = args[-1].size == 2 and lax.axis_size("pipe") == 2
+    plan = direct if one_each and lax.axis_size("dp") <= DIRECT_REPLICAS else routed
+    return plan(*args)
+
+
 def solution(mesh):
     in_specs = (
         P("pipe", "dp", "tensor"),

time: 78.3 us -> 36 us (0.46)
  waiting for transfers between devices: 19 us -> 6.24 us
  local copies, waits for them, and re-layouts: 14 us -> 3.01 us
  Pallas kernels: 0 us -> 8.91 us
  blocking collectives: 8.1 us -> 0 us
  other arithmetic: 9.39 us -> 1.66 us
  starting transfers between devices: 21.5 us -> 15.2 us
  matrix products: 4.73 us -> 0 us
    all_to_all x4 -> x0, waiting for transfers between devices: 19 us -> none  [the longest x1 5.47 us: local(): lax.all_to_all(wanted.reshape(replicas, 1), 'dp', split_axis=0, concat_ax...]
    all_to_all x4 -> x0, starting transfers between devices: 16.2 us -> none  [the longest x1 6.32 us: local(): lax.all_to_all(wanted.reshape(replicas, 1), 'dp', split_axis=0, concat_ax...]
    ppermute x2 -> x12, starting transfers between devices: 5.35 us -> 15.2 us  [the longest x9 14.7 us: around(): lax.ppermute(x, 'dp', [(i, (i + d) % replicas) for i in range(replicas)])]
    pallas_call x0 -> x3, Pallas kernels: none -> 8.91 us  [the longest x1 4.32 us: direct(): pl.pallas_call(functools.partial(score_kernel, replicas, slots), out_shap...]
    all_to_all x1 -> x0, blocking collectives: 8.1 us -> none  [local(): lax.all_to_all(send_values, 'dp', split_axis=0, concat_axis=0, tiled=True)]
    convert_element_type x3 -> x0, other arithmetic: 7.16 us -> none  [the longest x1 3.27 us: local(): (stream_in[0].astype(jnp.float32) + attended).astype(jnp.bfloat16)]
    ppermute x2 -> x12, waiting for transfers between devices: 0.01 us -> 6.24 us  [the longest x9 6.23 us: around(): lax.ppermute(x, 'dp', [(i, (i + d) % replicas) for i in range(replicas)])]
    reshape x2 -> x0, local copies, waits for them, and re-layouts: 3.76 us -> none  [the longest x1 1.88 us: backward_part(): grad_queries = jnp.einsum('htk,khd->thd', grad_scores, key_rows, preferre...]
  transfers between devices with their start and end apart: 6 -> 12, of which waited for: 4 -> 7; matrix products, arithmetic and copies ran while one was open for 15% -> 0% of each run, Pallas kernels for 0% -> 16%
where the time goes in v1:
time: 36 us; the launch traced here: 35.8 us
  starting transfers between devices  15.2 us (42%)
  Pallas kernels  8.91 us (25%)
  waiting for transfers between devices  6.24 us (17%)
  local copies, waits for them, and re-layouts  3.01 us (8%)
  other arithmetic  1.66 us (5%)
  between operations  0.71 us (2%)
    ppermute x9, starting transfers between devices, around(): lax.ppermute(x, 'dp', [(i, (i + d) % replicas) for i in range(replicas)])  14.7 us
    ppermute x9, waiting for transfers between devices, around(): lax.ppermute(x, 'dp', [(i, (i + d) % replicas) for i in range(replicas)])  6.23 us
    pallas_call x1, Pallas kernels, direct(): pl.pallas_call(functools.partial(score_kernel, replicas, slots), out_shap...  4.32 us
    pallas_call x1, Pallas kernels, direct(): pl.pallas_call(output_kernel, out_shape=(jax.ShapeDtypeStruct((rows, widt...  3.1 us
    unnamed x28, local copies, waits for them, and re-layouts  3.01 us
    select_n x1, other arithmetic, direct(): sent = jnp.where(section == 0, stream_in[0], grad_out[0])  1.66 us
    pallas_call x1, Pallas kernels, direct(): pl.pallas_call(functools.partial(sum_kernel, replicas, slots), out_shape=...  1.49 us
  transfers between devices with their start and end apart: 12, of which 7 were waited for; matrix products, arithmetic and copies ran while one was open for 0% of the time, Pallas kernels for 16%

profile of v1, /device:TPU:0, one launch (start us, length us, event | category | flops | bytes accessed | tf_op | source)
XLA Modules:
  0.0 35.8 jit_solution(13499585721110558097)
XLA Ops:
  0.7 1.7 %broadcast_select_fusion = bf16[512,1024]{1,0:T(8,128)(2,1)S(1)} fusion(pred[]{:T(512)S(6)} %eq.3, bf16[1,512,1024]{2,1,0:T(8,128)(2,1)} %param.9, bf16[1,512,1024]{2,1,0:T(8,128)(2,1)} %param.7), kind=kLoop, calls=%fused_computation | loop fusion | flops 524288 | bytes 3145729 | tf_op jit(solution)/shard_map/jit(_where)/select_n | solution.py:138
  2.3 0.5 %collective-permute-start = (bf16[512,1024]{1,0:T(8,128)(2,1)S(1)}, bf16[512,1024]{1,0:T(8,128)(2,1)S(1)}, u32[]{:S(2)}, u32[]{:S(2)}) collective-permute-start(bf16[512,1024]{1,0:T(8,128)(2,1)S(1)} %broadcast_select_fusion), channel_id=1, source_target_pairs={{0,16},{16,0},{1,17},{17,1},{2,18},{18,2},{3,19},{19,3},{4,20},{20... | collective-permute-start | bytes 3145736 | tf_op jit(solution)/shard_map/ppermute | solution.py:139
  2.8 2.6 %collective-permute-start.1 = (bf16[2,8,1024]{2,1,0:T(8,128)(2,1)S(1)}, bf16[2,8,1024]{2,1,0:T(8,128)(2,1)S(1)}, u32[]{:S(2)}, u32[]{:S(2)}) collective-permute-start(bf16[2,8,1024]{2,1,0:T(8,128)(2,1)S(1)} %bitcast.16), channel_id=1, source_target_pairs={{0,4},{4,8},{8,12},{12,0},{1,5},{5,9},{9,13},{13,1},{2,6},{6,10},{... | collective-permute-start | bytes 98312 | tf_op jit(solution)/shard_map/ppermute | solution.py:124
  5.5 2.6 %collective-permute-start.2 = (bf16[2,8,1024]{2,1,0:T(8,128)(2,1)S(1)}, bf16[2,8,1024]{2,1,0:T(8,128)(2,1)S(1)}, u32[]{:S(2)}, u32[]{:S(2)}) collective-permute-start(bf16[2,8,1024]{2,1,0:T(8,128)(2,1)S(1)} %bitcast.17), channel_id=1, source_target_pairs={{0,8},{4,12},{8,0},{12,4},{1,9},{5,13},{9,1},{13,5},{2,10},{6,14},... | collective-permute-start | bytes 98312 | tf_op jit(solution)/shard_map/ppermute | solution.py:124
  8.1 1.3 %collective-permute-start.3 = (bf16[2,8,1024]{2,1,0:T(8,128)(2,1)S(1)}, bf16[2,8,1024]{2,1,0:T(8,128)(2,1)S(1)}, u32[]{:S(2)}, u32[]{:S(2)}) collective-permute-start(bf16[2,8,1024]{2,1,0:T(8,128)(2,1)S(1)} %bitcast.18), channel_id=1, source_target_pairs={{0,12},{4,0},{8,4},{12,8},{1,13},{5,1},{9,5},{13,9},{2,14},{6,2},{... | collective-permute-start | bytes 98312 | tf_op jit(solution)/shard_map/ppermute | solution.py:124
  9.4 0.7 %collective-permute-start.4 = (bf16[2,8,1024]{2,1,0:T(8,128)(2,1)S(1)}, bf16[2,8,1024]{2,1,0:T(8,128)(2,1)S(1)}, u32[]{:S(2)}, u32[]{:S(2)}) collective-permute-start(bf16[2,8,1024]{2,1,0:T(8,128)(2,1)S(1)} %bitcast.20), channel_id=1, source_target_pairs={{0,4},{4,8},{8,12},{12,0},{1,5},{5,9},{9,13},{13,1},{2,6},{6,10},{... | collective-permute-start | bytes 98312 | tf_op jit(solution)/shard_map/ppermute | solution.py:124
  10.1 0.3 collective-permute-start.5
  10.4 0.3 collective-permute-done.2.refs_7_
  10.7 2.6 %collective-permute-start.6 = (bf16[2,8,1024]{2,1,0:T(8,128)(2,1)S(1)}, bf16[2,8,1024]{2,1,0:T(8,128)(2,1)S(1)}, u32[]{:S(2)}, u32[]{:S(2)}) collective-permute-start(bf16[2,8,1024]{2,1,0:T(8,128)(2,1)S(1)} %bitcast.22), channel_id=1, source_target_pairs={{0,12},{4,0},{8,4},{12,8},{1,13},{5,1},{9,5},{13,9},{2,14},{6,2},{... | collective-permute-start | bytes 98312 | tf_op jit(solution)/shard_map/ppermute | solution.py:124
  13.3 1.9 %collective-permute-done.4.refs_10_ = bf16[2,8,1024]{2,1,0:T(8,128)(2,1)S(1)} collective-permute-done((bf16[2,8,1024]{2,1,0:T(8,128)(2,1)S(1)}, bf16[2,8,1024]{2,1,0:T(8,128)(2,1)S(1)}, u32[]{:S(2)}, u32[]{:S(2)}) %collective-permute-start.4) | collective-permute-done | bytes 32800 | tf_op jit(solution)/shard_map/ppermute | solution.py:124
  15.2 0.4 %collective-permute-done.5.refs_11_ = bf16[2,8,1024]{2,1,0:T(8,128)(2,1)S(1)} collective-permute-done((bf16[2,8,1024]{2,1,0:T(8,128)(2,1)S(1)}, bf16[2,8,1024]{2,1,0:T(8,128)(2,1)S(1)}, u32[]{:S(2)}, u32[]{:S(2)}) %collective-permute-start.5) | collective-permute-done | bytes 32800 | tf_op jit(solution)/shard_map/ppermute | solution.py:124
  15.9 0.4 %copy-done.11 = bf16[2,8,1024]{2,1,0:T(8,128)(2,1)} copy-done((bf16[2,8,1024]{2,1,0:T(8,128)(2,1)}, bf16[2,8,1024]{2,1,0:T(8,128)(2,1)S(1)}, u32[]{:S(2)}) %copy-start.11) | copy-done | bytes 32792
  16.4 4.3 %scores.1 = (bf16[8,2176]{1,0:T(8,128)(2,1)}, bf16[64,512]{1,0:T(8,128)(2,1)}, bf16[8,1024]{1,0:T(8,128)(2,1)}) custom-call(s32[8]{0:T(128)} %refs_0_.1, s32[2]{0:T(128)} %bitcast.23, bf16[512,1024]{1,0:T(8,128)(2,1)} %bitcast.13, bf16[512,1024]{1,0:T(8,128)(2,1)} %bitcast.14, bf16[512,1024]{1,0:T(8,128)(2,1)} %bitcast.12, bf16[2,8,1024]{2,1,0:T(8,128)(2,1)} %bitcast.15, ...), custom_call_target="tpu_custom_call" | custom-call | tf_op jit(solution)/shard_map/scores/pallas_call | solution.py:140
  20.7 2.0 %collective-permute-start.9 = (bf16[8,2176]{1,0:T(8,128)(2,1)}, bf16[8,2176]{1,0:T(8,128)(2,1)S(1)}, u32[]{:S(2)}, u32[]{:S(2)}) collective-permute-start(bf16[8,2176]{1,0:T(8,128)(2,1)} %get-tuple-element.15.refs_0_), channel_id=1, source_target_pairs={{0,4},{4,8},{8,12},{12,0},{1,5},{5,9},{9,13},{13,1},{2,6},{6,10},{... | collective-permute-start | bytes 104456 | tf_op jit(solution)/shard_map/ppermute | solution.py:124
  22.7 1.9 %collective-permute-start.10 = (bf16[8,2176]{1,0:T(8,128)(2,1)}, bf16[8,2176]{1,0:T(8,128)(2,1)S(1)}, u32[]{:S(2)}, u32[]{:S(2)}) collective-permute-start(bf16[8,2176]{1,0:T(8,128)(2,1)} %get-tuple-element.15.refs_0_), channel_id=1, source_target_pairs={{0,8},{4,12},{8,0},{12,4},{1,9},{5,13},{9,1},{13,5},{2,10},{6,14},... | collective-permute-start | bytes 104456 | tf_op jit(solution)/shard_map/ppermute | solution.py:124
  24.6 0.6 %collective-permute-start.11 = (bf16[8,2176]{1,0:T(8,128)(2,1)}, bf16[8,2176]{1,0:T(8,128)(2,1)S(1)}, u32[]{:S(2)}, u32[]{:S(2)}) collective-permute-start(bf16[8,2176]{1,0:T(8,128)(2,1)} %get-tuple-element.15.refs_0_), channel_id=1, source_target_pairs={{0,12},{4,0},{8,4},{12,8},{1,13},{5,1},{9,5},{13,9},{2,14},{6,2},{... | collective-permute-start | bytes 104456 | tf_op jit(solution)/shard_map/ppermute | solution.py:124
  25.2 1.9 %collective-permute-done.9.refs_1_ = bf16[8,2176]{1,0:T(8,128)(2,1)S(1)} collective-permute-done((bf16[8,2176]{1,0:T(8,128)(2,1)}, bf16[8,2176]{1,0:T(8,128)(2,1)S(1)}, u32[]{:S(2)}, u32[]{:S(2)}) %collective-permute-start.9) | collective-permute-done | bytes 34848 | tf_op jit(solution)/shard_map/ppermute | solution.py:124
  27.1 1.2 %collective-permute-done.10.refs_2_ = bf16[8,2176]{1,0:T(8,128)(2,1)S(1)} collective-permute-done((bf16[8,2176]{1,0:T(8,128)(2,1)}, bf16[8,2176]{1,0:T(8,128)(2,1)S(1)}, u32[]{:S(2)}, u32[]{:S(2)}) %collective-permute-start.10) | collective-permute-done | bytes 34848 | tf_op jit(solution)/shard_map/ppermute | solution.py:124
  28.3 0.5 %collective-permute-done.11.refs_3_ = bf16[8,2176]{1,0:T(8,128)(2,1)S(1)} collective-permute-done((bf16[8,2176]{1,0:T(8,128)(2,1)}, bf16[8,2176]{1,0:T(8,128)(2,1)S(1)}, u32[]{:S(2)}, u32[]{:S(2)}) %collective-permute-start.11) | collective-permute-done | bytes 34848 | tf_op jit(solution)/shard_map/ppermute | solution.py:124
  28.9 0.6 %copy-done.4 = bf16[8,2176]{1,0:T(8,128)(2,1)} copy-done((bf16[8,2176]{1,0:T(8,128)(2,1)}, bf16[8,2176]{1,0:T(8,128)(2,1)S(1)}, u32[]{:S(2)}) %copy-start.4) | copy-done | bytes 34840
  29.5 1.5 %sums.1 = (bf16[2,8,1024]{2,1,0:T(8,128)(2,1)}, bf16[2,8,1024]{2,1,0:T(8,128)(2,1)}) custom-call(bf16[8,2176]{1,0:T(8,128)(2,1)} %get-tuple-element.15.refs_0_, bf16[8,2176]{1,0:T(8,128)(2,1)} %copy-done.2, bf16[8,2176]{1,0:T(8,128)(2,1)} %copy-done.3, bf16[8,2176]{1,0:T(8,128)(2,1)} %copy-done.4), custom_call_target="tpu_custom_call" | custom-call | tf_op jit(solution)/shard_map/sums/pallas_call | solution.py:162
  31.0 0.6 %copy-done.13 = bf16[8,1024]{1,0:T(8,128)(2,1)} copy-done((bf16[8,1024]{1,0:T(8,128)(2,1)}, bf16[8,1024]{1,0:T(8,128)(2,1)S(1)}, u32[]{:S(2)}) %copy-start.13) | copy-done | bytes 16408
  31.6 1.0 %copy-done = bf16[512,1024]{1,0:T(8,128)(2,1)} copy-done((bf16[512,1024]{1,0:T(8,128)(2,1)}, bf16[512,1024]{1,0:T(8,128)(2,1)S(1)}, u32[]{:S(2)}) %copy-start) | copy-done | bytes 1048600
  32.7 3.1 %outputs.1 = (bf16[512,1024]{1,0:T(8,128)(2,1)}, bf16[512,1024]{1,0:T(8,128)(2,1)}) custom-call(bf16[512,1024]{1,0:T(8,128)(2,1)} %copy-done, bf16[64,512]{1,0:T(8,128)(2,1)} %copy-done.1, bf16[8,1024]{1,0:T(8,128)(2,1)} %copy-done.13), custom_call_target="tpu_custom_call" | custom-call | flops 268435456 | bytes 3145728 | tf_op jit(solution)/shard_map/outputs/pallas_call | solution.py:154
  (32 shorter events, 0.5 us)
Async XLA Ops:
  0.6 2.2 %copy-start.5 = (bf16[1,2,8,1024]{3,2,1,0:T(8,128)(2,1)S(1)}, bf16[1,2,8,1024]{3,2,1,0:T(8,128)(2,1)}, u32[]{:S(2)}) copy-start(bf16[1,2,8,1024]{3,2,1,0:T(8,128)(2,1)} %param.10) | copy-start | bytes 98308
  0.6 8.8 %copy-start.6 = (bf16[1,2,8,1024]{3,2,1,0:T(8,128)(2,1)S(1)}, bf16[1,2,8,1024]{3,2,1,0:T(8,128)(2,1)}, u32[]{:S(2)}) copy-start(bf16[1,2,8,1024]{3,2,1,0:T(8,128)(2,1)} %param.11) | copy-start | bytes 98308
  2.3 28.7 %collective-permute-start = (bf16[512,1024]{1,0:T(8,128)(2,1)S(1)}, bf16[512,1024]{1,0:T(8,128)(2,1)S(1)}, u32[]{:S(2)}, u32[]{:S(2)}) collective-permute-start(bf16[512,1024]{1,0:T(8,128)(2,1)S(1)} %broadcast_select_fusion), channel_id=1, source_target_pairs={{0,16},{16,0},{1,17},{17,1},{2,18},{18,2},{3,19},{19,3},{4,20},{20... | collective-permute-start | bytes 3145736 | tf_op jit(solution)/shard_map/ppermute | solution.py:139
  2.8 7.3 %collective-permute-start.1 = (bf16[2,8,1024]{2,1,0:T(8,128)(2,1)S(1)}, bf16[2,8,1024]{2,1,0:T(8,128)(2,1)S(1)}, u32[]{:S(2)}, u32[]{:S(2)}) collective-permute-start(bf16[2,8,1024]{2,1,0:T(8,128)(2,1)S(1)} %bitcast.16), channel_id=1, source_target_pairs={{0,4},{4,8},{8,12},{12,0},{1,5},{5,9},{9,13},{13,1},{2,6},{6,10},{... | collective-permute-start | bytes 98312 | tf_op jit(solution)/shard_map/ppermute | solution.py:124
  5.5 5.2 %collective-permute-start.2 = (bf16[2,8,1024]{2,1,0:T(8,128)(2,1)S(1)}, bf16[2,8,1024]{2,1,0:T(8,128)(2,1)S(1)}, u32[]{:S(2)}, u32[]{:S(2)}) collective-permute-start(bf16[2,8,1024]{2,1,0:T(8,128)(2,1)S(1)} %bitcast.17), channel_id=1, source_target_pairs={{0,8},{4,12},{8,0},{12,4},{1,9},{5,13},{9,1},{13,5},{2,10},{6,14},... | collective-permute-start | bytes 98312 | tf_op jit(solution)/shard_map/ppermute | solution.py:124
  8.1 5.3 %collective-permute-start.3 = (bf16[2,8,1024]{2,1,0:T(8,128)(2,1)S(1)}, bf16[2,8,1024]{2,1,0:T(8,128)(2,1)S(1)}, u32[]{:S(2)}, u32[]{:S(2)}) collective-permute-start(bf16[2,8,1024]{2,1,0:T(8,128)(2,1)S(1)} %bitcast.18), channel_id=1, source_target_pairs={{0,12},{4,0},{8,4},{12,8},{1,13},{5,1},{9,5},{13,9},{2,14},{6,2},{... | collective-permute-start | bytes 98312 | tf_op jit(solution)/shard_map/ppermute | solution.py:124
  9.4 5.8 %collective-permute-start.4 = (bf16[2,8,1024]{2,1,0:T(8,128)(2,1)S(1)}, bf16[2,8,1024]{2,1,0:T(8,128)(2,1)S(1)}, u32[]{:S(2)}, u32[]{:S(2)}) collective-permute-start(bf16[2,8,1024]{2,1,0:T(8,128)(2,1)S(1)} %bitcast.20), channel_id=1, source_target_pairs={{0,4},{4,8},{8,12},{12,0},{1,5},{5,9},{9,13},{13,1},{2,6},{6,10},{... | collective-permute-start | bytes 98312 | tf_op jit(solution)/shard_map/ppermute | solution.py:124
  10.1 5.7 %copy-start.7 = (bf16[2,8,1024]{2,1,0:T(8,128)(2,1)}, bf16[2,8,1024]{2,1,0:T(8,128)(2,1)S(1)}, u32[]{:S(2)}) copy-start(bf16[2,8,1024]{2,1,0:T(8,128)(2,1)S(1)} %collective-permute-done.1.refs_6_) | copy-start | bytes 98308
  10.1 5.6 %collective-permute-start.5 = (bf16[2,8,1024]{2,1,0:T(8,128)(2,1)S(1)}, bf16[2,8,1024]{2,1,0:T(8,128)(2,1)S(1)}, u32[]{:S(2)}, u32[]{:S(2)}) collective-permute-start(bf16[2,8,1024]{2,1,0:T(8,128)(2,1)S(1)} %bitcast.21), channel_id=1, source_target_pairs={{0,8},{4,12},{8,0},{12,4},{1,9},{5,13},{9,1},{13,5},{2,10},{6,14},... | collective-permute-start | bytes 98312 | tf_op jit(solution)/shard_map/ppermute | solution.py:124
  10.7 5.1 %copy-start.8 = (bf16[2,8,1024]{2,1,0:T(8,128)(2,1)}, bf16[2,8,1024]{2,1,0:T(8,128)(2,1)S(1)}, u32[]{:S(2)}) copy-start(bf16[2,8,1024]{2,1,0:T(8,128)(2,1)S(1)} %collective-permute-done.2.refs_7_) | copy-start | bytes 98308
  10.7 5.0 %collective-permute-start.6 = (bf16[2,8,1024]{2,1,0:T(8,128)(2,1)S(1)}, bf16[2,8,1024]{2,1,0:T(8,128)(2,1)S(1)}, u32[]{:S(2)}, u32[]{:S(2)}) collective-permute-start(bf16[2,8,1024]{2,1,0:T(8,128)(2,1)S(1)} %bitcast.22), channel_id=1, source_target_pairs={{0,12},{4,0},{8,4},{12,8},{1,13},{5,1},{9,5},{13,9},{2,14},{6,2},{... | collective-permute-start | bytes 98312 | tf_op jit(solution)/shard_map/ppermute | solution.py:124
  13.3 2.4 %copy-start.9 = (bf16[2,8,1024]{2,1,0:T(8,128)(2,1)}, bf16[2,8,1024]{2,1,0:T(8,128)(2,1)S(1)}, u32[]{:S(2)}) copy-start(bf16[2,8,1024]{2,1,0:T(8,128)(2,1)S(1)} %collective-permute-done.3.refs_8_) | copy-start | bytes 98308
  15.2 0.6 %copy-start.10 = (bf16[2,8,1024]{2,1,0:T(8,128)(2,1)}, bf16[2,8,1024]{2,1,0:T(8,128)(2,1)S(1)}, u32[]{:S(2)}) copy-start(bf16[2,8,1024]{2,1,0:T(8,128)(2,1)S(1)} %collective-permute-done.4.refs_10_) | copy-start | bytes 98308
  15.7 0.6 %copy-start.11 = (bf16[2,8,1024]{2,1,0:T(8,128)(2,1)}, bf16[2,8,1024]{2,1,0:T(8,128)(2,1)S(1)}, u32[]{:S(2)}) copy-start(bf16[2,8,1024]{2,1,0:T(8,128)(2,1)S(1)} %collective-permute-done.5.refs_11_) | copy-start | bytes 98308
  15.8 0.6 %copy-start.12 = (bf16[2,8,1024]{2,1,0:T(8,128)(2,1)}, bf16[2,8,1024]{2,1,0:T(8,128)(2,1)S(1)}, u32[]{:S(2)}) copy-start(bf16[2,8,1024]{2,1,0:T(8,128)(2,1)S(1)} %collective-permute-done.6.refs_12_) | copy-start | bytes 98308
  20.7 10.3 %collective-permute-start.7 = (bf16[64,512]{1,0:T(8,128)(2,1)}, bf16[64,512]{1,0:T(8,128)(2,1)S(1)}, u32[]{:S(2)}, u32[]{:S(2)}) collective-permute-start(bf16[64,512]{1,0:T(8,128)(2,1)} %get-tuple-element.11), channel_id=1, source_target_pairs={{0,16},{16,0},{1,17},{17,1},{2,18},{18,2},{3,19},{19,3},{4,20},{20... | collective-permute-start | bytes 196616 | tf_op jit(solution)/shard_map/ppermute | solution.py:152
  20.7 6.4 %collective-permute-start.9 = (bf16[8,2176]{1,0:T(8,128)(2,1)}, bf16[8,2176]{1,0:T(8,128)(2,1)S(1)}, u32[]{:S(2)}, u32[]{:S(2)}) collective-permute-start(bf16[8,2176]{1,0:T(8,128)(2,1)} %get-tuple-element.15.refs_0_), channel_id=1, source_target_pairs={{0,4},{4,8},{8,12},{12,0},{1,5},{5,9},{9,13},{13,1},{2,6},{6,10},{... | collective-permute-start | bytes 104456 | tf_op jit(solution)/shard_map/ppermute | solution.py:124
  22.7 5.6 %collective-permute-start.10 = (bf16[8,2176]{1,0:T(8,128)(2,1)}, bf16[8,2176]{1,0:T(8,128)(2,1)S(1)}, u32[]{:S(2)}, u32[]{:S(2)}) collective-permute-start(bf16[8,2176]{1,0:T(8,128)(2,1)} %get-tuple-element.15.refs_0_), channel_id=1, source_target_pairs={{0,8},{4,12},{8,0},{12,4},{1,9},{5,13},{9,1},{13,5},{2,10},{6,14},... | collective-permute-start | bytes 104456 | tf_op jit(solution)/shard_map/ppermute | solution.py:124
  24.6 4.1 %collective-permute-start.11 = (bf16[8,2176]{1,0:T(8,128)(2,1)}, bf16[8,2176]{1,0:T(8,128)(2,1)S(1)}, u32[]{:S(2)}, u32[]{:S(2)}) collective-permute-start(bf16[8,2176]{1,0:T(8,128)(2,1)} %get-tuple-element.15.refs_0_), channel_id=1, source_target_pairs={{0,12},{4,0},{8,4},{12,8},{1,13},{5,1},{9,5},{13,9},{2,14},{6,2},{... | collective-permute-start | bytes 104456 | tf_op jit(solution)/shard_map/ppermute | solution.py:124
  27.1 1.7 %copy-start.2 = (bf16[8,2176]{1,0:T(8,128)(2,1)}, bf16[8,2176]{1,0:T(8,128)(2,1)S(1)}, u32[]{:S(2)}) copy-start(bf16[8,2176]{1,0:T(8,128)(2,1)S(1)} %collective-permute-done.9.refs_1_) | copy-start | bytes 104452
  27.1 3.9 %collective-permute-start.8 = (bf16[8,1024]{1,0:T(8,128)(2,1)}, bf16[8,1024]{1,0:T(8,128)(2,1)S(1)}, u32[]{:S(2)}, u32[]{:S(2)}) collective-permute-start(bf16[8,1024]{1,0:T(8,128)(2,1)} %get-tuple-element.12), channel_id=1, source_target_pairs={{0,16},{16,0},{1,17},{17,1},{2,18},{18,2},{3,19},{19,3},{4,20},{20... | collective-permute-start | bytes 49160 | tf_op jit(solution)/shard_map/ppermute | solution.py:153
  28.9 0.6 %copy-start.4 = (bf16[8,2176]{1,0:T(8,128)(2,1)}, bf16[8,2176]{1,0:T(8,128)(2,1)S(1)}, u32[]{:S(2)}) copy-start(bf16[8,2176]{1,0:T(8,128)(2,1)S(1)} %collective-permute-done.11.refs_3_) | copy-start | bytes 104452
  31.0 0.6 %copy-start.1 = (bf16[64,512]{1,0:T(8,128)(2,1)}, bf16[64,512]{1,0:T(8,128)(2,1)S(1)}, u32[]{:S(2)}) copy-start(bf16[64,512]{1,0:T(8,128)(2,1)S(1)} %collective-permute-done.7.weights_ref) | copy-start | bytes 196612
  31.6 1.0 %copy-start = (bf16[512,1024]{1,0:T(8,128)(2,1)}, bf16[512,1024]{1,0:T(8,128)(2,1)S(1)}, u32[]{:S(2)}) copy-start(bf16[512,1024]{1,0:T(8,128)(2,1)S(1)} %collective-permute-done.rows_ref) | copy-start | bytes 3145732
  (2 other events, 1.2 us)

commit v2 on v0

--- a/solution.py
+++ b/solution.py
@@ -1,11 +1,282 @@
+import functools
 import math
 
 import jax
 import jax.numpy as jnp
 from jax import lax
+from jax.experimental import pallas as pl
+from jax.experimental.pallas import tpu as pltpu
 from jax.sharding import PartitionSpec as P
 
 HEAD_DIM = 128
+DIRECT_REPLICAS = 8
+FETCH_ORDER = (2, 3, 1)
+SEND_ORDER = (1, 3, 2)
+HBM = pl.BlockSpec(memory_space=pltpu.HBM)
+VMEM = pl.BlockSpec(memory_space=pltpu.VMEM)
+SMEM = pl.BlockSpec(memory_space=pltpu.SMEM)
+NT = (((1,), (1,)), ((), ()))
+NN = (((1,), (0,)), ((), ()))
+TN = (((0,), (0,)), ((), ()))
+
+
+def padded(rows):
+    return -(-rows // 16) * 16
+
+
+def dot(a, b, dims):
+    return lax.dot_general(a, b, dims, preferred_element_type=jnp.float32)
+
+
+def by_head(block):
+    keys, width = block.shape
+    heads = width // HEAD_DIM
+    wide = jnp.broadcast_to(block.astype(jnp.float32)[None], (heads, keys, width))
+    head = lax.broadcasted_iota(jnp.int32, wide.shape, 0)
+    feature_head = lax.broadcasted_iota(jnp.int32, wide.shape, 2) // HEAD_DIM
+    return jnp.where(head == feature_head, wide, 0.0).reshape(heads * keys, width).astype(block.dtype)
+
+
+def own_head(product, keys):
+    heads = product.shape[0] // keys
+    parts = [
+        product[h * keys : (h + 1) * keys, h * HEAD_DIM : (h + 1) * HEAD_DIM] for h in range(heads)
+    ]
+    return jnp.concatenate(parts, axis=1)
+
+
+def softmax_t(keys_by_head, rows, heads):
+    scores = dot(keys_by_head, rows, NT) * (1.0 / math.sqrt(HEAD_DIM))
+    scores = scores.reshape(heads, -1, rows.shape[0])
+    exponent = jnp.exp(scores - jnp.max(scores, axis=1, keepdims=True))
+    return exponent / jnp.sum(exponent, axis=1, keepdims=True)
+
+
+def pick(refs, first, owner, slot, me):
+    block = refs[0][first + slot]
+    for d in range(1, len(refs)):
+        block = jnp.where(owner == me ^ d, refs[d][first + slot], block)
+    return block
+
+
+def stack_kernel(keys_ref, values_ref, out_ref, sems):
+    slots = keys_ref.shape[0]
+    copies = [
+        pltpu.make_async_copy(keys_ref, out_ref.at[:slots], sems.at[0]),
+        pltpu.make_async_copy(values_ref, out_ref.at[slots:], sems.at[1]),
+    ]
+    for copy in copies:
+        copy.start()
+    for copy in copies:
+        copy.wait()
+
+
+def fetch_kernel(map_ref, ids_ref, stream_ref, saved_ref, grad_ref, *refs):
+    saved_near, grad_near, sent_ref, place_ref, map_near, ids_near, sems = refs
+    rows = sent_ref.at[: stream_ref.shape[0]]
+    section = lax.axis_index("pipe")
+    small = [
+        pltpu.make_async_copy(map_ref, map_near, sems.at[0]),
+        pltpu.make_async_copy(ids_ref, ids_near, sems.at[1]),
+    ]
+    large = [
+        pltpu.make_async_copy(saved_ref, saved_near, sems.at[2]),
+        pltpu.make_async_copy(grad_ref, grad_near, sems.at[3]),
+    ]
+    for copy in small + large:
+        copy.start()
+
+    @pl.when(section == 0)
+    def _():
+        pltpu.make_async_copy(stream_ref, rows, sems.at[4]).start()
+
+    @pl.when(section != 0)
+    def _():
+        pltpu.make_async_copy(grad_ref, rows, sems.at[4]).start()
+
+    for copy in small:
+        copy.wait()
+    for i in range(place_ref.shape[0]):
+        place_ref[i] = map_near[ids_near[i]]
+    for copy in large:
+        copy.wait()
+    pltpu.make_async_copy(grad_ref, rows, sems.at[4]).wait()
+
+
+def score_kernel(slots, place_ref, saved_ref, grad_ref, rows_ref, *refs):
+    memory, (terms_ref, sent_ref) = refs[:-2], refs[-2:]
+    me = lax.axis_index("dp")
+    tokens, width = saved_ref.shape
+    heads = width // HEAD_DIM
+    back = place_ref[1]
+    owner, slot = back // slots, back % slots
+    keys = pick(memory, 0, owner, slot, me)
+    values = pick(memory, slots, owner, slot, me)
+    count = keys.shape[0]
+    saved, grads = saved_ref[...], grad_ref[...]
+    weights = softmax_t(by_head(keys), saved, heads)
+    grad_weights = dot(by_head(values), grads, NT).reshape(weights.shape)
+    centre = jnp.sum(weights * grad_weights, axis=1, keepdims=True)
+    grad_scores = weights * (grad_weights - centre) * (1.0 / math.sqrt(HEAD_DIM))
+    flat = heads * count
+    grad_scores = grad_scores.astype(jnp.bfloat16).reshape(flat, tokens)
+    rounded = weights.astype(jnp.bfloat16).reshape(flat, tokens)
+    terms_ref[:, :width] = own_head(dot(grad_scores, saved, NN), count).astype(jnp.bfloat16)
+    terms_ref[:, width : 2 * width] = own_head(dot(rounded, grads, NN), count).astype(jnp.bfloat16)
+    place = jnp.full((count, HEAD_DIM), back, jnp.int32)
+    terms_ref[:, 2 * width :] = place.astype(jnp.float32).astype(jnp.bfloat16)
+    first, second = tokens, tokens + padded(count)
+    section = lax.axis_index("pipe")
+
+    @pl.when(section == 0)
+    def _():
+        ahead = place_ref[0]
+        owner, slot = ahead // slots, ahead % slots
+        sent_ref[first : first + count, :] = pick(memory, 0, owner, slot, me)
+        sent_ref[second : second + count, :] = pick(memory, slots, owner, slot, me)
+
+    @pl.when(section != 0)
+    def _():
+        sent_ref[first : first + count, :] = keys
+        part = flat * tokens // width
+        for i in range(width // tokens):
+            at = slice(i * tokens, (i + 1) * tokens)
+            sent_ref[second : second + part, at] = grad_scores[i * part : (i + 1) * part, :]
+
+
+def output_kernel(tokens, count, sent_ref, next_ref, back_ref):
+    width = sent_ref.shape[1]
+    heads = width // HEAD_DIM
+    first, second = tokens, tokens + padded(count)
+    keys = by_head(sent_ref[first : first + count, :])
+    rows = sent_ref[:tokens, :]
+    section = lax.axis_index("pipe")
+
+    @pl.when(section == 0)
+    def _():
+        next_ref[...] = jnp.zeros_like(next_ref)
+        part = heads * count * tokens // width
+        grad_scores = [
+            sent_ref[second : second + part, i * tokens : (i + 1) * tokens]
+            for i in range(width // tokens)
+        ]
+        added = dot(jnp.concatenate(grad_scores, axis=0), keys, TN)
+        back_ref[...] = (rows.astype(jnp.float32) + added).astype(jnp.bfloat16)
+
+    @pl.when(section != 0)
+    def _():
+        back_ref[...] = jnp.zeros_like(back_ref)
+        values = by_head(sent_ref[second : second + count, :])
+        weights = softmax_t(keys, rows, heads).astype(jnp.bfloat16).reshape(-1, tokens)
+        added = dot(weights, values, TN)
+        next_ref[...] = (rows.astype(jnp.float32) + added).astype(jnp.bfloat16)
+
+
+def sum_kernel(slots, *refs):
+    terms_refs, (key_ref, value_ref) = refs[:-2], refs[-2:]
+    me = lax.axis_index("dp")
+    width = key_ref.shape[2]
+    tiles = width // HEAD_DIM
+    terms = [ref[...].astype(jnp.float32) for ref in terms_refs]
+    for slot in range(slots):
+        here = (me * slots + slot).astype(jnp.float32)
+        hits = [t[:, 2 * width :] == here for t in terms]
+        for i in range(2 * tiles):
+            at = slice(i * HEAD_DIM, (i + 1) * HEAD_DIM)
+            total = sum(jnp.where(hit, t[:, at], 0.0) for hit, t in zip(hits, terms))
+            out, j = (key_ref, i) if i < tiles else (value_ref, i - tiles)
+            out[slot, :, j * HEAD_DIM : (j + 1) * HEAD_DIM] = total.astype(jnp.bfloat16)
+
+
+def around(x, replicas, order):
+    parts = {0: x}
+    for d in order:
+        parts[d] = lax.ppermute(x, "dp", [(i, i ^ d) for i in range(replicas)])
+    return [parts[d] for d in range(replicas)]
+
+
+def vmem(x):
+    return pltpu.with_memory_space_constraint(x, pltpu.VMEM)
+
+
+def hbm(x):
+    return pltpu.with_memory_space_constraint(x, pltpu.HBM)
+
+
+def smem(x):
+    return pltpu.with_memory_space_constraint(x, pltpu.SMEM)
+
+
+def call(kernel, name, out, in_specs, scratch=(), moved=0, aliases=()):
+    return pl.pallas_call(
+        kernel,
+        out_shape=out,
+        in_specs=in_specs,
+        out_specs=jax.tree.map(lambda o: SMEM if o.shape == (2,) else VMEM, out),
+        scratch_shapes=scratch,
+        input_output_aliases=dict(aliases),
+        compiler_params=pltpu.CompilerParams(vmem_limit_bytes=16 * 1024 * 1024),
+        cost_estimate=pl.CostEstimate(flops=0, bytes_accessed=moved, transcendentals=0),
+        name=name,
+    )
+
+
+def direct(stream_in, saved_in, grad_out, mem_keys, mem_values, owner_map, block_ids):
+    replicas = lax.axis_size("dp")
+    slots, block_rows, width = mem_keys.shape[1:]
+    tokens = stream_in.shape[1]
+    rows = pltpu.VMEM((tokens, width), jnp.bfloat16)
+    grad_lines = width // HEAD_DIM * block_rows * tokens // width
+    sent_rows = tokens + padded(block_rows) + padded(max(block_rows, grad_lines))
+    sent = pltpu.VMEM((sent_rows, width), jnp.bfloat16)
+    stacked = call(
+        stack_kernel,
+        "stack",
+        pltpu.VMEM((2 * slots, block_rows, width), jnp.bfloat16),
+        [HBM] * 2,
+        [pltpu.SemaphoreType.DMA((2,))],
+    )(hbm(mem_keys[0]), hbm(mem_values[0]))
+    stacked, *own = lax.optimization_barrier(
+        (stacked, owner_map, block_ids.reshape(-1), stream_in[0], saved_in[0], grad_out[0])
+    )
+    memory = around(stacked, replicas, FETCH_ORDER)
+    saved, grads, to_send, places = call(
+        fetch_kernel,
+        "fetch",
+        (rows, rows, sent, pltpu.SMEM((2,), jnp.int32)),
+        [HBM] * 5,
+        [
+            pltpu.SMEM(owner_map.shape, jnp.int32),
+            pltpu.SMEM((2,), jnp.int32),
+            pltpu.SemaphoreType.DMA((5,)),
+        ],
+        12 * tokens * width,
+    )(*map(hbm, own))
+    terms, to_send = call(
+        functools.partial(score_kernel, slots),
+        "scores",
+        (pltpu.VMEM((block_rows, 2 * width + HEAD_DIM), jnp.bfloat16), sent),
+        [SMEM] + [VMEM] * (3 + replicas),
+        aliases={3: 1}.items(),
+    )(smem(places), *map(vmem, (saved, grads, to_send, *memory)))
+    other_sent = lax.ppermute(to_send, "pipe", [(0, 1), (1, 0)])
+    term_parts = around(terms, replicas, SEND_ORDER)
+    next_input, grad_back = call(
+        functools.partial(output_kernel, tokens, block_rows),
+        "outputs",
+        (jax.ShapeDtypeStruct((tokens, width), jnp.bfloat16),) * 2,
+        [VMEM],
+        (),
+        4 * tokens * width,
+    )(vmem(other_sent))
+    *term_parts, next_input, grad_back = lax.optimization_barrier((*term_parts, next_input, grad_back))
+    key_grad, value_grad = call(
+        functools.partial(sum_kernel, slots),
+        "sums",
+        (jax.ShapeDtypeStruct((slots, block_rows, width), jnp.bfloat16),) * 2,
+        [VMEM] * replicas,
+    )(*map(vmem, term_parts))
+    return next_input[None], grad_back[None], key_grad[None], value_grad[None]
 
 
 def from_behind(x, axis, by):
@@ -60,7 +331,7 @@
     )
 
 
-def local(stream_in, saved_in, grad_out, mem_keys, mem_values, owner_map, block_ids):
+def routed(stream_in, saved_in, grad_out, mem_keys, mem_values, owner_map, block_ids):
     replicas = lax.axis_size("dp")
     local_blocks = mem_keys.shape[1]
     block_rows = mem_keys.shape[2]
@@ -123,6 +394,13 @@
     return (next_input, grad_back, key_grad[None], value_grad[None])
 
 
+def local(*args):
+    replicas, (_, tokens, width) = lax.axis_size("dp"), args[0].shape
+    few = replicas <= DIRECT_REPLICAS and replicas & (replicas - 1) == 0
+    one_each = args[-1].size == 2 and lax.axis_size("pipe") == 2 and width % tokens == 0
+    return (direct if few and one_each else routed)(*args)
+
+
 def solution(mesh):
     in_specs = (
         P("pipe", "dp", "tensor"),

time: 78.3 us -> 22 us (0.28)
  waiting for transfers between devices: 19 us -> 4.31 us
  local copies, waits for them, and re-layouts: 14 us -> 0 us
  starting transfers between devices: 21.5 us -> 10.3 us
  other arithmetic: 9.39 us -> 0 us
  blocking collectives: 8.1 us -> 0 us
  Pallas kernels: 0 us -> 6.5 us
  matrix products: 4.73 us -> 0 us
    all_to_all x4 -> x0, waiting for transfers between devices: 19 us -> none  [the longest x1 5.47 us: local(): lax.all_to_all(wanted.reshape(replicas, 1), 'dp', split_axis=0, concat_ax...]
    all_to_all x4 -> x0, starting transfers between devices: 16.2 us -> none  [the longest x1 6.32 us: local(): lax.all_to_all(wanted.reshape(replicas, 1), 'dp', split_axis=0, concat_ax...]
    all_to_all x1 -> x0, blocking collectives: 8.1 us -> none  [local(): lax.all_to_all(send_values, 'dp', split_axis=0, concat_axis=0, tiled=True)]
    convert_element_type x3 -> x0, other arithmetic: 7.16 us -> none  [the longest x1 3.27 us: local(): (stream_in[0].astype(jnp.float32) + attended).astype(jnp.bfloat16)]
    unnamed x19 -> x0, local copies, waits for them, and re-layouts: 6.62 us -> none
    pallas_call x0 -> x5, Pallas kernels: none -> 6.5 us  [the longest x1 1.9 us: direct(): call(functools.partial(output_kernel, tokens, block_rows), 'outputs', (ja...]
    ppermute x2 -> x7, starting transfers between devices: 5.35 us -> 10.3 us  [the longest x6 10.2 us: around(): parts[d] = lax.ppermute(x, 'dp', [(i, i ^ d) for i in range(replicas)])]
    ppermute x2 -> x7, waiting for transfers between devices: 0.01 us -> 4.31 us  [the longest x6 4.31 us: around(): parts[d] = lax.ppermute(x, 'dp', [(i, i ^ d) for i in range(replicas)])]
  transfers between devices with their start and end apart: 6 -> 7, of which waited for: 4 -> 2; matrix products, arithmetic and copies ran while one was open for 15% -> 0% of each run, Pallas kernels for 0% -> 17%
where the time goes in v2:
time: 22 us; the launch traced here: 21.8 us
  starting transfers between devices  10.3 us (47%)
  Pallas kernels  6.5 us (30%)
  waiting for transfers between devices  4.31 us (20%)
  between operations  0.67 us (3%)
    ppermute x6, starting transfers between devices, around(): parts[d] = lax.ppermute(x, 'dp', [(i, i ^ d) for i in range(replicas)])  10.2 us
    ppermute x6, waiting for transfers between devices, around(): parts[d] = lax.ppermute(x, 'dp', [(i, i ^ d) for i in range(replicas)])  4.31 us
    pallas_call x1, Pallas kernels, direct(): call(functools.partial(output_kernel, tokens, block_rows), 'outputs', (ja...  1.9 us
    pallas_call x1, Pallas kernels, direct(): call(fetch_kernel, 'fetch', (rows, rows, sent, pltpu.SMEM((2,), jnp.int32...  1.9 us
    pallas_call x1, Pallas kernels, direct(): call(functools.partial(score_kernel, slots), 'scores', (pltpu.VMEM((block...  1.23 us
    pallas_call x1, Pallas kernels, direct(): call(stack_kernel, 'stack', pltpu.VMEM((2 * slots, block_rows, width), jn...  0.79 us
    pallas_call x1, Pallas kernels, direct(): call(functools.partial(sum_kernel, slots), 'sums', (jax.ShapeDtypeStruct(...  0.68 us
  transfers between devices with their start and end apart: 7, of which 2 were waited for; matrix products, arithmetic and copies ran while one was open for 0% of the time, Pallas kernels for 17%

profile of v2, /device:TPU:0, one launch (start us, length us, event | category | flops | bytes accessed | tf_op | source)
XLA Modules:
  0.0 21.8 jit_solution(11892489534828910899)
XLA Ops:
  0.6 0.8 %stack.1.refs_0_ = bf16[4,8,1024]{2,1,0:T(8,128)(2,1)S(1)} custom-call(bf16[2,8,1024]{2,1,0:T(8,128)(2,1)} %bitcast.13, bf16[2,8,1024]{2,1,0:T(8,128)(2,1)} %bitcast.14), custom_call_target="tpu_custom_call" | custom-call | tf_op jit(solution)/shard_map/stack/pallas_call | solution.py:232
  1.4 5.1 %collective-permute-start.2 = (bf16[4,8,1024]{2,1,0:T(8,128)(2,1)S(1)}, bf16[4,8,1024]{2,1,0:T(8,128)(2,1)S(1)}, u32[]{:S(2)}, u32[]{:S(2)}) collective-permute-start(bf16[4,8,1024]{2,1,0:T(8,128)(2,1)S(1)} %stack.1.refs_0_), channel_id=1, source_target_pairs={{0,12},{4,8},{8,4},{12,0},{1,13},{5,9},{9,5},{13,1},{2,14},{6,10},... | collective-permute-start | bytes 196616 | tf_op jit(solution)/shard_map/ppermute | solution.py:194
  6.5 0.0 collective-permute-start.1
  6.5 0.6 %collective-permute-start = (bf16[4,8,1024]{2,1,0:T(8,128)(2,1)S(1)}, bf16[4,8,1024]{2,1,0:T(8,128)(2,1)S(1)}, u32[]{:S(2)}, u32[]{:S(2)}) collective-permute-start(bf16[4,8,1024]{2,1,0:T(8,128)(2,1)S(1)} %stack.1.refs_0_), channel_id=1, source_target_pairs={{0,4},{4,0},{8,12},{12,8},{1,5},{5,1},{9,13},{13,9},{2,6},{6,2},{1... | collective-permute-start | bytes 196616 | tf_op jit(solution)/shard_map/ppermute | solution.py:194
  7.2 1.9 %fetch.1 = (bf16[512,1024]{1,0:T(8,128)(2,1)S(1)}, bf16[512,1024]{1,0:T(8,128)(2,1)S(1)}, bf16[560,1024]{1,0:T(8,128)(2,1)S(1)}, s32[2]{0:T(128)S(4)}) custom-call(s32[8]{0:T(128)} %map_ref, s32[2]{0:T(128)} %bitcast.15, bf16[512,1024]{1,0:T(8,128)(2,1)} %bitcast.10, bf16[512,1024]{1,0:T(8,128)(2,1)} %bitcast.11, bf16[512,1024]{1,0:T(8,128)(2,1)} %bitcast.12), custom_call_target="tpu_custom_call" | custom-call | bytes 6291456 | tf_op jit(solution)/shard_map/fetch/pallas_call | solution.py:243
  9.1 0.0 collective-permute-done.2.refs_3_
  9.1 3.0 %collective-permute-done.1.refs_2_ = bf16[4,8,1024]{2,1,0:T(8,128)(2,1)S(1)} collective-permute-done((bf16[4,8,1024]{2,1,0:T(8,128)(2,1)S(1)}, bf16[4,8,1024]{2,1,0:T(8,128)(2,1)S(1)}, u32[]{:S(2)}, u32[]{:S(2)}) %collective-permute-start.1) | collective-permute-done | bytes 65568 | tf_op jit(solution)/shard_map/ppermute | solution.py:194
  12.1 0.0 collective-permute-done.refs_1_
  12.2 1.2 %scores.1 = (bf16[8,2176]{1,0:T(8,128)(2,1)S(1)}, bf16[560,1024]{1,0:T(8,128)(2,1)S(1)}) custom-call(s32[2]{0:T(128)S(4)} %get-tuple-element.31.place_ref, bf16[512,1024]{1,0:T(8,128)(2,1)S(1)} %get-tuple-element.32.saved_ref, bf16[512,1024]{1,0:T(8,128)(2,1)S(1)} %get-tuple-element.33.grad_ref, ...), custom_call_target="tpu_custom_call", output_to_operand_aliasing={{1}: (3, {})} | custom-call | tf_op jit(solution)/shard_map/scores/pallas_call | solution.py:255
  13.4 0.1 collective-permute-start.6
  13.5 2.8 %collective-permute-start.5 = (bf16[8,2176]{1,0:T(8,128)(2,1)S(1)}, bf16[8,2176]{1,0:T(8,128)(2,1)S(1)}, u32[]{:S(2)}, u32[]{:S(2)}) collective-permute-start(bf16[8,2176]{1,0:T(8,128)(2,1)S(1)} %get-tuple-element.42.refs_0_), channel_id=1, source_target_pairs={{0,12},{4,8},{8,4},{12,0},{1,13},{5,9},{9,5},{13,1},{2,14},{6,10},... | collective-permute-start | bytes 104456 | tf_op jit(solution)/shard_map/ppermute | solution.py:194
  16.2 0.0 collective-permute-start.4
  16.2 1.7 %collective-permute-start.3 = (bf16[8,2176]{1,0:T(8,128)(2,1)S(1)}, bf16[8,2176]{1,0:T(8,128)(2,1)S(1)}, u32[]{:S(2)}, u32[]{:S(2)}) collective-permute-start(bf16[8,2176]{1,0:T(8,128)(2,1)S(1)} %get-tuple-element.42.refs_0_), channel_id=1, source_target_pairs={{0,4},{4,0},{8,12},{12,8},{1,5},{5,1},{9,13},{13,9},{2,6},{6,2},{1... | collective-permute-start | bytes 104456 | tf_op jit(solution)/shard_map/ppermute | solution.py:194
  17.9 0.0 collective-permute-done.6.sent_ref
  17.9 1.9 %outputs.1 = (bf16[512,1024]{1,0:T(8,128)(2,1)}, bf16[512,1024]{1,0:T(8,128)(2,1)}) custom-call(bf16[560,1024]{1,0:T(8,128)(2,1)S(1)} %collective-permute-done.6.sent_ref), custom_call_target="tpu_custom_call" | custom-call | bytes 2097152 | tf_op jit(solution)/shard_map/outputs/pallas_call | solution.py:264
  19.8 0.0 collective-permute-done.5.refs_3_
  19.8 1.3 %collective-permute-done.4.refs_2_ = bf16[8,2176]{1,0:T(8,128)(2,1)S(1)} collective-permute-done((bf16[8,2176]{1,0:T(8,128)(2,1)S(1)}, bf16[8,2176]{1,0:T(8,128)(2,1)S(1)}, u32[]{:S(2)}, u32[]{:S(2)}) %collective-permute-start.4) | collective-permute-done | bytes 34848 | tf_op jit(solution)/shard_map/ppermute | solution.py:194
  21.1 0.0 collective-permute-done.3.refs_1_
  21.1 0.7 %sums.1 = (bf16[2,8,1024]{2,1,0:T(8,128)(2,1)}, bf16[2,8,1024]{2,1,0:T(8,128)(2,1)}) custom-call(bf16[8,2176]{1,0:T(8,128)(2,1)S(1)} %get-tuple-element.42.refs_0_, bf16[8,2176]{1,0:T(8,128)(2,1)S(1)} %collective-permute-done.3.refs_1_, bf16[8,2176]{1,0:T(8,128)(2,1)S(1)} %collective-permute-done.4.refs_2_, bf16[8,2176]{1,0:T(8,128)(2,1)S(1)} %collective-permute-done.5.refs_3_), custom_call_target="tpu_custom_call" | custom-call | tf_op jit(solution)/shard_map/sums/pallas_call | solution.py:273
Async XLA Ops:
  1.4 7.7 %collective-permute-start.2 = (bf16[4,8,1024]{2,1,0:T(8,128)(2,1)S(1)}, bf16[4,8,1024]{2,1,0:T(8,128)(2,1)S(1)}, u32[]{:S(2)}, u32[]{:S(2)}) collective-permute-start(bf16[4,8,1024]{2,1,0:T(8,128)(2,1)S(1)} %stack.1.refs_0_), channel_id=1, source_target_pairs={{0,12},{4,8},{8,4},{12,0},{1,13},{5,9},{9,5},{13,1},{2,14},{6,10},... | collective-permute-start | bytes 196616 | tf_op jit(solution)/shard_map/ppermute | solution.py:194
  6.5 5.6 %collective-permute-start.1 = (bf16[4,8,1024]{2,1,0:T(8,128)(2,1)S(1)}, bf16[4,8,1024]{2,1,0:T(8,128)(2,1)S(1)}, u32[]{:S(2)}, u32[]{:S(2)}) collective-permute-start(bf16[4,8,1024]{2,1,0:T(8,128)(2,1)S(1)} %stack.1.refs_0_), channel_id=1, source_target_pairs={{0,8},{4,12},{8,0},{12,4},{1,9},{5,13},{9,1},{13,5},{2,10},{6,14},... | collective-permute-start | bytes 196616 | tf_op jit(solution)/shard_map/ppermute | solution.py:194
  6.5 5.6 %collective-permute-start = (bf16[4,8,1024]{2,1,0:T(8,128)(2,1)S(1)}, bf16[4,8,1024]{2,1,0:T(8,128)(2,1)S(1)}, u32[]{:S(2)}, u32[]{:S(2)}) collective-permute-start(bf16[4,8,1024]{2,1,0:T(8,128)(2,1)S(1)} %stack.1.refs_0_), channel_id=1, source_target_pairs={{0,4},{4,0},{8,12},{12,8},{1,5},{5,1},{9,13},{13,9},{2,6},{6,2},{1... | collective-permute-start | bytes 196616 | tf_op jit(solution)/shard_map/ppermute | solution.py:194
  13.4 4.5 %collective-permute-start.6 = (bf16[560,1024]{1,0:T(8,128)(2,1)S(1)}, bf16[560,1024]{1,0:T(8,128)(2,1)S(1)}, u32[]{:S(2)}, u32[]{:S(2)}) collective-permute-start(bf16[560,1024]{1,0:T(8,128)(2,1)S(1)} %get-tuple-element.37), channel_id=1, source_target_pairs={{0,16},{16,0},{1,17},{17,1},{2,18},{18,2},{3,19},{19,3},{4,20},{20... | collective-permute-start | bytes 3440648 | tf_op jit(solution)/shard_map/ppermute | solution.py:262
  13.5 6.4 %collective-permute-start.5 = (bf16[8,2176]{1,0:T(8,128)(2,1)S(1)}, bf16[8,2176]{1,0:T(8,128)(2,1)S(1)}, u32[]{:S(2)}, u32[]{:S(2)}) collective-permute-start(bf16[8,2176]{1,0:T(8,128)(2,1)S(1)} %get-tuple-element.42.refs_0_), channel_id=1, source_target_pairs={{0,12},{4,8},{8,4},{12,0},{1,13},{5,9},{9,5},{13,1},{2,14},{6,10},... | collective-permute-start | bytes 104456 | tf_op jit(solution)/shard_map/ppermute | solution.py:194
  16.2 4.8 %collective-permute-start.4 = (bf16[8,2176]{1,0:T(8,128)(2,1)S(1)}, bf16[8,2176]{1,0:T(8,128)(2,1)S(1)}, u32[]{:S(2)}, u32[]{:S(2)}) collective-permute-start(bf16[8,2176]{1,0:T(8,128)(2,1)S(1)} %get-tuple-element.42.refs_0_), channel_id=1, source_target_pairs={{0,8},{4,12},{8,0},{12,4},{1,9},{5,13},{9,1},{13,5},{2,10},{6,14},... | collective-permute-start | bytes 104456 | tf_op jit(solution)/shard_map/ppermute | solution.py:194
  16.2 4.8 %collective-permute-start.3 = (bf16[8,2176]{1,0:T(8,128)(2,1)S(1)}, bf16[8,2176]{1,0:T(8,128)(2,1)S(1)}, u32[]{:S(2)}, u32[]{:S(2)}) collective-permute-start(bf16[8,2176]{1,0:T(8,128)(2,1)S(1)} %get-tuple-element.42.refs_0_), channel_id=1, source_target_pairs={{0,4},{4,0},{8,12},{12,8},{1,5},{5,1},{9,13},{13,9},{2,6},{6,2},{1... | collective-permute-start | bytes 104456 | tf_op jit(solution)/shard_map/ppermute | solution.py:194

commit v3 on v2

--- a/solution.py
+++ b/solution.py
@@ -10,8 +10,6 @@
 
 HEAD_DIM = 128
 DIRECT_REPLICAS = 8
-FETCH_ORDER = (2, 3, 1)
-SEND_ORDER = (1, 3, 2)
 HBM = pl.BlockSpec(memory_space=pltpu.HBM)
 VMEM = pl.BlockSpec(memory_space=pltpu.VMEM)
 SMEM = pl.BlockSpec(memory_space=pltpu.SMEM)
@@ -52,10 +50,10 @@
     return exponent / jnp.sum(exponent, axis=1, keepdims=True)
 
 
-def pick(refs, first, owner, slot, me):
+def pick(refs, first, behind, slot):
     block = refs[0][first + slot]
-    for d in range(1, len(refs)):
-        block = jnp.where(owner == me ^ d, refs[d][first + slot], block)
+    for i in range(1, len(refs)):
+        block = jnp.where(behind == len(refs) - i, refs[i][first + slot], block)
     return block
 
 
@@ -106,12 +104,13 @@
 def score_kernel(slots, place_ref, saved_ref, grad_ref, rows_ref, *refs):
     memory, (terms_ref, sent_ref) = refs[:-2], refs[-2:]
     me = lax.axis_index("dp")
+    section = lax.axis_index("pipe")
     tokens, width = saved_ref.shape
     heads = width // HEAD_DIM
     back = place_ref[1]
-    owner, slot = back // slots, back % slots
-    keys = pick(memory, 0, owner, slot, me)
-    values = pick(memory, slots, owner, slot, me)
+    behind, slot = lax.rem(me - back // slots + len(memory), len(memory)), back % slots
+    keys = pick(memory, 0, behind, slot)
+    values = pick(memory, slots, behind, slot)
     count = keys.shape[0]
     saved, grads = saved_ref[...], grad_ref[...]
     weights = softmax_t(by_head(keys), saved, heads)
@@ -126,14 +125,13 @@
     place = jnp.full((count, HEAD_DIM), back, jnp.int32)
     terms_ref[:, 2 * width :] = place.astype(jnp.float32).astype(jnp.bfloat16)
     first, second = tokens, tokens + padded(count)
-    section = lax.axis_index("pipe")
 
     @pl.when(section == 0)
     def _():
         ahead = place_ref[0]
-        owner, slot = ahead // slots, ahead % slots
-        sent_ref[first : first + count, :] = pick(memory, 0, owner, slot, me)
-        sent_ref[second : second + count, :] = pick(memory, slots, owner, slot, me)
+        behind, slot = lax.rem(me - ahead // slots + len(memory), len(memory)), ahead % slots
+        sent_ref[first : first + count, :] = pick(memory, 0, behind, slot)
+        sent_ref[second : second + count, :] = pick(memory, slots, behind, slot)
 
     @pl.when(section != 0)
     def _():
@@ -188,11 +186,11 @@
             out[slot, :, j * HEAD_DIM : (j + 1) * HEAD_DIM] = total.astype(jnp.bfloat16)
 
 
-def around(x, replicas, order):
-    parts = {0: x}
-    for d in order:
-        parts[d] = lax.ppermute(x, "dp", [(i, i ^ d) for i in range(replicas)])
-    return [parts[d] for d in range(replicas)]
+def exchange(x, replicas):
+    return [x] + [
+        lax.ppermute(x, "dp", [(i, (i + d) % replicas) for i in range(replicas)])
+        for d in range(replicas - 1, 0, -1)
+    ]
 
 
 def vmem(x):
@@ -239,7 +237,7 @@
     stacked, *own = lax.optimization_barrier(
         (stacked, owner_map, block_ids.reshape(-1), stream_in[0], saved_in[0], grad_out[0])
     )
-    memory = around(stacked, replicas, FETCH_ORDER)
+    memory = exchange(stacked, replicas)
     saved, grads, to_send, places = call(
         fetch_kernel,
         "fetch",
@@ -260,7 +258,7 @@
         aliases={3: 1}.items(),
     )(smem(places), *map(vmem, (saved, grads, to_send, *memory)))
     other_sent = lax.ppermute(to_send, "pipe", [(0, 1), (1, 0)])
-    term_parts = around(terms, replicas, SEND_ORDER)
+    term_parts = exchange(terms, replicas)
     next_input, grad_back = call(
         functools.partial(output_kernel, tokens, block_rows),
         "outputs",
@@ -396,7 +394,7 @@
 
 def local(*args):
     replicas, (_, tokens, width) = lax.axis_size("dp"), args[0].shape
-    few = replicas <= DIRECT_REPLICAS and replicas & (replicas - 1) == 0
+    few = replicas <= DIRECT_REPLICAS
     one_each = args[-1].size == 2 and lax.axis_size("pipe") == 2 and width % tokens == 0
     return (direct if few and one_each else routed)(*args)
 

time: 22 us -> 21.6 us (0.982)
  waiting for transfers between devices: 4.31 us -> 3.05 us
  starting transfers between devices: 10.3 us -> 11.2 us
    ppermute x6, waiting for transfers between devices: 4.31 us -> 3.05 us  [exchange(): lax.ppermute(x, 'dp', [(i, (i + d) % replicas) for i in range(replicas)])]
    ppermute x6, starting transfers between devices: 10.2 us -> 11.1 us  [exchange(): lax.ppermute(x, 'dp', [(i, (i + d) % replicas) for i in range(replicas)])]
  transfers between devices with their start and end apart: 7 -> 7, of which waited for: 2 -> 5; matrix products, arithmetic and copies ran while one was open for 0% -> 0% of each run, Pallas kernels for 17% -> 18%
where the time goes in v3:
time: 21.6 us; the launch traced here: 21.4 us
  starting transfers between devices  11.2 us (52%)
  Pallas kernels  6.5 us (30%)
  waiting for transfers between devices  3.05 us (14%)
  between operations  0.68 us (3%)
    ppermute x6, starting transfers between devices, exchange(): lax.ppermute(x, 'dp', [(i, (i + d) % replicas) for i in range(replicas)])  11.1 us
    ppermute x6, waiting for transfers between devices, exchange(): lax.ppermute(x, 'dp', [(i, (i + d) % replicas) for i in range(replicas)])  3.05 us
    pallas_call x1, Pallas kernels, direct(): call(functools.partial(output_kernel, tokens, block_rows), 'outputs', (ja...  1.91 us
    pallas_call x1, Pallas kernels, direct(): call(fetch_kernel, 'fetch', (rows, rows, sent, pltpu.SMEM((2,), jnp.int32...  1.9 us
    pallas_call x1, Pallas kernels, direct(): call(functools.partial(score_kernel, slots), 'scores', (pltpu.VMEM((block...  1.23 us
    pallas_call x1, Pallas kernels, direct(): call(stack_kernel, 'stack', pltpu.VMEM((2 * slots, block_rows, width), jn...  0.79 us
    pallas_call x1, Pallas kernels, direct(): call(functools.partial(sum_kernel, slots), 'sums', (jax.ShapeDtypeStruct(...  0.68 us
  transfers between devices with their start and end apart: 7, of which 5 were waited for; matrix products, arithmetic and copies ran while one was open for 0% of the time, Pallas kernels for 18%

profile of v3, /device:TPU:0, one launch (start us, length us, event | category | flops | bytes accessed | tf_op | source)
XLA Modules:
  0.0 21.4 jit_solution(3518057939948235708)
XLA Ops:
  0.6 0.8 %stack.1.refs_0_ = bf16[4,8,1024]{2,1,0:T(8,128)(2,1)S(1)} custom-call(bf16[2,8,1024]{2,1,0:T(8,128)(2,1)} %bitcast.13, bf16[2,8,1024]{2,1,0:T(8,128)(2,1)} %bitcast.14), custom_call_target="tpu_custom_call" | custom-call | tf_op jit(solution)/shard_map/stack/pallas_call | solution.py:230
  1.4 3.1 %collective-permute-start.2 = (bf16[4,8,1024]{2,1,0:T(8,128)(2,1)S(1)}, bf16[4,8,1024]{2,1,0:T(8,128)(2,1)S(1)}, u32[]{:S(2)}, u32[]{:S(2)}) collective-permute-start(bf16[4,8,1024]{2,1,0:T(8,128)(2,1)S(1)} %stack.1.refs_0_), channel_id=1, source_target_pairs={{0,4},{4,8},{8,12},{12,0},{1,5},{5,9},{9,13},{13,1},{2,6},{6,10},{... | collective-permute-start | bytes 196616 | tf_op jit(solution)/shard_map/ppermute | solution.py:191
  4.5 2.6 %collective-permute-start.1 = (bf16[4,8,1024]{2,1,0:T(8,128)(2,1)S(1)}, bf16[4,8,1024]{2,1,0:T(8,128)(2,1)S(1)}, u32[]{:S(2)}, u32[]{:S(2)}) collective-permute-start(bf16[4,8,1024]{2,1,0:T(8,128)(2,1)S(1)} %stack.1.refs_0_), channel_id=1, source_target_pairs={{0,8},{4,12},{8,0},{12,4},{1,9},{5,13},{9,1},{13,5},{2,10},{6,14},... | collective-permute-start | bytes 196616 | tf_op jit(solution)/shard_map/ppermute | solution.py:191
  7.1 1.3 %collective-permute-start = (bf16[4,8,1024]{2,1,0:T(8,128)(2,1)S(1)}, bf16[4,8,1024]{2,1,0:T(8,128)(2,1)S(1)}, u32[]{:S(2)}, u32[]{:S(2)}) collective-permute-start(bf16[4,8,1024]{2,1,0:T(8,128)(2,1)S(1)} %stack.1.refs_0_), channel_id=1, source_target_pairs={{0,12},{4,0},{8,4},{12,8},{1,13},{5,1},{9,5},{13,9},{2,14},{6,2},{... | collective-permute-start | bytes 196616 | tf_op jit(solution)/shard_map/ppermute | solution.py:191
  8.4 1.9 %fetch.1 = (bf16[512,1024]{1,0:T(8,128)(2,1)S(1)}, bf16[512,1024]{1,0:T(8,128)(2,1)S(1)}, bf16[560,1024]{1,0:T(8,128)(2,1)S(1)}, s32[2]{0:T(128)S(4)}) custom-call(s32[8]{0:T(128)} %map_ref, s32[2]{0:T(128)} %bitcast.15, bf16[512,1024]{1,0:T(8,128)(2,1)} %bitcast.10, bf16[512,1024]{1,0:T(8,128)(2,1)} %bitcast.11, bf16[512,1024]{1,0:T(8,128)(2,1)} %bitcast.12), custom_call_target="tpu_custom_call" | custom-call | bytes 6291456 | tf_op jit(solution)/shard_map/fetch/pallas_call | solution.py:241
  10.4 0.0 collective-permute-done.2.refs_3_
  10.4 1.2 %collective-permute-done.1.refs_2_ = bf16[4,8,1024]{2,1,0:T(8,128)(2,1)S(1)} collective-permute-done((bf16[4,8,1024]{2,1,0:T(8,128)(2,1)S(1)}, bf16[4,8,1024]{2,1,0:T(8,128)(2,1)S(1)}, u32[]{:S(2)}, u32[]{:S(2)}) %collective-permute-start.1) | collective-permute-done | bytes 65568 | tf_op jit(solution)/shard_map/ppermute | solution.py:191
  11.6 0.2 %collective-permute-done.refs_1_ = bf16[4,8,1024]{2,1,0:T(8,128)(2,1)S(1)} collective-permute-done((bf16[4,8,1024]{2,1,0:T(8,128)(2,1)S(1)}, bf16[4,8,1024]{2,1,0:T(8,128)(2,1)S(1)}, u32[]{:S(2)}, u32[]{:S(2)}) %collective-permute-start) | collective-permute-done | bytes 65568 | tf_op jit(solution)/shard_map/ppermute | solution.py:191
  11.8 1.2 %scores.1 = (bf16[8,2176]{1,0:T(8,128)(2,1)S(1)}, bf16[560,1024]{1,0:T(8,128)(2,1)S(1)}) custom-call(s32[2]{0:T(128)S(4)} %get-tuple-element.31.place_ref, bf16[512,1024]{1,0:T(8,128)(2,1)S(1)} %get-tuple-element.32.saved_ref, bf16[512,1024]{1,0:T(8,128)(2,1)S(1)} %get-tuple-element.33.grad_ref, ...), custom_call_target="tpu_custom_call", output_to_operand_aliasing={{1}: (3, {})} | custom-call | tf_op jit(solution)/shard_map/scores/pallas_call | solution.py:253
  13.0 0.1 collective-permute-start.6
  13.1 1.6 %collective-permute-start.5 = (bf16[8,2176]{1,0:T(8,128)(2,1)S(1)}, bf16[8,2176]{1,0:T(8,128)(2,1)S(1)}, u32[]{:S(2)}, u32[]{:S(2)}) collective-permute-start(bf16[8,2176]{1,0:T(8,128)(2,1)S(1)} %get-tuple-element.42.refs_0_), channel_id=1, source_target_pairs={{0,4},{4,8},{8,12},{12,0},{1,5},{5,9},{9,13},{13,1},{2,6},{6,10},{... | collective-permute-start | bytes 104456 | tf_op jit(solution)/shard_map/ppermute | solution.py:191
  14.8 2.0 %collective-permute-start.4 = (bf16[8,2176]{1,0:T(8,128)(2,1)S(1)}, bf16[8,2176]{1,0:T(8,128)(2,1)S(1)}, u32[]{:S(2)}, u32[]{:S(2)}) collective-permute-start(bf16[8,2176]{1,0:T(8,128)(2,1)S(1)} %get-tuple-element.42.refs_0_), channel_id=1, source_target_pairs={{0,8},{4,12},{8,0},{12,4},{1,9},{5,13},{9,1},{13,5},{2,10},{6,14},... | collective-permute-start | bytes 104456 | tf_op jit(solution)/shard_map/ppermute | solution.py:191
  16.8 0.4 %collective-permute-start.3 = (bf16[8,2176]{1,0:T(8,128)(2,1)S(1)}, bf16[8,2176]{1,0:T(8,128)(2,1)S(1)}, u32[]{:S(2)}, u32[]{:S(2)}) collective-permute-start(bf16[8,2176]{1,0:T(8,128)(2,1)S(1)} %get-tuple-element.42.refs_0_), channel_id=1, source_target_pairs={{0,12},{4,0},{8,4},{12,8},{1,13},{5,1},{9,5},{13,9},{2,14},{6,2},{... | collective-permute-start | bytes 104456 | tf_op jit(solution)/shard_map/ppermute | solution.py:191
  17.2 0.0 collective-permute-done.6.sent_ref
  17.2 1.9 %outputs.1 = (bf16[512,1024]{1,0:T(8,128)(2,1)}, bf16[512,1024]{1,0:T(8,128)(2,1)}) custom-call(bf16[560,1024]{1,0:T(8,128)(2,1)S(1)} %collective-permute-done.6.sent_ref), custom_call_target="tpu_custom_call" | custom-call | bytes 2097152 | tf_op jit(solution)/shard_map/outputs/pallas_call | solution.py:262
  19.1 0.1 collective-permute-done.5.refs_3_
  19.2 1.1 %collective-permute-done.4.refs_2_ = bf16[8,2176]{1,0:T(8,128)(2,1)S(1)} collective-permute-done((bf16[8,2176]{1,0:T(8,128)(2,1)S(1)}, bf16[8,2176]{1,0:T(8,128)(2,1)S(1)}, u32[]{:S(2)}, u32[]{:S(2)}) %collective-permute-start.4) | collective-permute-done | bytes 34848 | tf_op jit(solution)/shard_map/ppermute | solution.py:191
  20.3 0.4 %collective-permute-done.3.refs_1_ = bf16[8,2176]{1,0:T(8,128)(2,1)S(1)} collective-permute-done((bf16[8,2176]{1,0:T(8,128)(2,1)S(1)}, bf16[8,2176]{1,0:T(8,128)(2,1)S(1)}, u32[]{:S(2)}, u32[]{:S(2)}) %collective-permute-start.3) | collective-permute-done | bytes 34848 | tf_op jit(solution)/shard_map/ppermute | solution.py:191
  20.7 0.7 %sums.1 = (bf16[2,8,1024]{2,1,0:T(8,128)(2,1)}, bf16[2,8,1024]{2,1,0:T(8,128)(2,1)}) custom-call(bf16[8,2176]{1,0:T(8,128)(2,1)S(1)} %get-tuple-element.42.refs_0_, bf16[8,2176]{1,0:T(8,128)(2,1)S(1)} %collective-permute-done.3.refs_1_, bf16[8,2176]{1,0:T(8,128)(2,1)S(1)} %collective-permute-done.4.refs_2_, bf16[8,2176]{1,0:T(8,128)(2,1)S(1)} %collective-permute-done.5.refs_3_), custom_call_target="tpu_custom_call" | custom-call | tf_op jit(solution)/shard_map/sums/pallas_call | solution.py:271
Async XLA Ops:
  1.4 8.9 %collective-permute-start.2 = (bf16[4,8,1024]{2,1,0:T(8,128)(2,1)S(1)}, bf16[4,8,1024]{2,1,0:T(8,128)(2,1)S(1)}, u32[]{:S(2)}, u32[]{:S(2)}) collective-permute-start(bf16[4,8,1024]{2,1,0:T(8,128)(2,1)S(1)} %stack.1.refs_0_), channel_id=1, source_target_pairs={{0,4},{4,8},{8,12},{12,0},{1,5},{5,9},{9,13},{13,1},{2,6},{6,10},{... | collective-permute-start | bytes 196616 | tf_op jit(solution)/shard_map/ppermute | solution.py:191
  4.5 7.1 %collective-permute-start.1 = (bf16[4,8,1024]{2,1,0:T(8,128)(2,1)S(1)}, bf16[4,8,1024]{2,1,0:T(8,128)(2,1)S(1)}, u32[]{:S(2)}, u32[]{:S(2)}) collective-permute-start(bf16[4,8,1024]{2,1,0:T(8,128)(2,1)S(1)} %stack.1.refs_0_), channel_id=1, source_target_pairs={{0,8},{4,12},{8,0},{12,4},{1,9},{5,13},{9,1},{13,5},{2,10},{6,14},... | collective-permute-start | bytes 196616 | tf_op jit(solution)/shard_map/ppermute | solution.py:191
  7.1 4.7 %collective-permute-start = (bf16[4,8,1024]{2,1,0:T(8,128)(2,1)S(1)}, bf16[4,8,1024]{2,1,0:T(8,128)(2,1)S(1)}, u32[]{:S(2)}, u32[]{:S(2)}) collective-permute-start(bf16[4,8,1024]{2,1,0:T(8,128)(2,1)S(1)} %stack.1.refs_0_), channel_id=1, source_target_pairs={{0,12},{4,0},{8,4},{12,8},{1,13},{5,1},{9,5},{13,9},{2,14},{6,2},{... | collective-permute-start | bytes 196616 | tf_op jit(solution)/shard_map/ppermute | solution.py:191
  13.0 4.2 %collective-permute-start.6 = (bf16[560,1024]{1,0:T(8,128)(2,1)S(1)}, bf16[560,1024]{1,0:T(8,128)(2,1)S(1)}, u32[]{:S(2)}, u32[]{:S(2)}) collective-permute-start(bf16[560,1024]{1,0:T(8,128)(2,1)S(1)} %get-tuple-element.37), channel_id=1, source_target_pairs={{0,16},{16,0},{1,17},{17,1},{2,18},{18,2},{3,19},{19,3},{4,20},{20... | collective-permute-start | bytes 3440648 | tf_op jit(solution)/shard_map/ppermute | solution.py:260
  13.1 6.1 %collective-permute-start.5 = (bf16[8,2176]{1,0:T(8,128)(2,1)S(1)}, bf16[8,2176]{1,0:T(8,128)(2,1)S(1)}, u32[]{:S(2)}, u32[]{:S(2)}) collective-permute-start(bf16[8,2176]{1,0:T(8,128)(2,1)S(1)} %get-tuple-element.42.refs_0_), channel_id=1, source_target_pairs={{0,4},{4,8},{8,12},{12,0},{1,5},{5,9},{9,13},{13,1},{2,6},{6,10},{... | collective-permute-start | bytes 104456 | tf_op jit(solution)/shard_map/ppermute | solution.py:191
  14.8 5.6 %collective-permute-start.4 = (bf16[8,2176]{1,0:T(8,128)(2,1)S(1)}, bf16[8,2176]{1,0:T(8,128)(2,1)S(1)}, u32[]{:S(2)}, u32[]{:S(2)}) collective-permute-start(bf16[8,2176]{1,0:T(8,128)(2,1)S(1)} %get-tuple-element.42.refs_0_), channel_id=1, source_target_pairs={{0,8},{4,12},{8,0},{12,4},{1,9},{5,13},{9,1},{13,5},{2,10},{6,14},... | collective-permute-start | bytes 104456 | tf_op jit(solution)/shard_map/ppermute | solution.py:191
  16.8 3.9 %collective-permute-start.3 = (bf16[8,2176]{1,0:T(8,128)(2,1)S(1)}, bf16[8,2176]{1,0:T(8,128)(2,1)S(1)}, u32[]{:S(2)}, u32[]{:S(2)}) collective-permute-start(bf16[8,2176]{1,0:T(8,128)(2,1)S(1)} %get-tuple-element.42.refs_0_), channel_id=1, source_target_pairs={{0,12},{4,0},{8,4},{12,8},{1,13},{5,1},{9,5},{13,9},{2,14},{6,2},{... | collective-permute-start | bytes 104456 | tf_op jit(solution)/shard_map/ppermute | solution.py:191

commit v4 on v3

--- a/solution.py
+++ b/solution.py
@@ -35,17 +35,31 @@
     return jnp.where(head == feature_head, wide, 0.0).reshape(heads * keys, width).astype(block.dtype)
 
 
-def own_head(product, keys):
-    heads = product.shape[0] // keys
-    parts = [
-        product[h * keys : (h + 1) * keys, h * HEAD_DIM : (h + 1) * HEAD_DIM] for h in range(heads)
-    ]
+def groups(width):
+    step = min(width, 2 * HEAD_DIM)
+    return [slice(i, i + step) for i in range(0, width, step)]
+
+
+def per_head(block, rows):
+    parts = [dot(by_head(block[:, at]), rows[:, at], NT) for at in groups(rows.shape[1])]
+    return jnp.concatenate(parts, axis=0).reshape(-1, block.shape[0], rows.shape[0])
+
+
+def reduced(by_key, rows):
+    keys, tokens = by_key.shape[1:]
+    parts = []
+    for at in groups(rows.shape[1]):
+        heads = slice(at.start // HEAD_DIM, at.stop // HEAD_DIM)
+        product = dot(by_key[heads].reshape(-1, tokens), rows[:, at], NN)
+        parts += [
+            product[h * keys : (h + 1) * keys, h * HEAD_DIM : (h + 1) * HEAD_DIM]
+            for h in range(heads.stop - heads.start)
+        ]
     return jnp.concatenate(parts, axis=1)
 
 
-def softmax_t(keys_by_head, rows, heads):
-    scores = dot(keys_by_head, rows, NT) * (1.0 / math.sqrt(HEAD_DIM))
-    scores = scores.reshape(heads, -1, rows.shape[0])
+def softmax_t(keys, rows):
+    scores = per_head(keys, rows) * (1.0 / math.sqrt(HEAD_DIM))
     exponent = jnp.exp(scores - jnp.max(scores, axis=1, keepdims=True))
     return exponent / jnp.sum(exponent, axis=1, keepdims=True)
 
@@ -113,15 +127,15 @@
     values = pick(memory, slots, behind, slot)
     count = keys.shape[0]
     saved, grads = saved_ref[...], grad_ref[...]
-    weights = softmax_t(by_head(keys), saved, heads)
-    grad_weights = dot(by_head(values), grads, NT).reshape(weights.shape)
+    weights = softmax_t(keys, saved)
+    grad_weights = per_head(values, grads)
     centre = jnp.sum(weights * grad_weights, axis=1, keepdims=True)
     grad_scores = weights * (grad_weights - centre) * (1.0 / math.sqrt(HEAD_DIM))
     flat = heads * count
-    grad_scores = grad_scores.astype(jnp.bfloat16).reshape(flat, tokens)
-    rounded = weights.astype(jnp.bfloat16).reshape(flat, tokens)
-    terms_ref[:, :width] = own_head(dot(grad_scores, saved, NN), count).astype(jnp.bfloat16)
-    terms_ref[:, width : 2 * width] = own_head(dot(rounded, grads, NN), count).astype(jnp.bfloat16)
+    grad_scores = grad_scores.astype(jnp.bfloat16)
+    terms_ref[:, :width] = reduced(grad_scores, saved).astype(jnp.bfloat16)
+    terms_ref[:, width : 2 * width] = reduced(weights.astype(jnp.bfloat16), grads).astype(jnp.bfloat16)
+    grad_scores = grad_scores.reshape(flat, tokens)
     place = jnp.full((count, HEAD_DIM), back, jnp.int32)
     terms_ref[:, 2 * width :] = place.astype(jnp.float32).astype(jnp.bfloat16)
     first, second = tokens, tokens + padded(count)
@@ -146,7 +160,7 @@
     width = sent_ref.shape[1]
     heads = width // HEAD_DIM
     first, second = tokens, tokens + padded(count)
-    keys = by_head(sent_ref[first : first + count, :])
+    keys = sent_ref[first : first + count, :]
     rows = sent_ref[:tokens, :]
     section = lax.axis_index("pipe")
 
@@ -158,14 +172,14 @@
             sent_ref[second : second + part, i * tokens : (i + 1) * tokens]
             for i in range(width // tokens)
         ]
-        added = dot(jnp.concatenate(grad_scores, axis=0), keys, TN)
+        added = dot(jnp.concatenate(grad_scores, axis=0), by_head(keys), TN)
         back_ref[...] = (rows.astype(jnp.float32) + added).astype(jnp.bfloat16)
 
     @pl.when(section != 0)
     def _():
         back_ref[...] = jnp.zeros_like(back_ref)
         values = by_head(sent_ref[second : second + count, :])
-        weights = softmax_t(keys, rows, heads).astype(jnp.bfloat16).reshape(-1, tokens)
+        weights = softmax_t(keys, rows).astype(jnp.bfloat16).reshape(-1, tokens)
         added = dot(weights, values, TN)
         next_ref[...] = (rows.astype(jnp.float32) + added).astype(jnp.bfloat16)
 

time: 21.6 us -> 21.4 us (level)
  Pallas kernels: 6.5 us -> 6.21 us
    pallas_call x1, Pallas kernels: 1.23 us -> 0.97 us  [direct(): call(functools.partial(score_kernel, slots), 'scores', (pltpu.VMEM((block...]
where the time goes in v4:
time: 21.4 us; the launch traced here: 21.2 us
  starting transfers between devices  11.2 us (52%)
  Pallas kernels  6.21 us (29%)
  waiting for transfers between devices  3.08 us (14%)
  between operations  0.68 us (3%)
    ppermute x6, starting transfers between devices, exchange(): lax.ppermute(x, 'dp', [(i, (i + d) % replicas) for i in range(replicas)])  11.1 us
    ppermute x6, waiting for transfers between devices, exchange(): lax.ppermute(x, 'dp', [(i, (i + d) % replicas) for i in range(replicas)])  3.08 us
    pallas_call x1, Pallas kernels, direct(): call(fetch_kernel, 'fetch', (rows, rows, sent, pltpu.SMEM((2,), jnp.int32...  1.9 us
    pallas_call x1, Pallas kernels, direct(): call(functools.partial(output_kernel, tokens, block_rows), 'outputs', (ja...  1.87 us
    pallas_call x1, Pallas kernels, direct(): call(functools.partial(score_kernel, slots), 'scores', (pltpu.VMEM((block...  0.97 us
    pallas_call x1, Pallas kernels, direct(): call(stack_kernel, 'stack', pltpu.VMEM((2 * slots, block_rows, width), jn...  0.79 us
    pallas_call x1, Pallas kernels, direct(): call(functools.partial(sum_kernel, slots), 'sums', (jax.ShapeDtypeStruct(...  0.68 us
  transfers between devices with their start and end apart: 7, of which 5 were waited for; matrix products, arithmetic and copies ran while one was open for 0% of the time, Pallas kernels for 18%

profile of v4, /device:TPU:0, one launch (start us, length us, event | category | flops | bytes accessed | tf_op | source)
XLA Modules:
  0.0 21.2 jit_solution(2029378257984464222)
XLA Ops:
  0.6 0.8 %stack.1.refs_0_ = bf16[4,8,1024]{2,1,0:T(8,128)(2,1)S(1)} custom-call(bf16[2,8,1024]{2,1,0:T(8,128)(2,1)} %bitcast.13, bf16[2,8,1024]{2,1,0:T(8,128)(2,1)} %bitcast.14), custom_call_target="tpu_custom_call" | custom-call | tf_op jit(solution)/shard_map/stack/pallas_call | solution.py:244
  1.4 3.1 %collective-permute-start.2 = (bf16[4,8,1024]{2,1,0:T(8,128)(2,1)S(1)}, bf16[4,8,1024]{2,1,0:T(8,128)(2,1)S(1)}, u32[]{:S(2)}, u32[]{:S(2)}) collective-permute-start(bf16[4,8,1024]{2,1,0:T(8,128)(2,1)S(1)} %stack.1.refs_0_), channel_id=1, source_target_pairs={{0,4},{4,8},{8,12},{12,0},{1,5},{5,9},{9,13},{13,1},{2,6},{6,10},{... | collective-permute-start | bytes 196616 | tf_op jit(solution)/shard_map/ppermute | solution.py:205
  4.5 2.6 %collective-permute-start.1 = (bf16[4,8,1024]{2,1,0:T(8,128)(2,1)S(1)}, bf16[4,8,1024]{2,1,0:T(8,128)(2,1)S(1)}, u32[]{:S(2)}, u32[]{:S(2)}) collective-permute-start(bf16[4,8,1024]{2,1,0:T(8,128)(2,1)S(1)} %stack.1.refs_0_), channel_id=1, source_target_pairs={{0,8},{4,12},{8,0},{12,4},{1,9},{5,13},{9,1},{13,5},{2,10},{6,14},... | collective-permute-start | bytes 196616 | tf_op jit(solution)/shard_map/ppermute | solution.py:205
  7.1 1.3 %collective-permute-start = (bf16[4,8,1024]{2,1,0:T(8,128)(2,1)S(1)}, bf16[4,8,1024]{2,1,0:T(8,128)(2,1)S(1)}, u32[]{:S(2)}, u32[]{:S(2)}) collective-permute-start(bf16[4,8,1024]{2,1,0:T(8,128)(2,1)S(1)} %stack.1.refs_0_), channel_id=1, source_target_pairs={{0,12},{4,0},{8,4},{12,8},{1,13},{5,1},{9,5},{13,9},{2,14},{6,2},{... | collective-permute-start | bytes 196616 | tf_op jit(solution)/shard_map/ppermute | solution.py:205
  8.4 1.9 %fetch.1 = (bf16[512,1024]{1,0:T(8,128)(2,1)S(1)}, bf16[512,1024]{1,0:T(8,128)(2,1)S(1)}, bf16[560,1024]{1,0:T(8,128)(2,1)S(1)}, s32[2]{0:T(128)S(4)}) custom-call(s32[8]{0:T(128)} %map_ref, s32[2]{0:T(128)} %bitcast.15, bf16[512,1024]{1,0:T(8,128)(2,1)} %bitcast.10, bf16[512,1024]{1,0:T(8,128)(2,1)} %bitcast.11, bf16[512,1024]{1,0:T(8,128)(2,1)} %bitcast.12), custom_call_target="tpu_custom_call" | custom-call | bytes 6291456 | tf_op jit(solution)/shard_map/fetch/pallas_call | solution.py:255
  10.4 0.0 collective-permute-done.2.refs_3_
  10.4 1.2 %collective-permute-done.1.refs_2_ = bf16[4,8,1024]{2,1,0:T(8,128)(2,1)S(1)} collective-permute-done((bf16[4,8,1024]{2,1,0:T(8,128)(2,1)S(1)}, bf16[4,8,1024]{2,1,0:T(8,128)(2,1)S(1)}, u32[]{:S(2)}, u32[]{:S(2)}) %collective-permute-start.1) | collective-permute-done | bytes 65568 | tf_op jit(solution)/shard_map/ppermute | solution.py:205
  11.6 0.2 %collective-permute-done.refs_1_ = bf16[4,8,1024]{2,1,0:T(8,128)(2,1)S(1)} collective-permute-done((bf16[4,8,1024]{2,1,0:T(8,128)(2,1)S(1)}, bf16[4,8,1024]{2,1,0:T(8,128)(2,1)S(1)}, u32[]{:S(2)}, u32[]{:S(2)}) %collective-permute-start) | collective-permute-done | bytes 65568 | tf_op jit(solution)/shard_map/ppermute | solution.py:205
  11.8 1.0 %scores.1 = (bf16[8,2176]{1,0:T(8,128)(2,1)S(1)}, bf16[560,1024]{1,0:T(8,128)(2,1)S(1)}) custom-call(s32[2]{0:T(128)S(4)} %get-tuple-element.31.place_ref, bf16[512,1024]{1,0:T(8,128)(2,1)S(1)} %get-tuple-element.32.saved_ref, bf16[512,1024]{1,0:T(8,128)(2,1)S(1)} %get-tuple-element.33.grad_ref, ...), custom_call_target="tpu_custom_call", output_to_operand_aliasing={{1}: (3, {})} | custom-call | tf_op jit(solution)/shard_map/scores/pallas_call | solution.py:267
  12.8 0.1 collective-permute-start.6
  12.9 1.6 %collective-permute-start.5 = (bf16[8,2176]{1,0:T(8,128)(2,1)S(1)}, bf16[8,2176]{1,0:T(8,128)(2,1)S(1)}, u32[]{:S(2)}, u32[]{:S(2)}) collective-permute-start(bf16[8,2176]{1,0:T(8,128)(2,1)S(1)} %get-tuple-element.42.refs_0_), channel_id=1, source_target_pairs={{0,4},{4,8},{8,12},{12,0},{1,5},{5,9},{9,13},{13,1},{2,6},{6,10},{... | collective-permute-start | bytes 104456 | tf_op jit(solution)/shard_map/ppermute | solution.py:205
  14.5 2.0 %collective-permute-start.4 = (bf16[8,2176]{1,0:T(8,128)(2,1)S(1)}, bf16[8,2176]{1,0:T(8,128)(2,1)S(1)}, u32[]{:S(2)}, u32[]{:S(2)}) collective-permute-start(bf16[8,2176]{1,0:T(8,128)(2,1)S(1)} %get-tuple-element.42.refs_0_), channel_id=1, source_target_pairs={{0,8},{4,12},{8,0},{12,4},{1,9},{5,13},{9,1},{13,5},{2,10},{6,14},... | collective-permute-start | bytes 104456 | tf_op jit(solution)/shard_map/ppermute | solution.py:205
  16.5 0.4 %collective-permute-start.3 = (bf16[8,2176]{1,0:T(8,128)(2,1)S(1)}, bf16[8,2176]{1,0:T(8,128)(2,1)S(1)}, u32[]{:S(2)}, u32[]{:S(2)}) collective-permute-start(bf16[8,2176]{1,0:T(8,128)(2,1)S(1)} %get-tuple-element.42.refs_0_), channel_id=1, source_target_pairs={{0,12},{4,0},{8,4},{12,8},{1,13},{5,1},{9,5},{13,9},{2,14},{6,2},{... | collective-permute-start | bytes 104456 | tf_op jit(solution)/shard_map/ppermute | solution.py:205
  17.0 0.0 collective-permute-done.6.sent_ref
  17.0 1.9 %outputs.1 = (bf16[512,1024]{1,0:T(8,128)(2,1)}, bf16[512,1024]{1,0:T(8,128)(2,1)}) custom-call(bf16[560,1024]{1,0:T(8,128)(2,1)S(1)} %collective-permute-done.6.sent_ref), custom_call_target="tpu_custom_call" | custom-call | bytes 2097152 | tf_op jit(solution)/shard_map/outputs/pallas_call | solution.py:276
  18.8 0.1 collective-permute-done.5.refs_3_
  19.0 1.1 %collective-permute-done.4.refs_2_ = bf16[8,2176]{1,0:T(8,128)(2,1)S(1)} collective-permute-done((bf16[8,2176]{1,0:T(8,128)(2,1)S(1)}, bf16[8,2176]{1,0:T(8,128)(2,1)S(1)}, u32[]{:S(2)}, u32[]{:S(2)}) %collective-permute-start.4) | collective-permute-done | bytes 34848 | tf_op jit(solution)/shard_map/ppermute | solution.py:205
  20.1 0.4 %collective-permute-done.3.refs_1_ = bf16[8,2176]{1,0:T(8,128)(2,1)S(1)} collective-permute-done((bf16[8,2176]{1,0:T(8,128)(2,1)S(1)}, bf16[8,2176]{1,0:T(8,128)(2,1)S(1)}, u32[]{:S(2)}, u32[]{:S(2)}) %collective-permute-start.3) | collective-permute-done | bytes 34848 | tf_op jit(solution)/shard_map/ppermute | solution.py:205
  20.5 0.7 %sums.1 = (bf16[2,8,1024]{2,1,0:T(8,128)(2,1)}, bf16[2,8,1024]{2,1,0:T(8,128)(2,1)}) custom-call(bf16[8,2176]{1,0:T(8,128)(2,1)S(1)} %get-tuple-element.42.refs_0_, bf16[8,2176]{1,0:T(8,128)(2,1)S(1)} %collective-permute-done.3.refs_1_, bf16[8,2176]{1,0:T(8,128)(2,1)S(1)} %collective-permute-done.4.refs_2_, bf16[8,2176]{1,0:T(8,128)(2,1)S(1)} %collective-permute-done.5.refs_3_), custom_call_target="tpu_custom_call" | custom-call | tf_op jit(solution)/shard_map/sums/pallas_call | solution.py:285
Async XLA Ops:
  1.4 8.9 %collective-permute-start.2 = (bf16[4,8,1024]{2,1,0:T(8,128)(2,1)S(1)}, bf16[4,8,1024]{2,1,0:T(8,128)(2,1)S(1)}, u32[]{:S(2)}, u32[]{:S(2)}) collective-permute-start(bf16[4,8,1024]{2,1,0:T(8,128)(2,1)S(1)} %stack.1.refs_0_), channel_id=1, source_target_pairs={{0,4},{4,8},{8,12},{12,0},{1,5},{5,9},{9,13},{13,1},{2,6},{6,10},{... | collective-permute-start | bytes 196616 | tf_op jit(solution)/shard_map/ppermute | solution.py:205
  4.5 7.1 %collective-permute-start.1 = (bf16[4,8,1024]{2,1,0:T(8,128)(2,1)S(1)}, bf16[4,8,1024]{2,1,0:T(8,128)(2,1)S(1)}, u32[]{:S(2)}, u32[]{:S(2)}) collective-permute-start(bf16[4,8,1024]{2,1,0:T(8,128)(2,1)S(1)} %stack.1.refs_0_), channel_id=1, source_target_pairs={{0,8},{4,12},{8,0},{12,4},{1,9},{5,13},{9,1},{13,5},{2,10},{6,14},... | collective-permute-start | bytes 196616 | tf_op jit(solution)/shard_map/ppermute | solution.py:205
  7.1 4.7 %collective-permute-start = (bf16[4,8,1024]{2,1,0:T(8,128)(2,1)S(1)}, bf16[4,8,1024]{2,1,0:T(8,128)(2,1)S(1)}, u32[]{:S(2)}, u32[]{:S(2)}) collective-permute-start(bf16[4,8,1024]{2,1,0:T(8,128)(2,1)S(1)} %stack.1.refs_0_), channel_id=1, source_target_pairs={{0,12},{4,0},{8,4},{12,8},{1,13},{5,1},{9,5},{13,9},{2,14},{6,2},{... | collective-permute-start | bytes 196616 | tf_op jit(solution)/shard_map/ppermute | solution.py:205
  12.8 4.2 %collective-permute-start.6 = (bf16[560,1024]{1,0:T(8,128)(2,1)S(1)}, bf16[560,1024]{1,0:T(8,128)(2,1)S(1)}, u32[]{:S(2)}, u32[]{:S(2)}) collective-permute-start(bf16[560,1024]{1,0:T(8,128)(2,1)S(1)} %get-tuple-element.37), channel_id=1, source_target_pairs={{0,16},{16,0},{1,17},{17,1},{2,18},{18,2},{3,19},{19,3},{4,20},{20... | collective-permute-start | bytes 3440648 | tf_op jit(solution)/shard_map/ppermute | solution.py:274
  12.9 6.1 %collective-permute-start.5 = (bf16[8,2176]{1,0:T(8,128)(2,1)S(1)}, bf16[8,2176]{1,0:T(8,128)(2,1)S(1)}, u32[]{:S(2)}, u32[]{:S(2)}) collective-permute-start(bf16[8,2176]{1,0:T(8,128)(2,1)S(1)} %get-tuple-element.42.refs_0_), channel_id=1, source_target_pairs={{0,4},{4,8},{8,12},{12,0},{1,5},{5,9},{9,13},{13,1},{2,6},{6,10},{... | collective-permute-start | bytes 104456 | tf_op jit(solution)/shard_map/ppermute | solution.py:205
  14.5 5.6 %collective-permute-start.4 = (bf16[8,2176]{1,0:T(8,128)(2,1)S(1)}, bf16[8,2176]{1,0:T(8,128)(2,1)S(1)}, u32[]{:S(2)}, u32[]{:S(2)}) collective-permute-start(bf16[8,2176]{1,0:T(8,128)(2,1)S(1)} %get-tuple-element.42.refs_0_), channel_id=1, source_target_pairs={{0,8},{4,12},{8,0},{12,4},{1,9},{5,13},{9,1},{13,5},{2,10},{6,14},... | collective-permute-start | bytes 104456 | tf_op jit(solution)/shard_map/ppermute | solution.py:205
  16.5 3.9 %collective-permute-start.3 = (bf16[8,2176]{1,0:T(8,128)(2,1)S(1)}, bf16[8,2176]{1,0:T(8,128)(2,1)S(1)}, u32[]{:S(2)}, u32[]{:S(2)}) collective-permute-start(bf16[8,2176]{1,0:T(8,128)(2,1)S(1)} %get-tuple-element.42.refs_0_), channel_id=1, source_target_pairs={{0,12},{4,0},{8,4},{12,8},{1,13},{5,1},{9,5},{13,9},{2,14},{6,2},{... | collective-permute-start | bytes 104456 | tf_op jit(solution)/shard_map/ppermute | solution.py:205

commit v5 on v4

--- a/solution.py
+++ b/solution.py
@@ -126,6 +126,15 @@
     keys = pick(memory, 0, behind, slot)
     values = pick(memory, slots, behind, slot)
     count = keys.shape[0]
+    first, second = tokens, tokens + padded(count)
+
+    @pl.when(section == 0)
+    def _():
+        ahead = place_ref[0]
+        behind, slot = lax.rem(me - ahead // slots + len(memory), len(memory)), ahead % slots
+        sent_ref[first : first + count, :] = pick(memory, 0, behind, slot)
+        sent_ref[second : second + count, :] = pick(memory, slots, behind, slot)
+
     saved, grads = saved_ref[...], grad_ref[...]
     weights = softmax_t(keys, saved)
     grad_weights = per_head(values, grads)
@@ -138,15 +147,6 @@
     grad_scores = grad_scores.reshape(flat, tokens)
     place = jnp.full((count, HEAD_DIM), back, jnp.int32)
     terms_ref[:, 2 * width :] = place.astype(jnp.float32).astype(jnp.bfloat16)
-    first, second = tokens, tokens + padded(count)
-
-    @pl.when(section == 0)
-    def _():
-        ahead = place_ref[0]
-        behind, slot = lax.rem(me - ahead // slots + len(memory), len(memory)), ahead % slots
-        sent_ref[first : first + count, :] = pick(memory, 0, behind, slot)
-        sent_ref[second : second + count, :] = pick(memory, slots, behind, slot)
-
     @pl.when(section != 0)
     def _():
         sent_ref[first : first + count, :] = keys
@@ -410,7 +410,8 @@
     replicas, (_, tokens, width) = lax.axis_size("dp"), args[0].shape
     few = replicas <= DIRECT_REPLICAS
     one_each = args[-1].size == 2 and lax.axis_size("pipe") == 2 and width % tokens == 0
-    return (direct if few and one_each else routed)(*args)
+    small = args[-2].size <= 256
+    return (direct if few and one_each and small else routed)(*args)
 
 
 def solution(mesh):

time: 21.4 us -> 21.3 us (level)
  no operation moved by 1% of the time
where the time goes in v5:
time: 21.3 us; the launch traced here: 21.1 us
  starting transfers between devices  11.1 us (52%)
  Pallas kernels  6.19 us (29%)
  waiting for transfers between devices  3.09 us (15%)
  between operations  0.67 us (3%)
    ppermute x6, starting transfers between devices, exchange(): lax.ppermute(x, 'dp', [(i, (i + d) % replicas) for i in range(replicas)])  11.1 us
    ppermute x6, waiting for transfers between devices, exchange(): lax.ppermute(x, 'dp', [(i, (i + d) % replicas) for i in range(replicas)])  3.09 us
    pallas_call x1, Pallas kernels, direct(): call(fetch_kernel, 'fetch', (rows, rows, sent, pltpu.SMEM((2,), jnp.int32...  1.9 us
    pallas_call x1, Pallas kernels, direct(): call(functools.partial(output_kernel, tokens, block_rows), 'outputs', (ja...  1.86 us
    pallas_call x1, Pallas kernels, direct(): call(functools.partial(score_kernel, slots), 'scores', (pltpu.VMEM((block...  0.96 us
    pallas_call x1, Pallas kernels, direct(): call(stack_kernel, 'stack', pltpu.VMEM((2 * slots, block_rows, width), jn...  0.79 us
    pallas_call x1, Pallas kernels, direct(): call(functools.partial(sum_kernel, slots), 'sums', (jax.ShapeDtypeStruct(...  0.68 us
  transfers between devices with their start and end apart: 7, of which 5 were waited for; matrix products, arithmetic and copies ran while one was open for 0% of the time, Pallas kernels for 18%

profile of v5, /device:TPU:0, one launch (start us, length us, event | category | flops | bytes accessed | tf_op | source)
XLA Modules:
  0.0 21.1 jit_solution(6251103310023891321)
XLA Ops:
  0.6 0.8 %stack.1.refs_0_ = bf16[4,8,1024]{2,1,0:T(8,128)(2,1)S(1)} custom-call(bf16[2,8,1024]{2,1,0:T(8,128)(2,1)} %bitcast.13, bf16[2,8,1024]{2,1,0:T(8,128)(2,1)} %bitcast.14), custom_call_target="tpu_custom_call" | custom-call | tf_op jit(solution)/shard_map/stack/pallas_call | solution.py:244
  1.4 3.1 %collective-permute-start.2 = (bf16[4,8,1024]{2,1,0:T(8,128)(2,1)S(1)}, bf16[4,8,1024]{2,1,0:T(8,128)(2,1)S(1)}, u32[]{:S(2)}, u32[]{:S(2)}) collective-permute-start(bf16[4,8,1024]{2,1,0:T(8,128)(2,1)S(1)} %stack.1.refs_0_), channel_id=1, source_target_pairs={{0,4},{4,8},{8,12},{12,0},{1,5},{5,9},{9,13},{13,1},{2,6},{6,10},{... | collective-permute-start | bytes 196616 | tf_op jit(solution)/shard_map/ppermute | solution.py:205
  4.5 2.6 %collective-permute-start.1 = (bf16[4,8,1024]{2,1,0:T(8,128)(2,1)S(1)}, bf16[4,8,1024]{2,1,0:T(8,128)(2,1)S(1)}, u32[]{:S(2)}, u32[]{:S(2)}) collective-permute-start(bf16[4,8,1024]{2,1,0:T(8,128)(2,1)S(1)} %stack.1.refs_0_), channel_id=1, source_target_pairs={{0,8},{4,12},{8,0},{12,4},{1,9},{5,13},{9,1},{13,5},{2,10},{6,14},... | collective-permute-start | bytes 196616 | tf_op jit(solution)/shard_map/ppermute | solution.py:205
  7.1 1.3 %collective-permute-start = (bf16[4,8,1024]{2,1,0:T(8,128)(2,1)S(1)}, bf16[4,8,1024]{2,1,0:T(8,128)(2,1)S(1)}, u32[]{:S(2)}, u32[]{:S(2)}) collective-permute-start(bf16[4,8,1024]{2,1,0:T(8,128)(2,1)S(1)} %stack.1.refs_0_), channel_id=1, source_target_pairs={{0,12},{4,0},{8,4},{12,8},{1,13},{5,1},{9,5},{13,9},{2,14},{6,2},{... | collective-permute-start | bytes 196616 | tf_op jit(solution)/shard_map/ppermute | solution.py:205
  8.4 1.9 %fetch.1 = (bf16[512,1024]{1,0:T(8,128)(2,1)S(1)}, bf16[512,1024]{1,0:T(8,128)(2,1)S(1)}, bf16[560,1024]{1,0:T(8,128)(2,1)S(1)}, s32[2]{0:T(128)S(4)}) custom-call(s32[8]{0:T(128)} %map_ref, s32[2]{0:T(128)} %bitcast.15, bf16[512,1024]{1,0:T(8,128)(2,1)} %bitcast.10, bf16[512,1024]{1,0:T(8,128)(2,1)} %bitcast.11, bf16[512,1024]{1,0:T(8,128)(2,1)} %bitcast.12), custom_call_target="tpu_custom_call" | custom-call | bytes 6291456 | tf_op jit(solution)/shard_map/fetch/pallas_call | solution.py:255
  10.4 0.0 collective-permute-done.2.refs_3_
  10.4 1.2 %collective-permute-done.1.refs_2_ = bf16[4,8,1024]{2,1,0:T(8,128)(2,1)S(1)} collective-permute-done((bf16[4,8,1024]{2,1,0:T(8,128)(2,1)S(1)}, bf16[4,8,1024]{2,1,0:T(8,128)(2,1)S(1)}, u32[]{:S(2)}, u32[]{:S(2)}) %collective-permute-start.1) | collective-permute-done | bytes 65568 | tf_op jit(solution)/shard_map/ppermute | solution.py:205
  11.6 0.2 %collective-permute-done.refs_1_ = bf16[4,8,1024]{2,1,0:T(8,128)(2,1)S(1)} collective-permute-done((bf16[4,8,1024]{2,1,0:T(8,128)(2,1)S(1)}, bf16[4,8,1024]{2,1,0:T(8,128)(2,1)S(1)}, u32[]{:S(2)}, u32[]{:S(2)}) %collective-permute-start) | collective-permute-done | bytes 65568 | tf_op jit(solution)/shard_map/ppermute | solution.py:205
  11.8 1.0 %scores.1 = (bf16[8,2176]{1,0:T(8,128)(2,1)S(1)}, bf16[560,1024]{1,0:T(8,128)(2,1)S(1)}) custom-call(s32[2]{0:T(128)S(4)} %get-tuple-element.31.place_ref, bf16[512,1024]{1,0:T(8,128)(2,1)S(1)} %get-tuple-element.32.saved_ref, bf16[512,1024]{1,0:T(8,128)(2,1)S(1)} %get-tuple-element.33.grad_ref, ...), custom_call_target="tpu_custom_call", output_to_operand_aliasing={{1}: (3, {})} | custom-call | tf_op jit(solution)/shard_map/scores/pallas_call | solution.py:267
  12.8 0.0 collective-permute-start.6
  12.8 1.6 %collective-permute-start.5 = (bf16[8,2176]{1,0:T(8,128)(2,1)S(1)}, bf16[8,2176]{1,0:T(8,128)(2,1)S(1)}, u32[]{:S(2)}, u32[]{:S(2)}) collective-permute-start(bf16[8,2176]{1,0:T(8,128)(2,1)S(1)} %get-tuple-element.42.refs_0_), channel_id=1, source_target_pairs={{0,4},{4,8},{8,12},{12,0},{1,5},{5,9},{9,13},{13,1},{2,6},{6,10},{... | collective-permute-start | bytes 104456 | tf_op jit(solution)/shard_map/ppermute | solution.py:205
  14.5 2.0 %collective-permute-start.4 = (bf16[8,2176]{1,0:T(8,128)(2,1)S(1)}, bf16[8,2176]{1,0:T(8,128)(2,1)S(1)}, u32[]{:S(2)}, u32[]{:S(2)}) collective-permute-start(bf16[8,2176]{1,0:T(8,128)(2,1)S(1)} %get-tuple-element.42.refs_0_), channel_id=1, source_target_pairs={{0,8},{4,12},{8,0},{12,4},{1,9},{5,13},{9,1},{13,5},{2,10},{6,14},... | collective-permute-start | bytes 104456 | tf_op jit(solution)/shard_map/ppermute | solution.py:205
  16.5 0.4 %collective-permute-start.3 = (bf16[8,2176]{1,0:T(8,128)(2,1)S(1)}, bf16[8,2176]{1,0:T(8,128)(2,1)S(1)}, u32[]{:S(2)}, u32[]{:S(2)}) collective-permute-start(bf16[8,2176]{1,0:T(8,128)(2,1)S(1)} %get-tuple-element.42.refs_0_), channel_id=1, source_target_pairs={{0,12},{4,0},{8,4},{12,8},{1,13},{5,1},{9,5},{13,9},{2,14},{6,2},{... | collective-permute-start | bytes 104456 | tf_op jit(solution)/shard_map/ppermute | solution.py:205
  16.9 0.0 collective-permute-done.6.sent_ref
  16.9 1.9 %outputs.1 = (bf16[512,1024]{1,0:T(8,128)(2,1)}, bf16[512,1024]{1,0:T(8,128)(2,1)}) custom-call(bf16[560,1024]{1,0:T(8,128)(2,1)S(1)} %collective-permute-done.6.sent_ref), custom_call_target="tpu_custom_call" | custom-call | bytes 2097152 | tf_op jit(solution)/shard_map/outputs/pallas_call | solution.py:276
  18.8 0.1 collective-permute-done.5.refs_3_
  18.9 1.1 %collective-permute-done.4.refs_2_ = bf16[8,2176]{1,0:T(8,128)(2,1)S(1)} collective-permute-done((bf16[8,2176]{1,0:T(8,128)(2,1)S(1)}, bf16[8,2176]{1,0:T(8,128)(2,1)S(1)}, u32[]{:S(2)}, u32[]{:S(2)}) %collective-permute-start.4) | collective-permute-done | bytes 34848 | tf_op jit(solution)/shard_map/ppermute | solution.py:205
  20.0 0.4 %collective-permute-done.3.refs_1_ = bf16[8,2176]{1,0:T(8,128)(2,1)S(1)} collective-permute-done((bf16[8,2176]{1,0:T(8,128)(2,1)S(1)}, bf16[8,2176]{1,0:T(8,128)(2,1)S(1)}, u32[]{:S(2)}, u32[]{:S(2)}) %collective-permute-start.3) | collective-permute-done | bytes 34848 | tf_op jit(solution)/shard_map/ppermute | solution.py:205
  20.4 0.7 %sums.1 = (bf16[2,8,1024]{2,1,0:T(8,128)(2,1)}, bf16[2,8,1024]{2,1,0:T(8,128)(2,1)}) custom-call(bf16[8,2176]{1,0:T(8,128)(2,1)S(1)} %get-tuple-element.42.refs_0_, bf16[8,2176]{1,0:T(8,128)(2,1)S(1)} %collective-permute-done.3.refs_1_, bf16[8,2176]{1,0:T(8,128)(2,1)S(1)} %collective-permute-done.4.refs_2_, bf16[8,2176]{1,0:T(8,128)(2,1)S(1)} %collective-permute-done.5.refs_3_), custom_call_target="tpu_custom_call" | custom-call | tf_op jit(solution)/shard_map/sums/pallas_call | solution.py:285
Async XLA Ops:
  1.4 8.9 %collective-permute-start.2 = (bf16[4,8,1024]{2,1,0:T(8,128)(2,1)S(1)}, bf16[4,8,1024]{2,1,0:T(8,128)(2,1)S(1)}, u32[]{:S(2)}, u32[]{:S(2)}) collective-permute-start(bf16[4,8,1024]{2,1,0:T(8,128)(2,1)S(1)} %stack.1.refs_0_), channel_id=1, source_target_pairs={{0,4},{4,8},{8,12},{12,0},{1,5},{5,9},{9,13},{13,1},{2,6},{6,10},{... | collective-permute-start | bytes 196616 | tf_op jit(solution)/shard_map/ppermute | solution.py:205
  4.5 7.1 %collective-permute-start.1 = (bf16[4,8,1024]{2,1,0:T(8,128)(2,1)S(1)}, bf16[4,8,1024]{2,1,0:T(8,128)(2,1)S(1)}, u32[]{:S(2)}, u32[]{:S(2)}) collective-permute-start(bf16[4,8,1024]{2,1,0:T(8,128)(2,1)S(1)} %stack.1.refs_0_), channel_id=1, source_target_pairs={{0,8},{4,12},{8,0},{12,4},{1,9},{5,13},{9,1},{13,5},{2,10},{6,14},... | collective-permute-start | bytes 196616 | tf_op jit(solution)/shard_map/ppermute | solution.py:205
  7.1 4.7 %collective-permute-start = (bf16[4,8,1024]{2,1,0:T(8,128)(2,1)S(1)}, bf16[4,8,1024]{2,1,0:T(8,128)(2,1)S(1)}, u32[]{:S(2)}, u32[]{:S(2)}) collective-permute-start(bf16[4,8,1024]{2,1,0:T(8,128)(2,1)S(1)} %stack.1.refs_0_), channel_id=1, source_target_pairs={{0,12},{4,0},{8,4},{12,8},{1,13},{5,1},{9,5},{13,9},{2,14},{6,2},{... | collective-permute-start | bytes 196616 | tf_op jit(solution)/shard_map/ppermute | solution.py:205
  12.8 4.1 %collective-permute-start.6 = (bf16[560,1024]{1,0:T(8,128)(2,1)S(1)}, bf16[560,1024]{1,0:T(8,128)(2,1)S(1)}, u32[]{:S(2)}, u32[]{:S(2)}) collective-permute-start(bf16[560,1024]{1,0:T(8,128)(2,1)S(1)} %get-tuple-element.37), channel_id=1, source_target_pairs={{0,16},{16,0},{1,17},{17,1},{2,18},{18,2},{3,19},{19,3},{4,20},{20... | collective-permute-start | bytes 3440648 | tf_op jit(solution)/shard_map/ppermute | solution.py:274
  12.8 6.1 %collective-permute-start.5 = (bf16[8,2176]{1,0:T(8,128)(2,1)S(1)}, bf16[8,2176]{1,0:T(8,128)(2,1)S(1)}, u32[]{:S(2)}, u32[]{:S(2)}) collective-permute-start(bf16[8,2176]{1,0:T(8,128)(2,1)S(1)} %get-tuple-element.42.refs_0_), channel_id=1, source_target_pairs={{0,4},{4,8},{8,12},{12,0},{1,5},{5,9},{9,13},{13,1},{2,6},{6,10},{... | collective-permute-start | bytes 104456 | tf_op jit(solution)/shard_map/ppermute | solution.py:205
  14.5 5.6 %collective-permute-start.4 = (bf16[8,2176]{1,0:T(8,128)(2,1)S(1)}, bf16[8,2176]{1,0:T(8,128)(2,1)S(1)}, u32[]{:S(2)}, u32[]{:S(2)}) collective-permute-start(bf16[8,2176]{1,0:T(8,128)(2,1)S(1)} %get-tuple-element.42.refs_0_), channel_id=1, source_target_pairs={{0,8},{4,12},{8,0},{12,4},{1,9},{5,13},{9,1},{13,5},{2,10},{6,14},... | collective-permute-start | bytes 104456 | tf_op jit(solution)/shard_map/ppermute | solution.py:205
  16.5 3.9 %collective-permute-start.3 = (bf16[8,2176]{1,0:T(8,128)(2,1)S(1)}, bf16[8,2176]{1,0:T(8,128)(2,1)S(1)}, u32[]{:S(2)}, u32[]{:S(2)}) collective-permute-start(bf16[8,2176]{1,0:T(8,128)(2,1)S(1)} %get-tuple-element.42.refs_0_), channel_id=1, source_target_pairs={{0,12},{4,0},{8,4},{12,8},{1,13},{5,1},{9,5},{13,9},{2,14},{6,2},{... | collective-permute-start | bytes 104456 | tf_op jit(solution)/shard_map/ppermute | solution.py:205

commit v6 on v5

--- a/solution.py
+++ b/solution.py
@@ -10,6 +10,7 @@
 
 HEAD_DIM = 128
 DIRECT_REPLICAS = 8
+SEND = ((2, 0, 3, 1), (3, 2, 1, 0), (1, 3, 0, 2))
 HBM = pl.BlockSpec(memory_space=pltpu.HBM)
 VMEM = pl.BlockSpec(memory_space=pltpu.VMEM)
 SMEM = pl.BlockSpec(memory_space=pltpu.SMEM)
@@ -200,11 +201,9 @@
             out[slot, :, j * HEAD_DIM : (j + 1) * HEAD_DIM] = total.astype(jnp.bfloat16)
 
 
-def exchange(x, replicas):
-    return [x] + [
-        lax.ppermute(x, "dp", [(i, (i + d) % replicas) for i in range(replicas)])
-        for d in range(replicas - 1, 0, -1)
-    ]
+def exchange(x, replicas, patterns=None):
+    shifts = [[(i + d) % replicas for i in range(replicas)] for d in range(replicas - 1, 0, -1)]
+    return [x] + [lax.ppermute(x, "dp", list(enumerate(p))) for p in patterns or shifts]
 
 
 def vmem(x):
@@ -272,7 +271,7 @@
         aliases={3: 1}.items(),
     )(smem(places), *map(vmem, (saved, grads, to_send, *memory)))
     other_sent = lax.ppermute(to_send, "pipe", [(0, 1), (1, 0)])
-    term_parts = exchange(terms, replicas)
+    term_parts = exchange(terms, replicas, SEND if replicas == 4 else None)
     next_input, grad_back = call(
         functools.partial(output_kernel, tokens, block_rows),
         "outputs",

time: 21.3 us -> 21.3 us (level)
  starting transfers between devices: 11.1 us -> 12.2 us
  waiting for transfers between devices: 3.09 us -> 2.03 us
    ppermute x6, waiting for transfers between devices: 3.09 us -> 2.03 us  [exchange(): lax.ppermute(x, 'dp', list(enumerate(p)))]
    ppermute x6, starting transfers between devices: 11.1 us -> 12.1 us  [exchange(): lax.ppermute(x, 'dp', list(enumerate(p)))]
  transfers between devices with their start and end apart: 7 -> 7, of which waited for: 5 -> 3; matrix products, arithmetic and copies ran while one was open for 0% -> 0% of each run, Pallas kernels for 18% -> 18%
where the time goes in v6:
time: 21.3 us; the launch traced here: 21.1 us
  starting transfers between devices  12.2 us (57%)
  Pallas kernels  6.19 us (29%)
  waiting for transfers between devices  2.03 us (10%)
  between operations  0.67 us (3%)
    ppermute x6, starting transfers between devices, exchange(): lax.ppermute(x, 'dp', list(enumerate(p)))  12.1 us
    ppermute x6, waiting for transfers between devices, exchange(): lax.ppermute(x, 'dp', list(enumerate(p)))  2.03 us
    pallas_call x1, Pallas kernels, direct(): call(fetch_kernel, 'fetch', (rows, rows, sent, pltpu.SMEM((2,), jnp.int32...  1.9 us
    pallas_call x1, Pallas kernels, direct(): call(functools.partial(output_kernel, tokens, block_rows), 'outputs', (ja...  1.86 us
    pallas_call x1, Pallas kernels, direct(): call(functools.partial(score_kernel, slots), 'scores', (pltpu.VMEM((block...  0.96 us
    pallas_call x1, Pallas kernels, direct(): call(stack_kernel, 'stack', pltpu.VMEM((2 * slots, block_rows, width), jn...  0.79 us
    pallas_call x1, Pallas kernels, direct(): call(functools.partial(sum_kernel, slots), 'sums', (jax.ShapeDtypeStruct(...  0.68 us
  transfers between devices with their start and end apart: 7, of which 3 were waited for; matrix products, arithmetic and copies ran while one was open for 0% of the time, Pallas kernels for 18%

profile of v6, /device:TPU:0, one launch (start us, length us, event | category | flops | bytes accessed | tf_op | source)
XLA Modules:
  0.0 21.1 jit_solution(12395710372247129834)
XLA Ops:
  0.6 0.8 %stack.1.refs_0_ = bf16[4,8,1024]{2,1,0:T(8,128)(2,1)S(1)} custom-call(bf16[2,8,1024]{2,1,0:T(8,128)(2,1)} %bitcast.13, bf16[2,8,1024]{2,1,0:T(8,128)(2,1)} %bitcast.14), custom_call_target="tpu_custom_call" | custom-call | tf_op jit(solution)/shard_map/stack/pallas_call | solution.py:243
  1.4 3.1 %collective-permute-start.2 = (bf16[4,8,1024]{2,1,0:T(8,128)(2,1)S(1)}, bf16[4,8,1024]{2,1,0:T(8,128)(2,1)S(1)}, u32[]{:S(2)}, u32[]{:S(2)}) collective-permute-start(bf16[4,8,1024]{2,1,0:T(8,128)(2,1)S(1)} %stack.1.refs_0_), channel_id=1, source_target_pairs={{0,4},{4,8},{8,12},{12,0},{1,5},{5,9},{9,13},{13,1},{2,6},{6,10},{... | collective-permute-start | bytes 196616 | tf_op jit(solution)/shard_map/ppermute | solution.py:206
  4.5 2.6 %collective-permute-start.1 = (bf16[4,8,1024]{2,1,0:T(8,128)(2,1)S(1)}, bf16[4,8,1024]{2,1,0:T(8,128)(2,1)S(1)}, u32[]{:S(2)}, u32[]{:S(2)}) collective-permute-start(bf16[4,8,1024]{2,1,0:T(8,128)(2,1)S(1)} %stack.1.refs_0_), channel_id=1, source_target_pairs={{0,8},{4,12},{8,0},{12,4},{1,9},{5,13},{9,1},{13,5},{2,10},{6,14},... | collective-permute-start | bytes 196616 | tf_op jit(solution)/shard_map/ppermute | solution.py:206
  7.1 1.3 %collective-permute-start = (bf16[4,8,1024]{2,1,0:T(8,128)(2,1)S(1)}, bf16[4,8,1024]{2,1,0:T(8,128)(2,1)S(1)}, u32[]{:S(2)}, u32[]{:S(2)}) collective-permute-start(bf16[4,8,1024]{2,1,0:T(8,128)(2,1)S(1)} %stack.1.refs_0_), channel_id=1, source_target_pairs={{0,12},{4,0},{8,4},{12,8},{1,13},{5,1},{9,5},{13,9},{2,14},{6,2},{... | collective-permute-start | bytes 196616 | tf_op jit(solution)/shard_map/ppermute | solution.py:206
  8.4 1.9 %fetch.1 = (bf16[512,1024]{1,0:T(8,128)(2,1)S(1)}, bf16[512,1024]{1,0:T(8,128)(2,1)S(1)}, bf16[560,1024]{1,0:T(8,128)(2,1)S(1)}, s32[2]{0:T(128)S(4)}) custom-call(s32[8]{0:T(128)} %map_ref, s32[2]{0:T(128)} %bitcast.15, bf16[512,1024]{1,0:T(8,128)(2,1)} %bitcast.10, bf16[512,1024]{1,0:T(8,128)(2,1)} %bitcast.11, bf16[512,1024]{1,0:T(8,128)(2,1)} %bitcast.12), custom_call_target="tpu_custom_call" | custom-call | bytes 6291456 | tf_op jit(solution)/shard_map/fetch/pallas_call | solution.py:254
  10.4 0.0 collective-permute-done.2.refs_3_
  10.4 1.2 %collective-permute-done.1.refs_2_ = bf16[4,8,1024]{2,1,0:T(8,128)(2,1)S(1)} collective-permute-done((bf16[4,8,1024]{2,1,0:T(8,128)(2,1)S(1)}, bf16[4,8,1024]{2,1,0:T(8,128)(2,1)S(1)}, u32[]{:S(2)}, u32[]{:S(2)}) %collective-permute-start.1) | collective-permute-done | bytes 65568 | tf_op jit(solution)/shard_map/ppermute | solution.py:206
  11.6 0.2 %collective-permute-done.refs_1_ = bf16[4,8,1024]{2,1,0:T(8,128)(2,1)S(1)} collective-permute-done((bf16[4,8,1024]{2,1,0:T(8,128)(2,1)S(1)}, bf16[4,8,1024]{2,1,0:T(8,128)(2,1)S(1)}, u32[]{:S(2)}, u32[]{:S(2)}) %collective-permute-start) | collective-permute-done | bytes 65568 | tf_op jit(solution)/shard_map/ppermute | solution.py:206
  11.8 1.0 %scores.1 = (bf16[8,2176]{1,0:T(8,128)(2,1)S(1)}, bf16[560,1024]{1,0:T(8,128)(2,1)S(1)}) custom-call(s32[2]{0:T(128)S(4)} %get-tuple-element.31.place_ref, bf16[512,1024]{1,0:T(8,128)(2,1)S(1)} %get-tuple-element.32.saved_ref, bf16[512,1024]{1,0:T(8,128)(2,1)S(1)} %get-tuple-element.33.grad_ref, ...), custom_call_target="tpu_custom_call", output_to_operand_aliasing={{1}: (3, {})} | custom-call | tf_op jit(solution)/shard_map/scores/pallas_call | solution.py:266
  12.8 0.0 collective-permute-start.6
  12.8 1.6 %collective-permute-start.5 = (bf16[8,2176]{1,0:T(8,128)(2,1)S(1)}, bf16[8,2176]{1,0:T(8,128)(2,1)S(1)}, u32[]{:S(2)}, u32[]{:S(2)}) collective-permute-start(bf16[8,2176]{1,0:T(8,128)(2,1)S(1)} %get-tuple-element.42.refs_0_), channel_id=1, source_target_pairs={{0,4},{4,12},{8,0},{12,8},{1,5},{5,13},{9,1},{13,9},{2,6},{6,14},{... | collective-permute-start | bytes 104456 | tf_op jit(solution)/shard_map/ppermute | solution.py:206
  14.5 1.5 %collective-permute-start.4 = (bf16[8,2176]{1,0:T(8,128)(2,1)S(1)}, bf16[8,2176]{1,0:T(8,128)(2,1)S(1)}, u32[]{:S(2)}, u32[]{:S(2)}) collective-permute-start(bf16[8,2176]{1,0:T(8,128)(2,1)S(1)} %get-tuple-element.42.refs_0_), channel_id=1, source_target_pairs={{0,12},{4,8},{8,4},{12,0},{1,13},{5,9},{9,5},{13,1},{2,14},{6,10},... | collective-permute-start | bytes 104456 | tf_op jit(solution)/shard_map/ppermute | solution.py:206
  16.0 1.9 %collective-permute-start.3 = (bf16[8,2176]{1,0:T(8,128)(2,1)S(1)}, bf16[8,2176]{1,0:T(8,128)(2,1)S(1)}, u32[]{:S(2)}, u32[]{:S(2)}) collective-permute-start(bf16[8,2176]{1,0:T(8,128)(2,1)S(1)} %get-tuple-element.42.refs_0_), channel_id=1, source_target_pairs={{0,8},{4,0},{8,12},{12,4},{1,9},{5,1},{9,13},{13,5},{2,10},{6,2},{... | collective-permute-start | bytes 104456 | tf_op jit(solution)/shard_map/ppermute | solution.py:206
  17.9 0.0 collective-permute-done.6.sent_ref
  17.9 1.9 %outputs.1 = (bf16[512,1024]{1,0:T(8,128)(2,1)}, bf16[512,1024]{1,0:T(8,128)(2,1)}) custom-call(bf16[560,1024]{1,0:T(8,128)(2,1)S(1)} %collective-permute-done.6.sent_ref), custom_call_target="tpu_custom_call" | custom-call | bytes 2097152 | tf_op jit(solution)/shard_map/outputs/pallas_call | solution.py:275
  19.8 0.0 collective-permute-done.5.refs_3_
  19.8 0.6 %collective-permute-done.4.refs_2_ = bf16[8,2176]{1,0:T(8,128)(2,1)S(1)} collective-permute-done((bf16[8,2176]{1,0:T(8,128)(2,1)S(1)}, bf16[8,2176]{1,0:T(8,128)(2,1)S(1)}, u32[]{:S(2)}, u32[]{:S(2)}) %collective-permute-start.4) | collective-permute-done | bytes 34848 | tf_op jit(solution)/shard_map/ppermute | solution.py:206
  20.4 0.0 collective-permute-done.3.refs_1_
  20.4 0.7 %sums.1 = (bf16[2,8,1024]{2,1,0:T(8,128)(2,1)}, bf16[2,8,1024]{2,1,0:T(8,128)(2,1)}) custom-call(bf16[8,2176]{1,0:T(8,128)(2,1)S(1)} %get-tuple-element.42.refs_0_, bf16[8,2176]{1,0:T(8,128)(2,1)S(1)} %collective-permute-done.3.refs_1_, bf16[8,2176]{1,0:T(8,128)(2,1)S(1)} %collective-permute-done.4.refs_2_, bf16[8,2176]{1,0:T(8,128)(2,1)S(1)} %collective-permute-done.5.refs_3_), custom_call_target="tpu_custom_call" | custom-call | tf_op jit(solution)/shard_map/sums/pallas_call | solution.py:284
Async XLA Ops:
  1.4 8.9 %collective-permute-start.2 = (bf16[4,8,1024]{2,1,0:T(8,128)(2,1)S(1)}, bf16[4,8,1024]{2,1,0:T(8,128)(2,1)S(1)}, u32[]{:S(2)}, u32[]{:S(2)}) collective-permute-start(bf16[4,8,1024]{2,1,0:T(8,128)(2,1)S(1)} %stack.1.refs_0_), channel_id=1, source_target_pairs={{0,4},{4,8},{8,12},{12,0},{1,5},{5,9},{9,13},{13,1},{2,6},{6,10},{... | collective-permute-start | bytes 196616 | tf_op jit(solution)/shard_map/ppermute | solution.py:206
  4.5 7.1 %collective-permute-start.1 = (bf16[4,8,1024]{2,1,0:T(8,128)(2,1)S(1)}, bf16[4,8,1024]{2,1,0:T(8,128)(2,1)S(1)}, u32[]{:S(2)}, u32[]{:S(2)}) collective-permute-start(bf16[4,8,1024]{2,1,0:T(8,128)(2,1)S(1)} %stack.1.refs_0_), channel_id=1, source_target_pairs={{0,8},{4,12},{8,0},{12,4},{1,9},{5,13},{9,1},{13,5},{2,10},{6,14},... | collective-permute-start | bytes 196616 | tf_op jit(solution)/shard_map/ppermute | solution.py:206
  7.1 4.7 %collective-permute-start = (bf16[4,8,1024]{2,1,0:T(8,128)(2,1)S(1)}, bf16[4,8,1024]{2,1,0:T(8,128)(2,1)S(1)}, u32[]{:S(2)}, u32[]{:S(2)}) collective-permute-start(bf16[4,8,1024]{2,1,0:T(8,128)(2,1)S(1)} %stack.1.refs_0_), channel_id=1, source_target_pairs={{0,12},{4,0},{8,4},{12,8},{1,13},{5,1},{9,5},{13,9},{2,14},{6,2},{... | collective-permute-start | bytes 196616 | tf_op jit(solution)/shard_map/ppermute | solution.py:206
  12.8 5.2 %collective-permute-start.6 = (bf16[560,1024]{1,0:T(8,128)(2,1)S(1)}, bf16[560,1024]{1,0:T(8,128)(2,1)S(1)}, u32[]{:S(2)}, u32[]{:S(2)}) collective-permute-start(bf16[560,1024]{1,0:T(8,128)(2,1)S(1)} %get-tuple-element.37), channel_id=1, source_target_pairs={{0,16},{16,0},{1,17},{17,1},{2,18},{18,2},{3,19},{19,3},{4,20},{20... | collective-permute-start | bytes 3440648 | tf_op jit(solution)/shard_map/ppermute | solution.py:273
  12.8 7.0 %collective-permute-start.5 = (bf16[8,2176]{1,0:T(8,128)(2,1)S(1)}, bf16[8,2176]{1,0:T(8,128)(2,1)S(1)}, u32[]{:S(2)}, u32[]{:S(2)}) collective-permute-start(bf16[8,2176]{1,0:T(8,128)(2,1)S(1)} %get-tuple-element.42.refs_0_), channel_id=1, source_target_pairs={{0,4},{4,12},{8,0},{12,8},{1,5},{5,13},{9,1},{13,9},{2,6},{6,14},{... | collective-permute-start | bytes 104456 | tf_op jit(solution)/shard_map/ppermute | solution.py:206
  14.5 5.9 %collective-permute-start.4 = (bf16[8,2176]{1,0:T(8,128)(2,1)S(1)}, bf16[8,2176]{1,0:T(8,128)(2,1)S(1)}, u32[]{:S(2)}, u32[]{:S(2)}) collective-permute-start(bf16[8,2176]{1,0:T(8,128)(2,1)S(1)} %get-tuple-element.42.refs_0_), channel_id=1, source_target_pairs={{0,12},{4,8},{8,4},{12,0},{1,13},{5,9},{9,5},{13,1},{2,14},{6,10},... | collective-permute-start | bytes 104456 | tf_op jit(solution)/shard_map/ppermute | solution.py:206
  16.0 4.4 %collective-permute-start.3 = (bf16[8,2176]{1,0:T(8,128)(2,1)S(1)}, bf16[8,2176]{1,0:T(8,128)(2,1)S(1)}, u32[]{:S(2)}, u32[]{:S(2)}) collective-permute-start(bf16[8,2176]{1,0:T(8,128)(2,1)S(1)} %get-tuple-element.42.refs_0_), channel_id=1, source_target_pairs={{0,8},{4,0},{8,12},{12,4},{1,9},{5,1},{9,13},{13,5},{2,10},{6,2},{... | collective-permute-start | bytes 104456 | tf_op jit(solution)/shard_map/ppermute | solution.py:206

commit v7 on v5

--- a/solution.py
+++ b/solution.py
@@ -73,10 +73,10 @@
 
 def stack_kernel(keys_ref, values_ref, out_ref, sems):
     slots = keys_ref.shape[0]
-    copies = [
-        pltpu.make_async_copy(keys_ref, out_ref.at[:slots], sems.at[0]),
-        pltpu.make_async_copy(values_ref, out_ref.at[slots:], sems.at[1]),
-    ]
+    copies = []
+    for i in range(slots):
+        copies.append(pltpu.make_async_copy(keys_ref.at[i], out_ref.at[i], sems.at[i]))
+        copies.append(pltpu.make_async_copy(values_ref.at[i], out_ref.at[slots + i], sems.at[slots + i]))
     for copy in copies:
         copy.start()
     for copy in copies:
@@ -246,7 +246,7 @@
         "stack",
         pltpu.VMEM((2 * slots, block_rows, width), jnp.bfloat16),
         [HBM] * 2,
-        [pltpu.SemaphoreType.DMA((2,))],
+        [pltpu.SemaphoreType.DMA((2 * slots,))],
     )(hbm(mem_keys[0]), hbm(mem_values[0]))
     stacked, *own = lax.optimization_barrier(
         (stacked, owner_map, block_ids.reshape(-1), stream_in[0], saved_in[0], grad_out[0])

time: 21.3 us -> 21.5 us (level)
  no operation moved by 1% of the time
where the time goes in v7:
time: 21.5 us; the launch traced here: 21.1 us
  starting transfers between devices  11.1 us (52%)
  Pallas kernels  6.2 us (29%)
  waiting for transfers between devices  3.09 us (14%)
  between operations  0.67 us (3%)
    ppermute x6, starting transfers between devices, exchange(): lax.ppermute(x, 'dp', [(i, (i + d) % replicas) for i in range(replicas)])  11.1 us
    ppermute x6, waiting for transfers between devices, exchange(): lax.ppermute(x, 'dp', [(i, (i + d) % replicas) for i in range(replicas)])  3.09 us
    pallas_call x1, Pallas kernels, direct(): call(fetch_kernel, 'fetch', (rows, rows, sent, pltpu.SMEM((2,), jnp.int32...  1.9 us
    pallas_call x1, Pallas kernels, direct(): call(functools.partial(output_kernel, tokens, block_rows), 'outputs', (ja...  1.86 us
    pallas_call x1, Pallas kernels, direct(): call(functools.partial(score_kernel, slots), 'scores', (pltpu.VMEM((block...  0.96 us
    pallas_call x1, Pallas kernels, direct(): call(stack_kernel, 'stack', pltpu.VMEM((2 * slots, block_rows, width), jn...  0.8 us
    pallas_call x1, Pallas kernels, direct(): call(functools.partial(sum_kernel, slots), 'sums', (jax.ShapeDtypeStruct(...  0.68 us
  transfers between devices with their start and end apart: 7, of which 5 were waited for; matrix products, arithmetic and copies ran while one was open for 0% of the time, Pallas kernels for 18%

profile of v7, /device:TPU:0, one launch (start us, length us, event | category | flops | bytes accessed | tf_op | source)
XLA Modules:
  0.0 21.1 jit_solution(4821029065158367065)
XLA Ops:
  0.6 0.8 %stack.1.refs_0_ = bf16[4,8,1024]{2,1,0:T(8,128)(2,1)S(1)} custom-call(bf16[2,8,1024]{2,1,0:T(8,128)(2,1)} %bitcast.13, bf16[2,8,1024]{2,1,0:T(8,128)(2,1)} %bitcast.14), custom_call_target="tpu_custom_call" | custom-call | tf_op jit(solution)/shard_map/stack/pallas_call | solution.py:244
  1.4 3.1 %collective-permute-start.2 = (bf16[4,8,1024]{2,1,0:T(8,128)(2,1)S(1)}, bf16[4,8,1024]{2,1,0:T(8,128)(2,1)S(1)}, u32[]{:S(2)}, u32[]{:S(2)}) collective-permute-start(bf16[4,8,1024]{2,1,0:T(8,128)(2,1)S(1)} %stack.1.refs_0_), channel_id=1, source_target_pairs={{0,4},{4,8},{8,12},{12,0},{1,5},{5,9},{9,13},{13,1},{2,6},{6,10},{... | collective-permute-start | bytes 196616 | tf_op jit(solution)/shard_map/ppermute | solution.py:205
  4.5 2.6 %collective-permute-start.1 = (bf16[4,8,1024]{2,1,0:T(8,128)(2,1)S(1)}, bf16[4,8,1024]{2,1,0:T(8,128)(2,1)S(1)}, u32[]{:S(2)}, u32[]{:S(2)}) collective-permute-start(bf16[4,8,1024]{2,1,0:T(8,128)(2,1)S(1)} %stack.1.refs_0_), channel_id=1, source_target_pairs={{0,8},{4,12},{8,0},{12,4},{1,9},{5,13},{9,1},{13,5},{2,10},{6,14},... | collective-permute-start | bytes 196616 | tf_op jit(solution)/shard_map/ppermute | solution.py:205
  7.1 1.3 %collective-permute-start = (bf16[4,8,1024]{2,1,0:T(8,128)(2,1)S(1)}, bf16[4,8,1024]{2,1,0:T(8,128)(2,1)S(1)}, u32[]{:S(2)}, u32[]{:S(2)}) collective-permute-start(bf16[4,8,1024]{2,1,0:T(8,128)(2,1)S(1)} %stack.1.refs_0_), channel_id=1, source_target_pairs={{0,12},{4,0},{8,4},{12,8},{1,13},{5,1},{9,5},{13,9},{2,14},{6,2},{... | collective-permute-start | bytes 196616 | tf_op jit(solution)/shard_map/ppermute | solution.py:205
  8.5 1.9 %fetch.1 = (bf16[512,1024]{1,0:T(8,128)(2,1)S(1)}, bf16[512,1024]{1,0:T(8,128)(2,1)S(1)}, bf16[560,1024]{1,0:T(8,128)(2,1)S(1)}, s32[2]{0:T(128)S(4)}) custom-call(s32[8]{0:T(128)} %map_ref, s32[2]{0:T(128)} %bitcast.15, bf16[512,1024]{1,0:T(8,128)(2,1)} %bitcast.10, bf16[512,1024]{1,0:T(8,128)(2,1)} %bitcast.11, bf16[512,1024]{1,0:T(8,128)(2,1)} %bitcast.12), custom_call_target="tpu_custom_call" | custom-call | bytes 6291456 | tf_op jit(solution)/shard_map/fetch/pallas_call | solution.py:255
  10.4 0.0 collective-permute-done.2.refs_3_
  10.4 1.2 %collective-permute-done.1.refs_2_ = bf16[4,8,1024]{2,1,0:T(8,128)(2,1)S(1)} collective-permute-done((bf16[4,8,1024]{2,1,0:T(8,128)(2,1)S(1)}, bf16[4,8,1024]{2,1,0:T(8,128)(2,1)S(1)}, u32[]{:S(2)}, u32[]{:S(2)}) %collective-permute-start.1) | collective-permute-done | bytes 65568 | tf_op jit(solution)/shard_map/ppermute | solution.py:205
  11.6 0.2 %collective-permute-done.refs_1_ = bf16[4,8,1024]{2,1,0:T(8,128)(2,1)S(1)} collective-permute-done((bf16[4,8,1024]{2,1,0:T(8,128)(2,1)S(1)}, bf16[4,8,1024]{2,1,0:T(8,128)(2,1)S(1)}, u32[]{:S(2)}, u32[]{:S(2)}) %collective-permute-start) | collective-permute-done | bytes 65568 | tf_op jit(solution)/shard_map/ppermute | solution.py:205
  11.8 1.0 %scores.1 = (bf16[8,2176]{1,0:T(8,128)(2,1)S(1)}, bf16[560,1024]{1,0:T(8,128)(2,1)S(1)}) custom-call(s32[2]{0:T(128)S(4)} %get-tuple-element.31.place_ref, bf16[512,1024]{1,0:T(8,128)(2,1)S(1)} %get-tuple-element.32.saved_ref, bf16[512,1024]{1,0:T(8,128)(2,1)S(1)} %get-tuple-element.33.grad_ref, ...), custom_call_target="tpu_custom_call", output_to_operand_aliasing={{1}: (3, {})} | custom-call | tf_op jit(solution)/shard_map/scores/pallas_call | solution.py:267
  12.8 0.0 collective-permute-start.6
  12.8 1.6 %collective-permute-start.5 = (bf16[8,2176]{1,0:T(8,128)(2,1)S(1)}, bf16[8,2176]{1,0:T(8,128)(2,1)S(1)}, u32[]{:S(2)}, u32[]{:S(2)}) collective-permute-start(bf16[8,2176]{1,0:T(8,128)(2,1)S(1)} %get-tuple-element.42.refs_0_), channel_id=1, source_target_pairs={{0,4},{4,8},{8,12},{12,0},{1,5},{5,9},{9,13},{13,1},{2,6},{6,10},{... | collective-permute-start | bytes 104456 | tf_op jit(solution)/shard_map/ppermute | solution.py:205
  14.5 2.0 %collective-permute-start.4 = (bf16[8,2176]{1,0:T(8,128)(2,1)S(1)}, bf16[8,2176]{1,0:T(8,128)(2,1)S(1)}, u32[]{:S(2)}, u32[]{:S(2)}) collective-permute-start(bf16[8,2176]{1,0:T(8,128)(2,1)S(1)} %get-tuple-element.42.refs_0_), channel_id=1, source_target_pairs={{0,8},{4,12},{8,0},{12,4},{1,9},{5,13},{9,1},{13,5},{2,10},{6,14},... | collective-permute-start | bytes 104456 | tf_op jit(solution)/shard_map/ppermute | solution.py:205
  16.5 0.4 %collective-permute-start.3 = (bf16[8,2176]{1,0:T(8,128)(2,1)S(1)}, bf16[8,2176]{1,0:T(8,128)(2,1)S(1)}, u32[]{:S(2)}, u32[]{:S(2)}) collective-permute-start(bf16[8,2176]{1,0:T(8,128)(2,1)S(1)} %get-tuple-element.42.refs_0_), channel_id=1, source_target_pairs={{0,12},{4,0},{8,4},{12,8},{1,13},{5,1},{9,5},{13,9},{2,14},{6,2},{... | collective-permute-start | bytes 104456 | tf_op jit(solution)/shard_map/ppermute | solution.py:205
  16.9 0.0 collective-permute-done.6.sent_ref
  16.9 1.9 %outputs.1 = (bf16[512,1024]{1,0:T(8,128)(2,1)}, bf16[512,1024]{1,0:T(8,128)(2,1)}) custom-call(bf16[560,1024]{1,0:T(8,128)(2,1)S(1)} %collective-permute-done.6.sent_ref), custom_call_target="tpu_custom_call" | custom-call | bytes 2097152 | tf_op jit(solution)/shard_map/outputs/pallas_call | solution.py:276
  18.8 0.1 collective-permute-done.5.refs_3_
  18.9 1.1 %collective-permute-done.4.refs_2_ = bf16[8,2176]{1,0:T(8,128)(2,1)S(1)} collective-permute-done((bf16[8,2176]{1,0:T(8,128)(2,1)S(1)}, bf16[8,2176]{1,0:T(8,128)(2,1)S(1)}, u32[]{:S(2)}, u32[]{:S(2)}) %collective-permute-start.4) | collective-permute-done | bytes 34848 | tf_op jit(solution)/shard_map/ppermute | solution.py:205
  20.0 0.4 %collective-permute-done.3.refs_1_ = bf16[8,2176]{1,0:T(8,128)(2,1)S(1)} collective-permute-done((bf16[8,2176]{1,0:T(8,128)(2,1)S(1)}, bf16[8,2176]{1,0:T(8,128)(2,1)S(1)}, u32[]{:S(2)}, u32[]{:S(2)}) %collective-permute-start.3) | collective-permute-done | bytes 34848 | tf_op jit(solution)/shard_map/ppermute | solution.py:205
  20.4 0.7 %sums.1 = (bf16[2,8,1024]{2,1,0:T(8,128)(2,1)}, bf16[2,8,1024]{2,1,0:T(8,128)(2,1)}) custom-call(bf16[8,2176]{1,0:T(8,128)(2,1)S(1)} %get-tuple-element.42.refs_0_, bf16[8,2176]{1,0:T(8,128)(2,1)S(1)} %collective-permute-done.3.refs_1_, bf16[8,2176]{1,0:T(8,128)(2,1)S(1)} %collective-permute-done.4.refs_2_, bf16[8,2176]{1,0:T(8,128)(2,1)S(1)} %collective-permute-done.5.refs_3_), custom_call_target="tpu_custom_call" | custom-call | tf_op jit(solution)/shard_map/sums/pallas_call | solution.py:285
Async XLA Ops:
  1.4 8.9 %collective-permute-start.2 = (bf16[4,8,1024]{2,1,0:T(8,128)(2,1)S(1)}, bf16[4,8,1024]{2,1,0:T(8,128)(2,1)S(1)}, u32[]{:S(2)}, u32[]{:S(2)}) collective-permute-start(bf16[4,8,1024]{2,1,0:T(8,128)(2,1)S(1)} %stack.1.refs_0_), channel_id=1, source_target_pairs={{0,4},{4,8},{8,12},{12,0},{1,5},{5,9},{9,13},{13,1},{2,6},{6,10},{... | collective-permute-start | bytes 196616 | tf_op jit(solution)/shard_map/ppermute | solution.py:205
  4.5 7.1 %collective-permute-start.1 = (bf16[4,8,1024]{2,1,0:T(8,128)(2,1)S(1)}, bf16[4,8,1024]{2,1,0:T(8,128)(2,1)S(1)}, u32[]{:S(2)}, u32[]{:S(2)}) collective-permute-start(bf16[4,8,1024]{2,1,0:T(8,128)(2,1)S(1)} %stack.1.refs_0_), channel_id=1, source_target_pairs={{0,8},{4,12},{8,0},{12,4},{1,9},{5,13},{9,1},{13,5},{2,10},{6,14},... | collective-permute-start | bytes 196616 | tf_op jit(solution)/shard_map/ppermute | solution.py:205
  7.1 4.7 %collective-permute-start = (bf16[4,8,1024]{2,1,0:T(8,128)(2,1)S(1)}, bf16[4,8,1024]{2,1,0:T(8,128)(2,1)S(1)}, u32[]{:S(2)}, u32[]{:S(2)}) collective-permute-start(bf16[4,8,1024]{2,1,0:T(8,128)(2,1)S(1)} %stack.1.refs_0_), channel_id=1, source_target_pairs={{0,12},{4,0},{8,4},{12,8},{1,13},{5,1},{9,5},{13,9},{2,14},{6,2},{... | collective-permute-start | bytes 196616 | tf_op jit(solution)/shard_map/ppermute | solution.py:205
  12.8 4.1 %collective-permute-start.6 = (bf16[560,1024]{1,0:T(8,128)(2,1)S(1)}, bf16[560,1024]{1,0:T(8,128)(2,1)S(1)}, u32[]{:S(2)}, u32[]{:S(2)}) collective-permute-start(bf16[560,1024]{1,0:T(8,128)(2,1)S(1)} %get-tuple-element.37), channel_id=1, source_target_pairs={{0,16},{16,0},{1,17},{17,1},{2,18},{18,2},{3,19},{19,3},{4,20},{20... | collective-permute-start | bytes 3440648 | tf_op jit(solution)/shard_map/ppermute | solution.py:274
  12.8 6.1 %collective-permute-start.5 = (bf16[8,2176]{1,0:T(8,128)(2,1)S(1)}, bf16[8,2176]{1,0:T(8,128)(2,1)S(1)}, u32[]{:S(2)}, u32[]{:S(2)}) collective-permute-start(bf16[8,2176]{1,0:T(8,128)(2,1)S(1)} %get-tuple-element.42.refs_0_), channel_id=1, source_target_pairs={{0,4},{4,8},{8,12},{12,0},{1,5},{5,9},{9,13},{13,1},{2,6},{6,10},{... | collective-permute-start | bytes 104456 | tf_op jit(solution)/shard_map/ppermute | solution.py:205
  14.5 5.6 %collective-permute-start.4 = (bf16[8,2176]{1,0:T(8,128)(2,1)S(1)}, bf16[8,2176]{1,0:T(8,128)(2,1)S(1)}, u32[]{:S(2)}, u32[]{:S(2)}) collective-permute-start(bf16[8,2176]{1,0:T(8,128)(2,1)S(1)} %get-tuple-element.42.refs_0_), channel_id=1, source_target_pairs={{0,8},{4,12},{8,0},{12,4},{1,9},{5,13},{9,1},{13,5},{2,10},{6,14},... | collective-permute-start | bytes 104456 | tf_op jit(solution)/shard_map/ppermute | solution.py:205
  16.5 3.9 %collective-permute-start.3 = (bf16[8,2176]{1,0:T(8,128)(2,1)S(1)}, bf16[8,2176]{1,0:T(8,128)(2,1)S(1)}, u32[]{:S(2)}, u32[]{:S(2)}) collective-permute-start(bf16[8,2176]{1,0:T(8,128)(2,1)S(1)} %get-tuple-element.42.refs_0_), channel_id=1, source_target_pairs={{0,12},{4,0},{8,4},{12,8},{1,13},{5,1},{9,5},{13,9},{2,14},{6,2},{... | collective-permute-start | bytes 104456 | tf_op jit(solution)/shard_map/ppermute | solution.py:205

commit v8 on v6

--- a/solution.py
+++ b/solution.py
@@ -74,10 +74,10 @@
 
 def stack_kernel(keys_ref, values_ref, out_ref, sems):
     slots = keys_ref.shape[0]
-    copies = [
-        pltpu.make_async_copy(keys_ref, out_ref.at[:slots], sems.at[0]),
-        pltpu.make_async_copy(values_ref, out_ref.at[slots:], sems.at[1]),
-    ]
+    copies = []
+    for i in range(slots):
+        copies.append(pltpu.make_async_copy(keys_ref.at[i], out_ref.at[i], sems.at[i]))
+        copies.append(pltpu.make_async_copy(values_ref.at[i], out_ref.at[slots + i], sems.at[slots + i]))
     for copy in copies:
         copy.start()
     for copy in copies:
@@ -245,7 +245,7 @@
         "stack",
         pltpu.VMEM((2 * slots, block_rows, width), jnp.bfloat16),
         [HBM] * 2,
-        [pltpu.SemaphoreType.DMA((2,))],
+        [pltpu.SemaphoreType.DMA((2 * slots,))],
     )(hbm(mem_keys[0]), hbm(mem_values[0]))
     stacked, *own = lax.optimization_barrier(
         (stacked, owner_map, block_ids.reshape(-1), stream_in[0], saved_in[0], grad_out[0])

time: 21.3 us -> 21.4 us (level)
  no operation moved by 1% of the time
where the time goes in v8:
time: 21.4 us; the launch traced here: 21.1 us
  starting transfers between devices  12.2 us (57%)
  Pallas kernels  6.21 us (29%)
  waiting for transfers between devices  2.02 us (9%)
  between operations  0.67 us (3%)
    ppermute x6, starting transfers between devices, exchange(): lax.ppermute(x, 'dp', list(enumerate(p)))  12.1 us
    ppermute x6, waiting for transfers between devices, exchange(): lax.ppermute(x, 'dp', list(enumerate(p)))  2.02 us
    pallas_call x1, Pallas kernels, direct(): call(fetch_kernel, 'fetch', (rows, rows, sent, pltpu.SMEM((2,), jnp.int32...  1.9 us
    pallas_call x1, Pallas kernels, direct(): call(functools.partial(output_kernel, tokens, block_rows), 'outputs', (ja...  1.86 us
    pallas_call x1, Pallas kernels, direct(): call(functools.partial(score_kernel, slots), 'scores', (pltpu.VMEM((block...  0.96 us
    pallas_call x1, Pallas kernels, direct(): call(stack_kernel, 'stack', pltpu.VMEM((2 * slots, block_rows, width), jn...  0.8 us
    pallas_call x1, Pallas kernels, direct(): call(functools.partial(sum_kernel, slots), 'sums', (jax.ShapeDtypeStruct(...  0.68 us
  transfers between devices with their start and end apart: 7, of which 3 were waited for; matrix products, arithmetic and copies ran while one was open for 0% of the time, Pallas kernels for 18%

profile of v8, /device:TPU:0, one launch (start us, length us, event | category | flops | bytes accessed | tf_op | source)
XLA Modules:
  0.0 21.1 jit_solution(5426659973291574874)
XLA Ops:
  0.6 0.8 %stack.1.refs_0_ = bf16[4,8,1024]{2,1,0:T(8,128)(2,1)S(1)} custom-call(bf16[2,8,1024]{2,1,0:T(8,128)(2,1)} %bitcast.13, bf16[2,8,1024]{2,1,0:T(8,128)(2,1)} %bitcast.14), custom_call_target="tpu_custom_call" | custom-call | tf_op jit(solution)/shard_map/stack/pallas_call | solution.py:243
  1.4 3.1 %collective-permute-start.2 = (bf16[4,8,1024]{2,1,0:T(8,128)(2,1)S(1)}, bf16[4,8,1024]{2,1,0:T(8,128)(2,1)S(1)}, u32[]{:S(2)}, u32[]{:S(2)}) collective-permute-start(bf16[4,8,1024]{2,1,0:T(8,128)(2,1)S(1)} %stack.1.refs_0_), channel_id=1, source_target_pairs={{0,4},{4,8},{8,12},{12,0},{1,5},{5,9},{9,13},{13,1},{2,6},{6,10},{... | collective-permute-start | bytes 196616 | tf_op jit(solution)/shard_map/ppermute | solution.py:206
  4.5 2.6 %collective-permute-start.1 = (bf16[4,8,1024]{2,1,0:T(8,128)(2,1)S(1)}, bf16[4,8,1024]{2,1,0:T(8,128)(2,1)S(1)}, u32[]{:S(2)}, u32[]{:S(2)}) collective-permute-start(bf16[4,8,1024]{2,1,0:T(8,128)(2,1)S(1)} %stack.1.refs_0_), channel_id=1, source_target_pairs={{0,8},{4,12},{8,0},{12,4},{1,9},{5,13},{9,1},{13,5},{2,10},{6,14},... | collective-permute-start | bytes 196616 | tf_op jit(solution)/shard_map/ppermute | solution.py:206
  7.1 1.3 %collective-permute-start = (bf16[4,8,1024]{2,1,0:T(8,128)(2,1)S(1)}, bf16[4,8,1024]{2,1,0:T(8,128)(2,1)S(1)}, u32[]{:S(2)}, u32[]{:S(2)}) collective-permute-start(bf16[4,8,1024]{2,1,0:T(8,128)(2,1)S(1)} %stack.1.refs_0_), channel_id=1, source_target_pairs={{0,12},{4,0},{8,4},{12,8},{1,13},{5,1},{9,5},{13,9},{2,14},{6,2},{... | collective-permute-start | bytes 196616 | tf_op jit(solution)/shard_map/ppermute | solution.py:206
  8.5 1.9 %fetch.1 = (bf16[512,1024]{1,0:T(8,128)(2,1)S(1)}, bf16[512,1024]{1,0:T(8,128)(2,1)S(1)}, bf16[560,1024]{1,0:T(8,128)(2,1)S(1)}, s32[2]{0:T(128)S(4)}) custom-call(s32[8]{0:T(128)} %map_ref, s32[2]{0:T(128)} %bitcast.15, bf16[512,1024]{1,0:T(8,128)(2,1)} %bitcast.10, bf16[512,1024]{1,0:T(8,128)(2,1)} %bitcast.11, bf16[512,1024]{1,0:T(8,128)(2,1)} %bitcast.12), custom_call_target="tpu_custom_call" | custom-call | bytes 6291456 | tf_op jit(solution)/shard_map/fetch/pallas_call | solution.py:254
  10.4 0.0 collective-permute-done.2.refs_3_
  10.4 1.2 %collective-permute-done.1.refs_2_ = bf16[4,8,1024]{2,1,0:T(8,128)(2,1)S(1)} collective-permute-done((bf16[4,8,1024]{2,1,0:T(8,128)(2,1)S(1)}, bf16[4,8,1024]{2,1,0:T(8,128)(2,1)S(1)}, u32[]{:S(2)}, u32[]{:S(2)}) %collective-permute-start.1) | collective-permute-done | bytes 65568 | tf_op jit(solution)/shard_map/ppermute | solution.py:206
  11.6 0.2 %collective-permute-done.refs_1_ = bf16[4,8,1024]{2,1,0:T(8,128)(2,1)S(1)} collective-permute-done((bf16[4,8,1024]{2,1,0:T(8,128)(2,1)S(1)}, bf16[4,8,1024]{2,1,0:T(8,128)(2,1)S(1)}, u32[]{:S(2)}, u32[]{:S(2)}) %collective-permute-start) | collective-permute-done | bytes 65568 | tf_op jit(solution)/shard_map/ppermute | solution.py:206
  11.8 1.0 %scores.1 = (bf16[8,2176]{1,0:T(8,128)(2,1)S(1)}, bf16[560,1024]{1,0:T(8,128)(2,1)S(1)}) custom-call(s32[2]{0:T(128)S(4)} %get-tuple-element.31.place_ref, bf16[512,1024]{1,0:T(8,128)(2,1)S(1)} %get-tuple-element.32.saved_ref, bf16[512,1024]{1,0:T(8,128)(2,1)S(1)} %get-tuple-element.33.grad_ref, ...), custom_call_target="tpu_custom_call", output_to_operand_aliasing={{1}: (3, {})} | custom-call | tf_op jit(solution)/shard_map/scores/pallas_call | solution.py:266
  12.8 0.0 collective-permute-start.6
  12.8 1.6 %collective-permute-start.5 = (bf16[8,2176]{1,0:T(8,128)(2,1)S(1)}, bf16[8,2176]{1,0:T(8,128)(2,1)S(1)}, u32[]{:S(2)}, u32[]{:S(2)}) collective-permute-start(bf16[8,2176]{1,0:T(8,128)(2,1)S(1)} %get-tuple-element.42.refs_0_), channel_id=1, source_target_pairs={{0,4},{4,12},{8,0},{12,8},{1,5},{5,13},{9,1},{13,9},{2,6},{6,14},{... | collective-permute-start | bytes 104456 | tf_op jit(solution)/shard_map/ppermute | solution.py:206
  14.5 1.5 %collective-permute-start.4 = (bf16[8,2176]{1,0:T(8,128)(2,1)S(1)}, bf16[8,2176]{1,0:T(8,128)(2,1)S(1)}, u32[]{:S(2)}, u32[]{:S(2)}) collective-permute-start(bf16[8,2176]{1,0:T(8,128)(2,1)S(1)} %get-tuple-element.42.refs_0_), channel_id=1, source_target_pairs={{0,12},{4,8},{8,4},{12,0},{1,13},{5,9},{9,5},{13,1},{2,14},{6,10},... | collective-permute-start | bytes 104456 | tf_op jit(solution)/shard_map/ppermute | solution.py:206
  16.0 1.9 %collective-permute-start.3 = (bf16[8,2176]{1,0:T(8,128)(2,1)S(1)}, bf16[8,2176]{1,0:T(8,128)(2,1)S(1)}, u32[]{:S(2)}, u32[]{:S(2)}) collective-permute-start(bf16[8,2176]{1,0:T(8,128)(2,1)S(1)} %get-tuple-element.42.refs_0_), channel_id=1, source_target_pairs={{0,8},{4,0},{8,12},{12,4},{1,9},{5,1},{9,13},{13,5},{2,10},{6,2},{... | collective-permute-start | bytes 104456 | tf_op jit(solution)/shard_map/ppermute | solution.py:206
  17.9 0.0 collective-permute-done.6.sent_ref
  17.9 1.9 %outputs.1 = (bf16[512,1024]{1,0:T(8,128)(2,1)}, bf16[512,1024]{1,0:T(8,128)(2,1)}) custom-call(bf16[560,1024]{1,0:T(8,128)(2,1)S(1)} %collective-permute-done.6.sent_ref), custom_call_target="tpu_custom_call" | custom-call | bytes 2097152 | tf_op jit(solution)/shard_map/outputs/pallas_call | solution.py:275
  19.8 0.0 collective-permute-done.5.refs_3_
  19.8 0.6 %collective-permute-done.4.refs_2_ = bf16[8,2176]{1,0:T(8,128)(2,1)S(1)} collective-permute-done((bf16[8,2176]{1,0:T(8,128)(2,1)S(1)}, bf16[8,2176]{1,0:T(8,128)(2,1)S(1)}, u32[]{:S(2)}, u32[]{:S(2)}) %collective-permute-start.4) | collective-permute-done | bytes 34848 | tf_op jit(solution)/shard_map/ppermute | solution.py:206
  20.4 0.0 collective-permute-done.3.refs_1_
  20.4 0.7 %sums.1 = (bf16[2,8,1024]{2,1,0:T(8,128)(2,1)}, bf16[2,8,1024]{2,1,0:T(8,128)(2,1)}) custom-call(bf16[8,2176]{1,0:T(8,128)(2,1)S(1)} %get-tuple-element.42.refs_0_, bf16[8,2176]{1,0:T(8,128)(2,1)S(1)} %collective-permute-done.3.refs_1_, bf16[8,2176]{1,0:T(8,128)(2,1)S(1)} %collective-permute-done.4.refs_2_, bf16[8,2176]{1,0:T(8,128)(2,1)S(1)} %collective-permute-done.5.refs_3_), custom_call_target="tpu_custom_call" | custom-call | tf_op jit(solution)/shard_map/sums/pallas_call | solution.py:284
Async XLA Ops:
  1.4 8.9 %collective-permute-start.2 = (bf16[4,8,1024]{2,1,0:T(8,128)(2,1)S(1)}, bf16[4,8,1024]{2,1,0:T(8,128)(2,1)S(1)}, u32[]{:S(2)}, u32[]{:S(2)}) collective-permute-start(bf16[4,8,1024]{2,1,0:T(8,128)(2,1)S(1)} %stack.1.refs_0_), channel_id=1, source_target_pairs={{0,4},{4,8},{8,12},{12,0},{1,5},{5,9},{9,13},{13,1},{2,6},{6,10},{... | collective-permute-start | bytes 196616 | tf_op jit(solution)/shard_map/ppermute | solution.py:206
  4.5 7.1 %collective-permute-start.1 = (bf16[4,8,1024]{2,1,0:T(8,128)(2,1)S(1)}, bf16[4,8,1024]{2,1,0:T(8,128)(2,1)S(1)}, u32[]{:S(2)}, u32[]{:S(2)}) collective-permute-start(bf16[4,8,1024]{2,1,0:T(8,128)(2,1)S(1)} %stack.1.refs_0_), channel_id=1, source_target_pairs={{0,8},{4,12},{8,0},{12,4},{1,9},{5,13},{9,1},{13,5},{2,10},{6,14},... | collective-permute-start | bytes 196616 | tf_op jit(solution)/shard_map/ppermute | solution.py:206
  7.1 4.7 %collective-permute-start = (bf16[4,8,1024]{2,1,0:T(8,128)(2,1)S(1)}, bf16[4,8,1024]{2,1,0:T(8,128)(2,1)S(1)}, u32[]{:S(2)}, u32[]{:S(2)}) collective-permute-start(bf16[4,8,1024]{2,1,0:T(8,128)(2,1)S(1)} %stack.1.refs_0_), channel_id=1, source_target_pairs={{0,12},{4,0},{8,4},{12,8},{1,13},{5,1},{9,5},{13,9},{2,14},{6,2},{... | collective-permute-start | bytes 196616 | tf_op jit(solution)/shard_map/ppermute | solution.py:206
  12.8 5.2 %collective-permute-start.6 = (bf16[560,1024]{1,0:T(8,128)(2,1)S(1)}, bf16[560,1024]{1,0:T(8,128)(2,1)S(1)}, u32[]{:S(2)}, u32[]{:S(2)}) collective-permute-start(bf16[560,1024]{1,0:T(8,128)(2,1)S(1)} %get-tuple-element.37), channel_id=1, source_target_pairs={{0,16},{16,0},{1,17},{17,1},{2,18},{18,2},{3,19},{19,3},{4,20},{20... | collective-permute-start | bytes 3440648 | tf_op jit(solution)/shard_map/ppermute | solution.py:273
  12.8 7.0 %collective-permute-start.5 = (bf16[8,2176]{1,0:T(8,128)(2,1)S(1)}, bf16[8,2176]{1,0:T(8,128)(2,1)S(1)}, u32[]{:S(2)}, u32[]{:S(2)}) collective-permute-start(bf16[8,2176]{1,0:T(8,128)(2,1)S(1)} %get-tuple-element.42.refs_0_), channel_id=1, source_target_pairs={{0,4},{4,12},{8,0},{12,8},{1,5},{5,13},{9,1},{13,9},{2,6},{6,14},{... | collective-permute-start | bytes 104456 | tf_op jit(solution)/shard_map/ppermute | solution.py:206
  14.5 5.9 %collective-permute-start.4 = (bf16[8,2176]{1,0:T(8,128)(2,1)S(1)}, bf16[8,2176]{1,0:T(8,128)(2,1)S(1)}, u32[]{:S(2)}, u32[]{:S(2)}) collective-permute-start(bf16[8,2176]{1,0:T(8,128)(2,1)S(1)} %get-tuple-element.42.refs_0_), channel_id=1, source_target_pairs={{0,12},{4,8},{8,4},{12,0},{1,13},{5,9},{9,5},{13,1},{2,14},{6,10},... | collective-permute-start | bytes 104456 | tf_op jit(solution)/shard_map/ppermute | solution.py:206
  16.0 4.4 %collective-permute-start.3 = (bf16[8,2176]{1,0:T(8,128)(2,1)S(1)}, bf16[8,2176]{1,0:T(8,128)(2,1)S(1)}, u32[]{:S(2)}, u32[]{:S(2)}) collective-permute-start(bf16[8,2176]{1,0:T(8,128)(2,1)S(1)} %get-tuple-element.42.refs_0_), channel_id=1, source_target_pairs={{0,8},{4,0},{8,12},{12,4},{1,9},{5,1},{9,13},{13,5},{2,10},{6,2},{... | collective-permute-start | bytes 104456 | tf_op jit(solution)/shard_map/ppermute | solution.py:206
